TPU v7x, 128 devices: a whole 4x4x4 slice. The times are simulated.
128 devices in a mesh: grp: 4 (over z), ctx: 32 (over y, x, core).
Axes of the slice: x: 4, y: 4, z: 4, core: 2. Of those that a mesh axis runs over, the one named last changes fastest.
Arguments:
- block_input: bfloat16 [8, 2048, 1024], P('grp', 'ctx'), may hold values from -6 to 6
- seq_lengths: int32 [8], P('grp'), may hold values from 256 to 2048, as said below
- in_gain: bfloat16 [1024], P('grp'), may hold values from 0.099609375 to 1.8984375
- w_mixer: bfloat16 [1024, 4096], P('grp'), may hold values from -0.1875 to 0.1875
- conv_weight: bfloat16 [4, 4096], P(None, 'grp'), may hold values from -3 to 3
- w_rates: bfloat16 [1024, 16], P('grp'), may hold values from -1 to 1
- decay_scale: bfloat16 [8], P('grp'), may hold values from -3 to 3
- decay_bias: bfloat16 [8], P('grp'), may hold values from -7 to -2
- w_outgate: bfloat16 [1024, 2048], P('grp'), may hold values from -0.1875 to 0.1875
- head_gain: bfloat16 [256], P('grp'), may hold values from 0.099609375 to 1.8984375
- w_output: bfloat16 [2048, 1024], P('grp'), may hold values from -0.1875 to 0.1875
- mlp_gain: bfloat16 [1024], P('grp'), may hold values from 0.099609375 to 1.8984375
- w_gateup: bfloat16 [1024, 5632], P('grp'), may hold values from -0.1875 to 0.1875
- w_down: bfloat16 [2816, 1024], P('grp'), may hold values from -0.15625 to 0.15625
- cotangent: bfloat16 [8, 2048, 1024], P('grp', 'ctx'), may hold values from -6 to 6
Outputs:
- block_output: bfloat16 [8, 2048, 1024], P('grp', 'ctx')
- input_grad: float32 [8, 2048, 1024], P('grp', 'ctx')
- grad_in_gain: float32 [1024], P('grp')
- grad_mixer: float32 [1024, 4096], P('grp')
- grad_conv: float32 [4, 4096], P(None, 'grp')
- grad_rates: float32 [1024, 16], P('grp')
- grad_decay_scale: float32 [8], P('grp')
- grad_decay_bias: float32 [8], P('grp')
- grad_outgate: float32 [1024, 2048], P('grp')
- grad_head_gain: float32 [256], P('grp')
- grad_output: float32 [2048, 1024], P('grp')
- grad_mlp_gain: float32 [1024], P('grp')
- grad_gateup: float32 [1024, 5632], P('grp')
- grad_down: float32 [2816, 1024], P('grp')
Inputs may be any that keep to these rules, and one draw needn't show every extreme that they name: `seq_lengths`: of each 2 consecutive sequences one, chosen by the seed, has all 2048 slots valid.
All inputs are finite; a program needn't handle non-finite values.
Results may differ from a plain program's by a relative error of at most 0.011.
The roundings to bfloat16 on the way count: a program that leaves them out, or rounds other values in their place, can miss the bound.
Values may be sent and summed in bfloat16 or wider, within the bound.
No kernel may reach another device: no remote copies, remote signals or barrier semaphores. Data moves between devices by JAX's collectives and lax.ppermute only.
A program may use at most 576 MiB of HBM per device.

v0:
```python
import jax
import jax.numpy as jnp
from jax import lax
from jax.sharding import PartitionSpec as P

HEADS = 8
KEY_DIM = 128
VALUE_DIM = 256
FF = 2816
CONV = 4
SPAN = 64


epsilon = 1e-06
precise = lax.Precision.HIGHEST


def shifted(value, axis, steps):
    count = lax.axis_size(axis)
    leading, last = (max(0, -steps), min(count, count - steps))
    return lax.ppermute(value, axis, [(source, source + steps) for source in range(leading, last)])


def carried_in(value, axis, join, neutral, backward):
    count, mine = (lax.axis_size(axis), lax.axis_index(axis))
    pieces = jax.tree.map(lambda part: lax.all_gather(part, axis), value)
    if backward:
        pieces = jax.tree.map(lambda part: part[::-1], pieces)
        mine = count - 1 - mine
    total = jax.tree.map(
        lambda part, zero: jnp.full_like(part, 0) + jnp.asarray(zero, part.dtype), value, neutral
    )

    def lap(position, total):
        longer = join(total, jax.tree.map(lambda part: part[position], pieces))
        return jax.tree.map(lambda new, old: jnp.where(position < mine, new, old), longer, total)

    return lax.fori_loop(0, count - 1, lap, total)


def matmul(left, right):
    return jnp.einsum("btd,df->btf", left, right, preferred_element_type=jnp.float32)


def matmul_back(grads, right):
    return jnp.einsum("btf,df->btd", grads, right, preferred_element_type=jnp.float32)


def outer_sum(left, grads):
    return jnp.einsum("btd,btf->df", left, grads, preferred_element_type=jnp.float32)


def norm_apply(values_in, gain):
    return (
        values_in
        * lax.rsqrt(jnp.mean(values_in * values_in, axis=-1, keepdims=True) + epsilon)
        * gain
    )


def swiglu(gateup):
    return jax.nn.silu(gateup[..., :FF]) * gateup[..., FF:]


def gate_heads(outputs, outgate, head_gain):
    normed = (
        outputs
        * lax.rsqrt(jnp.mean(outputs * outputs, axis=-1, keepdims=True) + epsilon)
        * head_gain
    )
    return normed.reshape(outgate.shape) * jax.nn.silu(outgate)


def prepare(extended, conv_weight, rate_logits, decay_scale, decay_bias):
    length = extended.shape[1] - (CONV - 1)
    count_seqs = extended.shape[0]
    mixed_conv = sum(
        (conv_weight[lagged] * extended[:, lagged : lagged + length] for lagged in range(CONV))
    )
    active = jax.nn.silu(mixed_conv)
    keydim = HEADS * KEY_DIM
    queries = active[..., :keydim].reshape(count_seqs, length, HEADS, KEY_DIM)
    keys_in = active[..., keydim : 2 * keydim].reshape(count_seqs, length, HEADS, KEY_DIM)
    values = active[..., 2 * keydim :].reshape(count_seqs, length, HEADS, VALUE_DIM)
    queries = (
        queries
        * lax.rsqrt(jnp.sum(queries * queries, axis=-1, keepdims=True) + epsilon)
        * KEY_DIM ** (-0.5)
    )
    keys_in = keys_in * lax.rsqrt(jnp.sum(keys_in * keys_in, axis=-1, keepdims=True) + epsilon)
    beta_rates = jax.nn.sigmoid(rate_logits[..., :HEADS])
    decays = -jnp.exp(decay_scale) * jax.nn.softplus(rate_logits[..., HEADS:] + decay_bias)
    return (queries, keys_in, values, beta_rates, decays)


def span_update(state, pieces):
    queries, keys_in, values, beta_rates, decays = pieces
    block_len = queries.shape[2]
    cumlog = jnp.cumsum(decays, axis=2)
    log_gaps = cumlog[..., :, None] - cumlog[..., None, :]
    rows_at = lax.broadcasted_iota(jnp.int32, (block_len, block_len), 0)
    cols_at = lax.broadcasted_iota(jnp.int32, (block_len, block_len), 1)
    strict = cols_at < rows_at
    inclusive = cols_at <= rows_at
    strict_decay = jnp.where(strict, jnp.exp(jnp.where(strict, log_gaps, 0.0)), 0.0)
    incl_decay = jnp.where(inclusive, jnp.exp(jnp.where(inclusive, log_gaps, 0.0)), 0.0)
    key_key = jnp.einsum("bhid,bhjd->bhij", keys_in, keys_in, precision=precise)
    system = (
        jnp.eye(block_len, dtype=jnp.float32) + beta_rates[..., :, None] * strict_decay * key_key
    )
    growth = jnp.exp(cumlog)
    from_state = jnp.einsum("bhid,bhrd->bhir", keys_in, state, precision=precise)
    right_side = beta_rates[..., None] * (values - growth[..., None] * from_state)
    updates = lax.linalg.triangular_solve(
        system, right_side, left_side=True, lower=True, unit_diagonal=True
    )
    query_key = jnp.einsum("bhid,bhjd->bhij", queries, keys_in, precision=precise) * incl_decay
    outputs = growth[..., None] * jnp.einsum("bhid,bhrd->bhir", queries, state, precision=precise)
    outputs = outputs + jnp.einsum("bhij,bhjr->bhir", query_key, updates, precision=precise)
    to_end = jnp.exp(cumlog[..., -1:] - cumlog)
    new_state = jnp.exp(cumlog[..., -1])[..., None, None] * state
    new_state = new_state + jnp.einsum(
        "bhir,bhid->bhrd", updates, to_end[..., None] * keys_in, precision=precise
    )
    return (new_state, outputs)


def to_blocks(values_in):
    count_seqs, length = (values_in.shape[0], values_in.shape[1])
    shaped = values_in.reshape((count_seqs, length // SPAN, SPAN) + values_in.shape[2:])
    return jnp.moveaxis(jnp.moveaxis(shaped, 1, 0), 3, 2)


def from_blocks(blocked):
    moved = jnp.moveaxis(jnp.moveaxis(blocked, 2, 3), 0, 1)
    return moved.reshape((moved.shape[0], moved.shape[1] * moved.shape[2]) + moved.shape[3:])


def run_segment(state, queries, keys_in, values, beta_rates, decays):
    pieces = (
        to_blocks(queries),
        to_blocks(keys_in),
        to_blocks(values),
        to_blocks(beta_rates),
        to_blocks(decays),
    )
    final_state, outputs = lax.scan(jax.checkpoint(span_update), state, pieces)
    return (final_state, from_blocks(outputs))


def compose(earlier, latter):
    first_map, first_add = earlier
    second_map, second_add = latter
    joined_map = jnp.einsum("bhij,bhjk->bhik", first_map, second_map, precision=precise)
    joined_add = (
        jnp.einsum("bhrj,bhjk->bhrk", first_add, second_map, precision=precise) + second_add
    )
    return (joined_map, joined_add)


def body(
    block_input,
    seq_lengths,
    in_gain,
    w_mixer,
    conv_weight,
    w_rates,
    decay_scale,
    decay_bias,
    w_outgate,
    head_gain,
    w_output,
    mlp_gain,
    w_gateup,
    w_down,
    cotangent,
):
    gathered = (
        lax.all_gather(in_gain, "grp", axis=0, tiled=True),
        lax.all_gather(w_mixer, "grp", axis=0, tiled=True),
        lax.all_gather(conv_weight, "grp", axis=1, tiled=True),
        lax.all_gather(w_rates, "grp", axis=0, tiled=True),
        lax.all_gather(decay_scale, "grp", axis=0, tiled=True),
        lax.all_gather(decay_bias, "grp", axis=0, tiled=True),
        lax.all_gather(w_outgate, "grp", axis=0, tiled=True),
        lax.all_gather(head_gain, "grp", axis=0, tiled=True),
        lax.all_gather(w_output, "grp", axis=0, tiled=True),
        lax.all_gather(mlp_gain, "grp", axis=0, tiled=True),
        lax.all_gather(w_gateup, "grp", axis=0, tiled=True),
        lax.all_gather(w_down, "grp", axis=0, tiled=True),
    )
    (
        gain_one,
        mixer_full,
        conv_full,
        rates_full,
        scale_full,
        bias_full,
        outgate_full,
        head_full,
        output_full,
        gain_two,
        gateup_full,
        down_full,
    ) = gathered
    gain_one = gain_one.astype(jnp.float32)
    gain_two = gain_two.astype(jnp.float32)
    conv_f32 = conv_full.astype(jnp.float32)
    scale_f32 = scale_full.astype(jnp.float32)
    bias_f32 = bias_full.astype(jnp.float32)
    head_f32 = head_full.astype(jnp.float32)
    count_seqs, seglen = (block_input.shape[0], block_input.shape[1])
    segment = lax.axis_index("ctx")
    positions = segment * seglen + lax.broadcasted_iota(jnp.int32, (count_seqs, seglen), 1)
    valid_mask = (positions < seq_lengths[:, None]).astype(jnp.float32)[..., None]
    inputs_f = block_input.astype(jnp.float32)
    first_norm, first_back = jax.vjp(norm_apply, inputs_f, gain_one)
    hidden_one = first_norm.astype(jnp.bfloat16)
    mixed_in = matmul(hidden_one, mixer_full).astype(jnp.bfloat16)
    behind = shifted(mixed_in[:, seglen - (CONV - 1) :], "ctx", 1)
    extended = jnp.concatenate([behind, mixed_in], axis=1).astype(jnp.float32)
    rate_logits = matmul(hidden_one, rates_full)
    prepared, prepare_back = jax.vjp(prepare, extended, conv_f32, rate_logits, scale_f32, bias_f32)
    queries, keys_in, values, beta_rates, decays = prepared
    eye_maps = jnp.broadcast_to(
        jnp.eye(KEY_DIM, dtype=jnp.float32), (count_seqs, HEADS, KEY_DIM, KEY_DIM)
    )
    zero_values = jnp.zeros(values.shape[:3] + (KEY_DIM,), jnp.float32)
    joined_values = jnp.concatenate([values, zero_values], axis=3)
    zero_state = jnp.zeros((count_seqs, HEADS, VALUE_DIM, KEY_DIM), jnp.float32)
    state_start = jnp.concatenate([zero_state, eye_maps], axis=2)
    joined_end, joined_out = run_segment(
        state_start, queries, keys_in, joined_values, beta_rates, decays
    )
    carried = joined_end[:, :, :VALUE_DIM]
    transfer = joined_end[:, :, VALUE_DIM:]
    local_out = joined_out[..., :VALUE_DIM]
    probe_out = joined_out[..., VALUE_DIM:]
    prefix = carried_in((transfer, carried), "ctx", compose, (eye_maps, zero_state), False)
    incoming = prefix[1]
    outputs = local_out + jnp.einsum("bthd,bhrd->bthr", probe_out, incoming, precision=precise)
    outgate = matmul(hidden_one, outgate_full)
    gated_out, gated_back = jax.vjp(gate_heads, outputs, outgate, head_f32)
    gated_low = gated_out.astype(jnp.bfloat16)
    middle = inputs_f + matmul(gated_low, output_full)
    second_norm, second_back = jax.vjp(norm_apply, middle, gain_two)
    hidden_two = second_norm.astype(jnp.bfloat16)
    gateup = matmul(hidden_two, gateup_full)
    activated, swiglu_back = jax.vjp(swiglu, gateup)
    act_low = activated.astype(jnp.bfloat16)
    block_out = middle + matmul(act_low, down_full)
    block_output = (block_out * valid_mask).astype(jnp.bfloat16)
    again = (mixer_full, rates_full, outgate_full, output_full, gateup_full, down_full)
    mixer_again, rates_again, outgate_again, output_again, gateup_again, down_again = again
    ff_grad = cotangent.astype(jnp.float32) * valid_mask
    ff_low = ff_grad.astype(jnp.bfloat16)
    act_grad = matmul_back(ff_low, down_again)
    (gateup_grad,) = swiglu_back(act_grad)
    gateup_low = gateup_grad.astype(jnp.bfloat16)
    hidden_two_grad = matmul_back(gateup_low, gateup_again)
    middle_part, grad_gain_two = second_back(hidden_two_grad)
    middle_grad = ff_grad + middle_part
    mixer_low = middle_grad.astype(jnp.bfloat16)
    gated_grad = matmul_back(mixer_low, output_again)
    outputs_grad, outgate_grad, grad_head = gated_back(gated_grad)
    outgate_low = outgate_grad.astype(jnp.bfloat16)
    local_adjoint = jnp.einsum("bthr,bthd->bhrd", outputs_grad, probe_out, precision=precise)
    suffix = carried_in(
        (jnp.swapaxes(transfer, 2, 3), local_adjoint), "ctx", compose, (eye_maps, zero_state), True
    )
    leaving = suffix[1]

    def segment_fn(seg_queries, seg_keys, seg_values, seg_betas, seg_decays):
        final_state, seg_outputs = run_segment(
            incoming, seg_queries, seg_keys, seg_values, seg_betas, seg_decays
        )
        return (seg_outputs, final_state)

    recomputed, segment_back = jax.vjp(segment_fn, queries, keys_in, values, beta_rates, decays)
    prepared_grad = segment_back((outputs_grad, leaving))
    ext_grad, grad_conv_full, rates_grad, grad_scale_full, grad_bias_full = prepare_back(
        prepared_grad
    )
    sent_back = shifted(ext_grad[:, : CONV - 1], "ctx", -1)
    own_grad = ext_grad[:, CONV - 1 :]
    own_grad = jnp.concatenate(
        [own_grad[:, : seglen - (CONV - 1)], own_grad[:, seglen - (CONV - 1) :] + sent_back], axis=1
    )
    mixed_low = own_grad.astype(jnp.bfloat16)
    rates_low = rates_grad.astype(jnp.bfloat16)
    hidden_one_grad = (
        matmul_back(mixed_low, mixer_again)
        + matmul_back(rates_low, rates_again)
        + matmul_back(outgate_low, outgate_again)
    )
    input_part, grad_gain_one = first_back(hidden_one_grad)
    input_grad = middle_grad + input_part
    grad_down_full = outer_sum(act_low, ff_low)
    grad_gateup_full = outer_sum(hidden_two, gateup_low)
    grad_output_full = outer_sum(gated_low, mixer_low)
    grad_mixer_full = outer_sum(hidden_one, mixed_low)
    grad_rates_full = outer_sum(hidden_one, rates_low)
    grad_outgate_full = outer_sum(hidden_one, outgate_low)
    owners = (
        lax.psum_scatter(grad_gain_one, "grp", scatter_dimension=0, tiled=True),
        lax.psum_scatter(grad_mixer_full, "grp", scatter_dimension=0, tiled=True),
        lax.psum_scatter(grad_conv_full, "grp", scatter_dimension=1, tiled=True),
        lax.psum_scatter(grad_rates_full, "grp", scatter_dimension=0, tiled=True),
        lax.psum_scatter(grad_scale_full, "grp", scatter_dimension=0, tiled=True),
        lax.psum_scatter(grad_bias_full, "grp", scatter_dimension=0, tiled=True),
        lax.psum_scatter(grad_outgate_full, "grp", scatter_dimension=0, tiled=True),
        lax.psum_scatter(grad_head, "grp", scatter_dimension=0, tiled=True),
        lax.psum_scatter(grad_output_full, "grp", scatter_dimension=0, tiled=True),
        lax.psum_scatter(grad_gain_two, "grp", scatter_dimension=0, tiled=True),
        lax.psum_scatter(grad_gateup_full, "grp", scatter_dimension=0, tiled=True),
        lax.psum_scatter(grad_down_full, "grp", scatter_dimension=0, tiled=True),
    )
    summed = lax.psum(
        (
            owners[0],
            owners[1],
            owners[2],
            owners[3],
            owners[4],
            owners[5],
            owners[6],
            owners[7],
            owners[8],
            owners[9],
            owners[10],
            owners[11],
        ),
        "ctx",
    )
    return (
        block_output,
        input_grad,
        summed[0],
        summed[1],
        summed[2],
        summed[3],
        summed[4],
        summed[5],
        summed[6],
        summed[7],
        summed[8],
        summed[9],
        summed[10],
        summed[11],
    )


def solution(mesh):
    placed = (
        P("grp", "ctx", None),
        P("grp"),
        P("grp"),
        P("grp", None),
        P(None, "grp"),
        P("grp", None),
        P("grp"),
        P("grp"),
        P("grp", None),
        P("grp"),
        P("grp", None),
        P("grp"),
        P("grp", None),
        P("grp", None),
        P("grp", "ctx", None),
    )
    return jax.shard_map(
        body,
        mesh=mesh,
        in_specs=placed,
        out_specs=(
            P("grp", "ctx", None),
            P("grp", "ctx", None),
            P("grp"),
            P("grp", None),
            P(None, "grp"),
            P("grp", None),
            P("grp"),
            P("grp"),
            P("grp", None),
            P("grp"),
            P("grp", None),
            P("grp"),
            P("grp", None),
            P("grp", None),
        ),
        check_vma=False,
    )
```

profile of v0, /device:TPU:1, one launch (start us, length us, event | category | flops | bytes accessed | tf_op | source)
XLA Modules:
  0.0 2028.7 jit_solution(11134282301387487101)
XLA Ops:
  10.7 10.6 all-reduce.30
  26.6 10.2 all_gather.62
  38.3 10.1 all_gather.64
  48.9 48.0 %all-gather.16.cloned.1.call-done = bf16[1024,4096]{1,0:T(8,128)(2,1)} async-done(((bf16[256,4096]{1,0:T(8,128)(2,1)}), bf16[1024,4096]{1,0:T(8,128)(2,1)}) %all-gather.16.cloned.1.call-update) | async-done | bytes 8388624 | tf_op jit(solution)/shard_map/all_gather | solution.py:180
  112.9 78.9 %custom-call.13 = f32[2,8,1,64,64]{3,4,2,1,0:T(8,128)S(1)} custom-call(f32[2,8,1,64,64]{4,3,2,1,0:T(8,128)S(1)} %fusion.77), custom_call_target="InvertDiagBlocksLowerTriangular" | custom-call | tf_op jit(solution)/shard_map/while/body/eval_jaxpr/checkpoint/triangular_solve | solution.py:114
  196.4 5.7 fusion.49
  211.7 7.0 all-gather.5
  226.9 93.2 %all-gather.26.cloned.1.call-done = f32[64,8,128,128]{3,2,1,0:T(8,128)} async-done(((f32[2,8,128,128]{3,2,1,0:T(8,128)}), f32[64,8,128,128]{3,2,1,0:T(8,128)}) %all-gather.26.cloned.1.call-update) | async-done | bytes 33554448 | tf_op jit(solution)/shard_map/all_gather | solution.py:26
  320.1 203.1 %all-gather.28.cloned.1.call-done = f32[64,8,256,128]{3,2,1,0:T(8,128)} async-done(((f32[2,8,256,128]{3,2,1,0:T(8,128)}), f32[64,8,256,128]{3,2,1,0:T(8,128)}) %all-gather.28.cloned.1.call-update) | async-done | bytes 67108880 | tf_op jit(solution)/shard_map/all_gather | solution.py:26
  523.3 347.7 %while.20 = (s32[]{:T(128)}, f32[2,8,256,128]{2,3,1,0:T(8,128)S(1)}, s32[]{:T(128)}, f32[32,2,8,128,128]{4,3,2,1,0:T(8,128)}, f32[32,2,8,256,128]{4,3,2,1,0:T(8,128)}, /*index=5*/s32[]{:T(128)}, s32[]{:T(128)}) while((s32[]{:T(128)}, f32[2,8,256,128]{2,3,1,0:T(8,128)S(1)}, s32[]{:T(128)}, f32[32,2,8,128,128]{4,3,2,1,0:T(8,128)}, ...), condition=%wide.region_5.6_spmd.clone, body=%wide.region_4.5_spmd.clone.sunk | while | flops 807403520 | bytes 30410876 | solution.py:38
  885.0 7.9 fusion.24
  893.0 8.1 fusion.193
  901.1 6.3 multiply_reduce_fusion.9
  907.6 5.5 fusion.92
  914.0 6.8 fusion.157
  934.1 5.9 convolution_bitcast_fusion.2
  941.3 11.1 convolution_bitcast_fusion
  956.5 34.1 %copy.216 = f32[32,2,8,128,128]{3,4,2,1,0:T(8,128)} copy(f32[32,2,8,128,128]{4,3,2,1,0:T(8,128)} %bitcast.349) | data formatting | bytes 67108864 | tf_op jit(solution)/shard_map/all_gather | solution.py:26
  990.5 23.5 %rev.6 = f32[32,2,8,128,128]{3,4,2,1,0:T(8,128)} reverse(f32[32,2,8,128,128]{3,4,2,1,0:T(8,128)} %copy.216), dimensions={0} | reverse | bytes 67108864 | tf_op jit(solution)/shard_map/rev | solution.py:28
  1015.3 107.5 %all-gather.32.cloned.1.call-done = f32[64,8,256,128]{3,2,1,0:T(8,128)} async-done(((f32[2,8,256,128]{3,2,1,0:T(8,128)}), f32[64,8,256,128]{3,2,1,0:T(8,128)}) %all-gather.32.cloned.1.call-update) | async-done | bytes 67108880 | tf_op jit(solution)/shard_map/all_gather | solution.py:26
  1122.8 66.3 %copy.218 = f32[32,2,8,256,128]{3,4,2,1,0:T(8,128)} copy(f32[32,2,8,256,128]{4,3,2,1,0:T(8,128)} %bitcast.48) | data formatting | bytes 134217728 | tf_op jit(solution)/shard_map/all_gather | solution.py:26
  1189.1 44.4 %rev.7 = f32[32,2,8,256,128]{3,4,2,1,0:T(8,128)} reverse(f32[32,2,8,256,128]{3,4,2,1,0:T(8,128)} %copy.218), dimensions={0} | reverse | bytes 134217728 | tf_op jit(solution)/shard_map/rev | solution.py:28
  1233.5 222.7 %while.21 = (s32[]{:T(128)}, f32[2,8,256,128]{2,3,1,0:T(8,128)}, s32[]{:T(128)}, f32[32,2,8,128,128]{3,4,2,1,0:T(8,128)}, f32[32,2,8,256,128]{3,4,2,1,0:T(8,128)}, /*index=5*/s32[]{:T(128)}, s32[]{:T(128)}) while((s32[]{:T(128)}, f32[2,8,256,128]{2,3,1,0:T(8,128)}, s32[]{:T(128)}, f32[32,2,8,128,128]{3,4,2,1,0:T(8,128)}, ...), condition=%wide.region_11.12_spmd.clone, body=%wide.region_10.11_spmd.clone.sunk | while | flops 807403520 | bytes 13634143 | solution.py:38
  1235.3 5.5 fusion.300
  1249.6 5.7 fusion.300
  1264.0 5.6 fusion.300
  1278.3 5.5 fusion.300
  1314.4 5.5 fusion.300
  1321.5 5.6 fusion.300
  1328.6 5.6 fusion.300
  1335.8 5.6 fusion.300
  1364.6 5.5 fusion.300
  1371.7 5.6 fusion.300
  1386.0 5.5 fusion.300
  1407.8 5.5 fusion.300
  1414.9 5.5 fusion.300
  1422.0 5.6 fusion.300
  1429.2 5.6 fusion.300
  1436.3 5.5 fusion.300
  1450.8 5.5 fusion.300
  1462.0 79.5 %custom-call.14 = f32[2,8,1,64,64]{3,4,2,1,0:T(8,128)S(1)} custom-call(f32[2,8,1,64,64]{4,3,2,1,0:T(8,128)} %fusion.122), custom_call_target="InvertDiagBlocksLowerTriangular" | custom-call | tf_op jit(solution)/shard_map/transpose(jvp())/while/body/eval_jaxpr/checkpoint/triangular_solve | solution.py:114
  1610.6 8.3 convolution_bitcast_fusion.1
  1629.3 138.6 %reduce-scatter.10.cloned.1.call-done = f32[256,4096]{1,0:T(8,128)} async-done(((f32[1024,4096]{1,0:T(8,128)}), f32[256,4096]{1,0:T(8,128)}) %reduce-scatter.10.cloned.1.call-update) | async-done | bytes 4194320 | tf_op jit(solution)/shard_map/reduce_scatter | solution.py:306
  1774.7 6.4 fusion.78
  1782.8 12.8 all-reduce.29
  1801.8 19.4 reduce-scatter.12.cloned.1.call-done
  1821.1 124.7 %all-reduce.27 = (f32[256]{0:T(256)}, f32[4,1024]{1,0:T(4,128)}, f32[256,16]{0,1:T(8,128)}, f32[2]{0:T(128)}, f32[2]{0:T(128)}, /*index=5*/f32[64]{0:T(128)}, f32[256]{0:T(256)}) all-reduce(f32[256]{0:T(256)S(1)} %dynamic-slice.21, f32[4,1024]{1,0:T(4,128)S(1)} %copy.266, ...), channel_id=1, replica_groups=mesh['grp'=4,'ctx'=32] {'ctx'}, use_global_device_ids=true, to_apply=%region_28.30 | all-reduce | flops 8772 | bytes 70176 | tf_op jit(solution)/shard_map/psum | solution.py:318
  1945.8 62.1 %all-reduce.33.cloned.1.call-done = (f32[256,4096]{1,0:T(8,128)}, f32[256,2048]{1,0:T(8,128)}, f32[512,1024]{1,0:T(8,128)}, f32[256,5632]{1,0:T(8,128)}, f32[704,1024]{1,0:T(8,128)}) async-done(((f32[256,4096]{1,0:T(8,128)}, f32[256,2048]{1,0:T(8,128)}, f32[512,1024]{1,0:T(8,128)}, f32[256,5632]{1,0:T(8,128)}, f32[704,1024]{1,0:T(8,128)}), (f32[256,4096]{1,0:T(8,128)}, f32[256,2048]{1,0:T(8,128)}, ...) | async-done | bytes 17039376 | tf_op jit(solution)/shard_map/psum | solution.py:318
  (667 shorter events, 668.3 us)
Async XLA Ops:
  7.2 14.1 copy-start.111
  7.2 19.3 copy-start.99
  7.2 29.5 %copy-start.20 = (bf16[2,64,1024]{2,1,0:T(8,128)(2,1)S(1)}, bf16[2,64,1024]{2,1,0:T(8,128)(2,1)}, u32[]{:S(2)}) copy-start(bf16[2,64,1024]{2,1,0:T(8,128)(2,1)} %param.21) | copy-start | bytes 786436
  7.3 31.0 %copy-start.100 = (bf16[4,1024]{1,0:T(4,128)(2,1)S(1)}, bf16[4,1024]{1,0:T(4,128)(2,1)}, u32[]{:S(2)}) copy-start(bf16[4,1024]{1,0:T(4,128)(2,1)} %param.25) | copy-start | bytes 24580
  7.3 89.6 %all-gather.16.cloned.1.call-start = ((), (), s32[]{:S(2)}) async-start(), calls=%async_computation.7 | async-start | bytes 10485760 | tf_op jit(solution)/shard_map/all_gather | solution.py:180
  8.0 312.1 %all-gather.26.cloned.1.call-start = ((), (), s32[]{:S(2)}) async-start(), calls=%async_computation.18 | async-start | bytes 34603008 | tf_op jit(solution)/shard_map/all_gather | solution.py:26
  21.3 16.5 copy-start.113
  26.5 894.3 %copy-start.53 = (f32[4,1,256]{2,1,0:T(1,128)}, f32[4,1,256]{2,1,0:T(1,128)S(1)}, u32[]{:S(2)}) copy-start(f32[4,1,256]{2,1,0:T(1,128)S(1)} %convert_element_type.107) | copy-start | bytes 12292
  26.6 22.0 %copy-start.103 = (f32[8]{0:T(128)}, f32[8]{0:T(128)S(1)}, u32[]{:S(2)}) copy-start(f32[8]{0:T(128)S(1)} %convert_element_type.88) | copy-start | bytes 100
  36.7 64.9 %copy-start.73 = (bf16[1024,16]{0,1:T(8,128)(2,1)}, bf16[1024,16]{0,1:T(8,128)(2,1)S(1)}, u32[]{:S(2)}) copy-start(bf16[1024,16]{0,1:T(8,128)(2,1)S(1)} %all_gather.62) | copy-start | bytes 98308
  36.9 11.7 copy-start.105
  36.9 884.0 %copy-start.71 = (f32[2,64]{1,0:T(2,128)}, f32[2,64]{1,0:T(2,128)S(1)}, u32[]{:S(2)}) copy-start(f32[2,64]{1,0:T(2,128)S(1)} %fusion.215) | copy-start | bytes 1540
  37.8 156.8 %copy-start.57 = (f32[2,8,64]{2,1,0:T(8,128)}, f32[2,8,64]{2,1,0:T(8,128)S(1)}, u32[]{:S(2)}) copy-start(f32[2,8,64]{2,1,0:T(8,128)S(1)} %get-tuple-element.366) | copy-start | bytes 12292
  48.6 63.3 %copy-start.75 = (f32[64,64]{1,0:T(8,128)}, f32[64,64]{1,0:T(8,128)S(1)}, u32[]{:S(2)}) copy-start(f32[64,64]{1,0:T(8,128)S(1)} %get-tuple-element.548) | copy-start | bytes 49156
  48.6 63.3 %copy-start.77 = (f32[64,64]{1,0:T(8,128)}, f32[64,64]{1,0:T(8,128)S(1)}, u32[]{:S(2)}) copy-start(f32[64,64]{1,0:T(8,128)S(1)} %get-tuple-element.549) | copy-start | bytes 49156
  48.7 63.2 %copy-start.61 = (pred[64,64]{1,0:T(8,128)(4,1)}, pred[64,64]{1,0:T(8,128)(4,1)S(1)}, u32[]{:S(2)}) copy-start(pred[64,64]{1,0:T(8,128)(4,1)S(1)} %get-tuple-element.546) | copy-start | bytes 12292
  48.7 63.2 %copy-start.79 = (pred[64,64]{1,0:T(8,128)(4,1)}, pred[64,64]{1,0:T(8,128)(4,1)S(1)}, u32[]{:S(2)}) copy-start(pred[64,64]{1,0:T(8,128)(4,1)S(1)} %get-tuple-element.547) | copy-start | bytes 12292
  48.9 58.1 %copy-start.63 = (f32[1,4096]{1,0:T(1,128)}, f32[1,4096]{1,0:T(1,128)S(1)}, u32[]{:S(2)}) copy-start(f32[1,4096]{1,0:T(1,128)S(1)} %get-tuple-element.515) | copy-start | bytes 49156
  48.9 58.1 %copy-start.65 = (f32[1,4096]{1,0:T(1,128)}, f32[1,4096]{1,0:T(1,128)S(1)}, u32[]{:S(2)}) copy-start(f32[1,4096]{1,0:T(1,128)S(1)} %get-tuple-element.516) | copy-start | bytes 49156
  48.9 58.1 %copy-start.67 = (f32[1,4096]{1,0:T(1,128)}, f32[1,4096]{1,0:T(1,128)S(1)}, u32[]{:S(2)}) copy-start(f32[1,4096]{1,0:T(1,128)S(1)} %get-tuple-element.517) | copy-start | bytes 49156
  48.9 58.1 %copy-start.69 = (f32[1,4096]{1,0:T(1,128)}, f32[1,4096]{1,0:T(1,128)S(1)}, u32[]{:S(2)}) copy-start(f32[1,4096]{1,0:T(1,128)S(1)} %get-tuple-element.518) | copy-start | bytes 49156
  101.6 5.0 collective-permute-start
  111.3 83.2 %copy-start.26 = (f32[2,64,2048]{2,1,0:T(8,128)}, f32[2,64,2048]{2,1,0:T(8,128)S(1)}, u32[]{:S(2)}) copy-start(f32[2,64,2048]{2,1,0:T(8,128)S(1)} %slice.146) | copy-start | bytes 3145732
  111.7 82.8 %copy-start.81 = (f32[2,64,8]{1,2,0:T(8,128)}, f32[2,64,8]{1,2,0:T(8,128)S(1)}, u32[]{:S(2)}) copy-start(f32[2,64,8]{1,2,0:T(8,128)S(1)} %copy.205) | copy-start | bytes 12292
  111.9 108.5 %copy-start.6 = (f32[2,8,64,128]{3,2,1,0:T(8,128)}, f32[2,8,64,128]{3,2,1,0:T(8,128)S(1)}, u32[]{:S(2)}) copy-start(f32[2,8,64,128]{3,2,1,0:T(8,128)S(1)} %fusion.146) | copy-start | bytes 1572868
  204.5 318.8 %all-gather.28.cloned.1.call-start = ((), (), s32[]{:S(2)}) async-start(), calls=%async_computation.19 | async-start | bytes 69206016 | tf_op jit(solution)/shard_map/all_gather | solution.py:26
  207.6 669.3 %all-gather.18.cloned.1.call-start = ((), (), s32[]{:S(2)}) async-start(), calls=%async_computation.8 | async-start | bytes 5242880 | tf_op jit(solution)/shard_map/all_gather | solution.py:185
  208.2 673.5 %all-gather.20.cloned.1.call-start = ((), (), s32[]{:S(2)}) async-start(), calls=%async_computation.9 | async-start | bytes 5242880 | tf_op jit(solution)/shard_map/all_gather | solution.py:187
  208.8 676.2 %all-gather.22.cloned.1.call-start = ((), (), s32[]{:S(2)}) async-start(), calls=%async_computation.10 | async-start | bytes 14417920 | tf_op jit(solution)/shard_map/all_gather | solution.py:189
  209.4 683.5 %all-gather.24.cloned.1.call-start = ((), (), s32[]{:S(2)}) async-start(), calls=%async_computation.11 | async-start | bytes 7208960 | tf_op jit(solution)/shard_map/all_gather | solution.py:190
  210.2 746.3 %all-gather.30.cloned.1.call-start = ((), (), s32[]{:S(2)}) async-start(), calls=%async_computation.20 | async-start | bytes 34603008 | tf_op jit(solution)/shard_map/all_gather | solution.py:26
  211.6 911.3 %all-gather.32.cloned.1.call-start = ((), (), s32[]{:S(2)}) async-start(), calls=%async_computation.21 | async-start | bytes 69206016 | tf_op jit(solution)/shard_map/all_gather | solution.py:26
  218.8 714.1 %copy-start.95 = (f32[2,64]{1,0:T(2,128)}, f32[2,64]{1,0:T(2,128)S(1)}, u32[]{:S(2)}) copy-start(f32[2,64]{1,0:T(2,128)S(1)} %compare_convert_fusion) | copy-start | bytes 1540
  885.0 55.1 %copy-start.13 = (f32[2,64,1024]{2,1,0:T(8,128)}, f32[2,64,1024]{2,1,0:T(8,128)S(1)}, u32[]{:S(2)}) copy-start(f32[2,64,1024]{2,1,0:T(8,128)S(1)} %get-tuple-element.536) | copy-start | bytes 1572868
  907.6 19.1 copy-start.39
  920.8 708.4 %reduce-scatter.14.cloned.1.call-start = ((), (), s32[]{:S(2)}) async-start(), calls=%async_computation.14 | async-start | bytes 10485760 | tf_op jit(solution)/shard_map/reduce_scatter | solution.py:311
  926.6 702.7 %reduce-scatter.16.cloned.1.call-start = ((), (), s32[]{:S(2)}) async-start(), calls=%async_computation.15 | async-start | bytes 10485760 | tf_op jit(solution)/shard_map/reduce_scatter | solution.py:313
  932.8 696.5 %reduce-scatter.20.cloned.1.call-start = ((), (), s32[]{:S(2)}) async-start(), calls=%async_computation.17 | async-start | bytes 14417920 | tf_op jit(solution)/shard_map/reduce_scatter | solution.py:316
  940.0 689.3 %reduce-scatter.18.cloned.1.call-start = ((), (), s32[]{:S(2)}) async-start(), calls=%async_computation.16 | async-start | bytes 28835840 | tf_op jit(solution)/shard_map/reduce_scatter | solution.py:315
  952.5 815.4 %reduce-scatter.10.cloned.1.call-start = ((), (), s32[]{:S(2)}) async-start(), calls=%async_computation.12 | async-start | bytes 20971520 | tf_op jit(solution)/shard_map/reduce_scatter | solution.py:306
  990.5 23.5 %copy-start.30 = (f32[2,64,2048]{2,1,0:T(8,128)S(1)}, f32[2,64,2048]{2,1,0:T(8,128)}, u32[]{:S(2)}) copy-start(f32[2,64,2048]{2,1,0:T(8,128)} %copy-done.29) | copy-start | bytes 3145732
  1233.5 222.7 %copy-start.1 = (f32[2,8,256,128]{2,3,1,0:T(8,128)S(1)}, f32[2,8,256,128]{2,3,1,0:T(8,128)}, u32[]{:S(2)}) copy-start(f32[2,8,256,128]{2,3,1,0:T(8,128)} %copy-done) | copy-start | bytes 6291460
  1604.2 6.3 collective-permute-start.1
  1618.9 181.7 %reduce-scatter.22.cloned.1.call-start = ((), (), s32[]{:S(2)}) async-start(), calls=%async_computation.22 | async-start | bytes 2621440
  1627.7 193.4 %reduce-scatter.12.cloned.1.call-start = ((), (), s32[]{:S(2)}) async-start(), calls=%async_computation.13 | async-start | bytes 81920 | tf_op jit(solution)/shard_map/reduce_scatter | solution.py:308
  1629.0 379.0 %all-reduce.33.cloned.1.call-start = ((), (), s32[]{:S(2)}) async-start(), calls=%async_computation.23 | async-start | bytes 34078720 | tf_op jit(solution)/shard_map/psum | solution.py:318
  1781.1 14.9 copy-start.98
  1781.1 14.9 copy-start.40
  (118 other events, 350.9 us)
Sparse Core Ops, SparseCore 0:
  9.8 87.0 all-gather.15
  204.6 115.5 all-gather.25
  323.0 200.2 all-gather.27
  524.8 47.1 all-gather.17
  573.5 48.6 all-gather.19
  623.7 109.9 all-gather.21
  735.4 62.4 all-gather.23
  800.2 114.5 all-gather.29
  920.9 201.8 all-gather.31
  1125.2 79.4 reduce-scatter.13
  1207.1 80.3 reduce-scatter.15
  1289.8 105.7 reduce-scatter.19
  1398.0 198.4 reduce-scatter.17
  1619.0 148.8 reduce-scatter.9
  1770.7 29.8 reduce-scatter.21
  1803.5 17.6 reduce-scatter.11
  1825.6 182.3 all-reduce.32
where the time goes:
time: 2040 us; the launch traced here: 2030 us
  waiting for transfers between devices  683 us (33%)
  local copies, waits for them, and re-layouts  523 us (26%)
  matrix products  425 us (21%)
  other arithmetic  189 us (9%)
  blocking collectives  181 us (9%)
    all_gather x4, waiting for transfers between devices, carried_in(): pieces = jax.tree.map(lambda part: lax.all_gather(part, axis), value)  404 us
    dot_general x62, matrix products, compose(): jnp.einsum('bhrj,bhjk->bhrk', first_add, second_map, precision=precise)  280 us
    dynamic_slice x62, local copies, waits for them, and re-layouts, lap(): longer = join(total, jax.tree.map(lambda part: part[position], pieces))  187 us
    another operation x4, other arithmetic, span_update(): lax.linalg.triangular_solve(system, right_side, left_side=True, lower=Tru...  160 us
    reduce_scatter x1, waiting for transfers between devices, body(): lax.psum_scatter(grad_mixer_full, 'grp', scatter_dimension=0, tiled=True)  139 us
    psum x1, blocking collectives, body(): lax.psum((owners[0], owners[1], owners[2], owners[3], owners[4], owners[5...  125 us
    while x124, local copies, waits for them, and re-layouts  102 us
    all_gather x2, local copies, waits for them, and re-layouts, carried_in(): pieces = jax.tree.map(lambda part: lax.all_gather(part, axis), value)  100 us
  transfers between devices with their start and end apart: 19, of which 10 were waited for; matrix products, arithmetic and copies ran while one was open for 48% of the time, Pallas kernels for 0%

commit v1 on v0

v1 whole, which is shorter than its diff:
```python
import jax
import jax.numpy as jnp
from jax import lax
from jax.sharding import PartitionSpec as P

HEADS = 8
KEY_DIM = 128
HALF = 128
VALUE_DIM = 256
FF = 2816
CONV = 4
CHUNK = 128

epsilon = 1e-06
precise = lax.Precision.HIGHEST
f32 = jnp.float32
bf16 = jnp.bfloat16

CHIPS = [[chip * 2 + core for chip in range(16)] for core in range(2)]
OTHER_CORE = [(place, place ^ 1) for place in range(32)]
OTHER_SEQ = [(place, place ^ 16) for place in range(32)]


def dot(left, right, dims, precision=None):
    return lax.dot_general(left, right, (dims, ((), ())), precision=precision, preferred_element_type=f32)


def mm(left, right):
    return dot(left, right, ((1,), (0,)))


def mm_t(left, right):
    return dot(left, right, ((1,), (1,)))


def t_mm(left, right):
    return dot(left, right, ((0,), (0,)))


def other_core(value):
    return lax.ppermute(value, "ctx", OTHER_CORE)


def other_seq(value):
    return lax.ppermute(value, "ctx", OTHER_SEQ)


def along_grp(value, steps):
    return lax.ppermute(value, "grp", [(at, (at + steps) % 4) for at in range(4)])


def from_grp(value):
    return [value] + [along_grp(value, steps) for steps in (1, 2, 3)]


def in_grp_order(pieces, place):
    turned = [pieces[0], pieces[3], pieces[2], pieces[1]]
    doubled = jnp.stack(turned + turned[:3])
    return lax.dynamic_slice_in_dim(doubled, (4 - place) % 4, 4, axis=0)


def over_chips(value):
    return lax.all_to_all(value, "ctx", 0, 0, axis_index_groups=CHIPS)


def both_cores(mine, core, axis):
    theirs = other_core(mine)
    low = jnp.where(core == 0, mine, theirs)
    high = jnp.where(core == 0, theirs, mine)
    return jnp.stack([low, high], axis=axis)


def to_units(tokens, core):
    received = over_chips(jnp.repeat(tokens, 8, axis=0))
    return both_cores(received, core, 1).reshape(2048, tokens.shape[-1])


def sum_over_units(partial, core):
    split = partial.reshape(16, 2, 64, partial.shape[-1])
    keep = jnp.where(core == 0, split[:, 0], split[:, 1])
    give = jnp.where(core == 0, split[:, 1], split[:, 0]).astype(bf16)
    summed = (keep + other_core(give).astype(f32)).astype(bf16)
    received = over_chips(summed).astype(f32)
    return received.reshape(2, 8, 64, partial.shape[-1]).sum(axis=1)


def prepare(extended, taps):
    length = extended.shape[0] - (CONV - 1)
    mixed_conv = sum(taps[lag] * extended[lag : lag + length] for lag in range(CONV))
    active = jax.nn.silu(mixed_conv)
    queries, keys, values = active[:, :128], active[:, 128:256], active[:, 256:]
    queries = queries * lax.rsqrt(jnp.sum(queries * queries, axis=-1, keepdims=True) + epsilon) * KEY_DIM ** (-0.5)
    keys = keys * lax.rsqrt(jnp.sum(keys * keys, axis=-1, keepdims=True) + epsilon)
    return queries, keys, values


def ein(spec, *args):
    return jnp.einsum(spec, *args, precision=precise)


def inverse_unit_lower(lower):
    size = lower.shape[-1]
    rows = lax.broadcasted_iota(jnp.int32, (size, size), 0)
    cols = lax.broadcasted_iota(jnp.int32, (size, size), 1)
    result = jnp.where(rows == cols, 1.0, 0.0) - jnp.where((rows // 2 == cols // 2), lower, 0.0)
    block = 2
    while block < size:
        mask = (rows // (2 * block) == cols // (2 * block)) & (rows // block != cols // block)
        part = jnp.where(mask, lower, 0.0)
        result = result - ein("nij,njk->nik", result, ein("nij,njk->nik", part, result))
        block *= 2
    return result


def chunk_parts(queries, keys, values, beta, glog):
    total = jnp.cumsum(glog, axis=1)
    rows = lax.broadcasted_iota(jnp.int32, (CHUNK, CHUNK), 0)
    cols = lax.broadcasted_iota(jnp.int32, (CHUNK, CHUNK), 1)
    gaps = total[:, :, None] - total[:, None, :]
    decay = jnp.where(cols <= rows, jnp.exp(jnp.where(cols <= rows, gaps, 0.0)), 0.0)
    lower = jnp.where(cols < rows, decay, 0.0) * ein("nid,njd->nij", keys, keys) * beta[:, :, None]
    inverse = inverse_unit_lower(lower)
    growth = jnp.exp(total)[:, :, None]
    to_end = jnp.exp(total[:, -1:] - total)[:, :, None]
    ending = jnp.exp(total[:, -1])[:, None, None]
    keys_grown = beta[:, :, None] * growth * keys
    from_state = ein("nij,njd->nid", inverse, keys_grown)
    local = ein("nij,njd->nid", inverse, beta[:, :, None] * values)
    scores = ein("nid,njd->nij", queries, keys) * decay
    keys_end = to_end * keys
    transfer = ending * jnp.eye(KEY_DIM, dtype=f32) - ein("nik,nid->nkd", keys_end, from_state)
    added = ein("nik,nir->nkr", keys_end, local)
    probe = growth * queries - ein("nij,njd->nid", scores, from_state)
    return dict(
        decay=decay, inverse=inverse, growth=growth, to_end=to_end, ending=ending, keys_grown=keys_grown,
        from_state=from_state, local=local, scores=scores, keys_end=keys_end, transfer=transfer, added=added,
        probe=probe,
    )


def delta_forward(queries, keys, values, beta, glog):
    parts = chunk_parts(queries, keys, values, beta, glog)

    def step(state, piece):
        transfer, added = piece
        return jnp.matmul(transfer, state, precision=precise) + added, state

    _, states = lax.scan(step, jnp.zeros((KEY_DIM, HALF), f32), (parts["transfer"], parts["added"]))
    updates = parts["local"] - ein("nid,ndr->nir", parts["from_state"], states)
    outputs = parts["growth"] * ein("nid,ndr->nir", queries, states) + ein("nij,njr->nir", parts["scores"], updates)
    return outputs, parts, states, updates


def delta_backward(queries, keys, values, beta, parts, states, updates, grads):
    local = ein("nid,nir->ndr", parts["probe"], grads)

    def step(after, piece):
        transfer, added = piece
        return jnp.matmul(transfer.T, after, precision=precise) + added, after

    _, afters = lax.scan(step, jnp.zeros((KEY_DIM, HALF), f32), (parts["transfer"], local), reverse=True)
    rows = lax.broadcasted_iota(jnp.int32, (CHUNK, CHUNK), 0)
    cols = lax.broadcasted_iota(jnp.int32, (CHUNK, CHUNK), 1)
    d_updates = ein("nij,nir->njr", parts["scores"], grads) + ein("nid,ndr->nir", parts["keys_end"], afters)
    right = ein("nij,nir->njr", parts["inverse"], d_updates)
    d_scores = ein("nir,njr->nij", grads, updates) * parts["decay"]
    d_lower = jnp.where(cols < rows, -ein("nir,njr->nij", right, updates) * parts["decay"], 0.0)
    bcol = beta[:, :, None]
    q_state = parts["growth"] * ein("nir,ndr->nid", grads, states)
    q_keys = ein("nij,njd->nid", d_scores, keys)
    k_queries = ein("nij,nid->njd", d_scores, queries)
    k_rows = ein("nij,njd->nid", d_lower, keys)
    k_cols = ein("nij,nid->njd", d_lower, bcol * keys)
    k_state = parts["growth"] * ein("nir,ndr->nid", right, states)
    k_end = parts["to_end"] * ein("nir,ndr->nid", updates, afters)
    d_queries = q_state + q_keys
    d_keys = k_queries + bcol * k_rows + k_cols + k_end - bcol * k_state
    d_values = bcol * right
    k_sum = lambda value: jnp.sum(keys * value, axis=-1)
    d_beta = k_sum(k_rows) - k_sum(k_state) + jnp.sum(right * values, axis=-1)
    ends = k_sum(k_end)
    d_total = (
        jnp.sum(queries * d_queries, axis=-1)
        - k_sum(k_queries)
        + beta * k_sum(k_rows)
        - k_sum(k_cols)
        - beta * k_sum(k_state)
        - ends
    )
    d_last = jnp.sum(ends, axis=1) + parts["ending"][:, 0, 0] * jnp.sum(states * afters, axis=(1, 2))
    d_total = d_total.at[:, -1].add(d_last)
    d_glog = jnp.flip(jnp.cumsum(jnp.flip(d_total, 1), axis=1), 1)
    return d_queries, d_keys, d_values, d_beta, d_glog


def body(
    block_input,
    seq_lengths,
    in_gain,
    w_mixer,
    conv_weight,
    w_rates,
    decay_scale,
    decay_bias,
    w_outgate,
    head_gain,
    w_output,
    mlp_gain,
    w_gateup,
    w_down,
    cotangent,
):
    place = lax.axis_index("ctx")
    grp = lax.axis_index("grp")
    core = place % 2
    head = (place % 16) // 2
    seq = place // 16

    small = jnp.concatenate(
        [
            w_rates.reshape(-1),
            conv_weight.reshape(-1),
            in_gain,
            mlp_gain,
            head_gain,
            decay_scale,
            decay_bias,
            jnp.zeros((60,), bf16),
        ]
    ).reshape(-1, 128)
    small = in_grp_order(from_grp(small), grp).reshape(4, -1)
    rates_full = small[:, :4096].reshape(1024, 16)
    conv_full = small[:, 4096:8192].reshape(4, 4, 1024).transpose(1, 0, 2).reshape(4, 4096).astype(f32)
    gain_one = small[:, 8192:8448].reshape(1024).astype(f32)
    gain_two = small[:, 8448:8704].reshape(1024).astype(f32)
    head_full = small[:, 8704:8768].reshape(256).astype(f32)
    scale_full = small[:, 8768:8770].reshape(8).astype(f32)
    bias_full = small[:, 8770:8772].reshape(8).astype(f32)

    def unit_columns(value, width=128):
        q_part = lax.dynamic_slice_in_dim(value, head * 128, 128, axis=1)
        k_part = lax.dynamic_slice_in_dim(value, 1024 + head * 128, 128, axis=1)
        v_part = lax.dynamic_slice_in_dim(value, 2048 + place % 16 * 128, 128, axis=1)
        return jnp.concatenate([q_part, k_part, v_part], axis=1)

    outgate_part = lax.dynamic_slice_in_dim(w_outgate, place % 16 * 128, 128, axis=1)
    unit_part = jnp.concatenate([unit_columns(w_mixer), outgate_part], axis=1)
    w_unit = in_grp_order(from_grp(unit_part), grp).reshape(1024, 512)
    w_unit_rates = jnp.stack(
        [
            lax.dynamic_index_in_dim(rates_full, head, 1, False),
            lax.dynamic_index_in_dim(rates_full, 8 + head, 1, False),
        ],
        axis=1,
    )
    taps = unit_columns(conv_full)
    scale = lax.dynamic_index_in_dim(scale_full, head, 0, False)
    bias = lax.dynamic_index_in_dim(bias_full, head, 0, False)
    head_half = lax.dynamic_slice_in_dim(head_full, core * 128, 128, axis=0)

    def ff_columns(owner):
        at = owner * 704 + core * 352
        gate = lax.dynamic_slice_in_dim(w_gateup, at, 352, axis=1)
        up = lax.dynamic_slice_in_dim(w_gateup, FF + at, 352, axis=1)
        return jnp.concatenate([gate, up], axis=1)

    gateup_pieces = [ff_columns(grp)] + [along_grp(ff_columns((grp + steps) % 4), steps) for steps in (1, 2, 3)]
    w_gu = in_grp_order(gateup_pieces, grp).reshape(1024, 704)
    w_dn = lax.dynamic_slice_in_dim(w_down, core * 352, 352, axis=0)
    output_full = lax.all_gather(w_output, "grp", axis=0, tiled=True)
    output_unit = lax.dynamic_slice_in_dim(output_full, place % 16 * 128, 128, axis=0)

    positions = place * 64 + lax.broadcasted_iota(jnp.int32, (2, 64), 1)
    valid = (positions < seq_lengths[:, None]).astype(f32)[..., None]
    inputs_f = block_input.astype(f32)
    inputs_rows = inputs_f.reshape(128, 1024)
    r_one = lax.rsqrt(jnp.mean(inputs_rows * inputs_rows, axis=-1, keepdims=True) + epsilon)
    dy = (cotangent.astype(f32) * valid).reshape(128, 1024)
    dy_low = dy.astype(bf16)

    x_unit = to_units(block_input, core).astype(f32)
    r_unit = lax.rsqrt(jnp.mean(x_unit * x_unit, axis=-1, keepdims=True) + epsilon)
    hidden_one = (x_unit * r_unit * gain_one).astype(bf16)
    projected = mm(hidden_one, w_unit)
    mixed_in = projected[:, :384].astype(bf16)
    outgate = projected[:, 384:]
    rate_logits = mm(hidden_one, w_unit_rates)
    extended = jnp.concatenate([jnp.zeros((3, 384), bf16), mixed_in], axis=0).astype(f32)
    (queries, keys, values), prepare_back = jax.vjp(prepare, extended, taps)
    beta = jax.nn.sigmoid(rate_logits[:, 0])
    decay_in = rate_logits[:, 1] + bias
    glog = -jnp.exp(scale) * jax.nn.softplus(decay_in)
    chunked = lambda value: value.reshape((16, CHUNK) + value.shape[1:])
    queries, keys, values, beta_c, glog_c = map(chunked, (queries, keys, values, beta, glog))
    heads_out, parts, states, updates = delta_forward(queries, keys, values, beta_c, glog_c)
    heads_out = heads_out.reshape(2048, HALF)
    squares = jnp.sum(heads_out * heads_out, axis=-1)
    r_head = lax.rsqrt((squares + other_core(squares)) / VALUE_DIM + epsilon)[:, None]
    normed = heads_out * r_head
    sg = jax.nn.silu(outgate)
    gated = (normed * head_half * sg).astype(bf16)

    gated_tokens = lax.all_to_all(gated.reshape(32, 64, 128), "ctx", 0, 0)
    gated_tokens = gated_tokens.reshape(2, 16, 64, 128).transpose(0, 2, 1, 3).reshape(128, 2048)
    middle = inputs_rows + mm(gated_tokens, output_full)
    r_two = lax.rsqrt(jnp.mean(middle * middle, axis=-1, keepdims=True) + epsilon)
    hidden_two = (middle * r_two * gain_two).astype(bf16)

    def to_wide(tokens):
        mine = jnp.concatenate(from_grp(tokens), axis=0)
        return jnp.concatenate([mine, other_core(mine)], axis=0)

    def from_wide(partial):
        mine = partial[:512] + other_core(partial[512:].astype(bf16)).astype(f32)
        low = mine.reshape(4, 128, 1024).astype(bf16)
        total = mine[:128]
        for steps in (1, 2, 3):
            total = total + along_grp(low[steps], -steps).astype(f32)
        return total

    dy_wide = to_wide(dy_low)
    two_wide = to_wide(hidden_two)
    gateup = mm(two_wide, w_gu)
    gate, up = gateup[:, :352], gateup[:, 352:]
    sig = jax.nn.sigmoid(gate)
    silu_gate = gate * sig
    swi = (silu_gate * up).astype(bf16)
    dswi = mm_t(dy_wide, w_dn)
    dgate = dswi * up * (sig * (1.0 + gate * (1.0 - sig)))
    dgateup = jnp.concatenate([dgate, dswi * silu_gate], axis=1).astype(bf16)
    dhidden_two = from_wide(mm_t(dgateup, w_gu))
    scaled = dhidden_two * gain_two
    dmiddle = dy + r_two * scaled - middle * r_two**3 * jnp.mean(scaled * middle, axis=-1, keepdims=True)
    dmix = dmiddle.astype(bf16)
    dmix_unit = to_units(dmix.reshape(2, 64, 1024), core)

    block_out = middle + from_wide(mm(swi, w_dn))
    block_output = (block_out.reshape(2, 64, 1024) * valid).astype(bf16)

    g_gu = t_mm(two_wide, dgateup)
    g_dn = t_mm(dy_wide, swi)
    g_ff = jnp.concatenate([g_gu, g_dn], axis=1).reshape(4, 16, 16, 1056).transpose(1, 0, 2, 3)
    g_ff = lax.psum_scatter(g_ff.reshape(1024, 1056), "ctx", scatter_dimension=0, tiled=True, axis_index_groups=CHIPS)
    g_ff = g_ff.astype(bf16).reshape(4, 16, 1056)
    g_gu_low = g_ff[:, :, :704]
    g_gu_pieces = [lax.dynamic_index_in_dim(g_gu_low, grp, 0, False)] + [
        along_grp(lax.dynamic_index_in_dim(g_gu_low, (grp + steps) % 4, 0, False), steps) for steps in (1, 2, 3)
    ]
    g_gu_mine = in_grp_order(g_gu_pieces, grp)
    ff_payload = jnp.concatenate([g_gu_mine, g_ff[:, :, 704:]], axis=2)
    ff_all = lax.all_gather(ff_payload, "ctx")
    ff_all = ff_all.reshape(16, 2, 4, 16, 1056).astype(f32)
    grad_gateup = ff_all[..., :704].reshape(16, 2, 4, 16, 2, 352).transpose(0, 3, 4, 2, 1, 5).reshape(256, 5632)
    grad_down = ff_all[..., 704:].transpose(1, 4, 2, 0, 3).reshape(704, 1024)
    grad_mlp_gain = jnp.sum(grad_gateup * w_gateup.astype(f32), axis=1) / mlp_gain.astype(f32)

    dgated = mm_t(dmix_unit, output_unit)
    g_output = t_mm(gated, dmix_unit)
    g_head = jnp.sum(dgated * normed * sg, axis=0)
    sig_og = jax.nn.sigmoid(outgate)
    doutgate = (dgated * head_half * normed * (sig_og * (1.0 + outgate * (1.0 - sig_og)))).astype(bf16)
    dnormed = dgated * head_half * sg
    inner = jnp.sum(dnormed * heads_out, axis=-1)
    inner = ((inner + other_core(inner)) / VALUE_DIM)[:, None]
    dheads = r_head * dnormed - heads_out * r_head**3 * inner
    d_queries, d_keys, d_values, d_beta, d_glog = delta_backward(
        queries, keys, values, beta_c, parts, states, updates, chunked(dheads)
    )
    flat = lambda value: value.reshape((2048,) + value.shape[2:])
    d_ext, g_taps = prepare_back((flat(d_queries), flat(d_keys), flat(d_values)))
    d_ext = jnp.concatenate([d_ext[3:], jnp.zeros((0, 384), f32)], axis=0)
    dmixed = d_ext.astype(bf16)
    d_glog, d_beta = flat(d_glog), flat(d_beta)
    d_decay = -d_glog * jnp.exp(scale) * jax.nn.sigmoid(decay_in)
    g_scale = jnp.sum(d_glog * glog)
    g_bias = jnp.sum(d_decay)
    drates = jnp.stack([d_beta * beta * (1.0 - beta), d_decay], axis=1).astype(bf16)
    d_unit = jnp.concatenate([dmixed, doutgate], axis=1)
    dhidden_one = mm_t(d_unit, w_unit) + mm_t(drates, w_unit_rates)
    g_unit = t_mm(hidden_one, d_unit)
    g_rates = t_mm(drates, hidden_one)

    dhidden_one = sum_over_units(dhidden_one, core).reshape(128, 1024)
    scaled = dhidden_one * gain_one
    input_grad = (
        dmiddle + r_one * scaled - inputs_rows * r_one**3 * jnp.mean(scaled * inputs_rows, axis=-1, keepdims=True)
    )

    g_low = g_unit.astype(bf16).reshape(4, 256, 512)
    g_sum = lax.dynamic_index_in_dim(g_unit.reshape(4, 256, 512), grp, 0, False)
    for steps in (1, 2, 3):
        piece = lax.dynamic_index_in_dim(g_low, (grp + steps) % 4, 0, False)
        g_sum = g_sum + along_grp(piece, steps).astype(f32)
    rows = g_sum.reshape(2, 128, 512)
    mine = lax.dynamic_index_in_dim(rows, seq, 0, False)
    given = lax.dynamic_index_in_dim(rows, 1 - seq, 0, False).astype(bf16)
    mine = mine + other_seq(given).astype(f32)
    halves = mine[:, :256].reshape(2, 64, 256)
    qk_mine = lax.dynamic_index_in_dim(halves, core, 0, False)
    qk_given = lax.dynamic_index_in_dim(halves, 1 - core, 0, False).astype(bf16)
    qk_mine = qk_mine + other_core(qk_given).astype(f32)
    unit_payload = jnp.concatenate([qk_mine.reshape(128, 128), mine[:, 256:384], mine[:, 384:]], axis=1).astype(bf16)
    unit_all = lax.all_gather(unit_payload, "ctx").reshape(2, 8, 2, 128, 384).astype(f32)
    qk_all = unit_all[..., :128].reshape(2, 8, 2, 64, 2, 128)
    grad_qk = qk_all.transpose(0, 2, 3, 4, 1, 5).reshape(256, 2048)
    grad_v = unit_all[..., 128:256].transpose(0, 3, 1, 2, 4).reshape(256, 2048)
    grad_outgate = unit_all[..., 256:].transpose(0, 3, 1, 2, 4).reshape(256, 2048)
    grad_mixer = jnp.concatenate([grad_qk, grad_v], axis=1)

    rows = g_output.reshape(2, 64, 1024)
    mine = lax.dynamic_index_in_dim(rows, seq, 0, False)
    given = lax.dynamic_index_in_dim(rows, 1 - seq, 0, False).astype(bf16)
    mine = (mine + other_seq(given).astype(f32)).reshape(4, 16, 1024)
    low = mine.astype(bf16)
    total = lax.dynamic_index_in_dim(mine, grp, 0, False)
    for steps in (1, 2, 3):
        piece = lax.dynamic_index_in_dim(low, (grp + steps) % 4, 0, False)
        total = total + along_grp(piece, steps).astype(f32)
    moves = []
    for at in range(4):
        for s_at in range(2):
            for h_at in range(8):
                for v_at in range(2):
                    source = at * 32 + s_at * 16 + h_at * 2 + v_at
                    target = (h_at // 2) * 32 + s_at * 16 + ((h_at % 2) * 4 + at) * 2 + v_at
                    moves.append((source, target))
    total = lax.ppermute(total.astype(bf16), ("grp", "ctx"), moves)
    output_all = lax.all_gather(total, "ctx").reshape(2, 2, 4, 2, 16, 1024)
    grad_output = output_all.transpose(1, 3, 0, 2, 4, 5).reshape(512, 1024).astype(f32)

    spread = jnp.zeros((4, 4096), f32)
    spread = lax.dynamic_update_slice(spread, g_taps[:, :128], (0, head * 128))
    spread = lax.dynamic_update_slice(spread, g_taps[:, 128:256], (0, 1024 + head * 128))
    spread = lax.dynamic_update_slice(spread, g_taps[:, 256:], (0, 2048 + place % 16 * 128))
    rates_spread = jnp.zeros((2, 8, 1024), f32)
    rates_spread = lax.dynamic_update_slice(rates_spread, g_rates[:, None], (0, head, 0))
    head_spread = lax.dynamic_update_slice(jnp.zeros((256,), f32), g_head, (core * 128,))
    scale_spread = jnp.where(jnp.arange(8) == head, g_scale, 0.0)
    bias_spread = jnp.where(jnp.arange(8) == head, g_bias, 0.0)
    spread, rates_spread, head_spread, scale_spread, bias_spread = lax.psum(
        (spread, rates_spread, head_spread, scale_spread, bias_spread), ("grp", "ctx")
    )
    grad_conv = lax.dynamic_slice_in_dim(spread, grp * 1024, 1024, axis=1)
    grad_rates = lax.dynamic_slice_in_dim(rates_spread.reshape(16, 1024), grp * 256, 256, axis=1).T
    grad_head = lax.dynamic_slice_in_dim(head_spread, grp * 64, 64, axis=0)
    grad_scale = lax.dynamic_slice_in_dim(scale_spread, grp * 2, 2, axis=0)
    grad_bias = lax.dynamic_slice_in_dim(bias_spread, grp * 2, 2, axis=0)
    grad_in_gain = (
        jnp.sum(grad_mixer * w_mixer.astype(f32), axis=1)
        + jnp.sum(grad_outgate * w_outgate.astype(f32), axis=1)
        + jnp.sum(grad_rates * w_rates.astype(f32), axis=1)
    ) / in_gain.astype(f32)

    return (
        block_output,
        input_grad.reshape(2, 64, 1024),
        grad_in_gain,
        grad_mixer,
        grad_conv,
        grad_rates,
        grad_scale,
        grad_bias,
        grad_outgate,
        grad_head,
        grad_output,
        grad_mlp_gain,
        grad_gateup,
        grad_down,
    )


def solution(mesh):
    placed = (
        P("grp", "ctx", None),
        P("grp"),
        P("grp"),
        P("grp", None),
        P(None, "grp"),
        P("grp", None),
        P("grp"),
        P("grp"),
        P("grp", None),
        P("grp"),
        P("grp", None),
        P("grp"),
        P("grp", None),
        P("grp", None),
        P("grp", "ctx", None),
    )
    return jax.shard_map(
        body,
        mesh=mesh,
        in_specs=placed,
        out_specs=(
            P("grp", "ctx", None),
            P("grp", "ctx", None),
            P("grp"),
            P("grp", None),
            P(None, "grp"),
            P("grp", None),
            P("grp"),
            P("grp"),
            P("grp", None),
            P("grp"),
            P("grp", None),
            P("grp"),
            P("grp", None),
            P("grp", None),
        ),
        check_vma=False,
    )
```

time: 2040 us -> 854 us (0.42)
  waiting for transfers between devices: 683 us -> 158 us
  local copies, waits for them, and re-layouts: 523 us -> 186 us
  matrix products: 425 us -> 160 us
  starting transfers between devices: 6.46 us -> 73 us
  blocking collectives: 181 us -> 116 us
  other arithmetic: 189 us -> 130 us
    all_gather x9 -> x4, waiting for transfers between devices: 452 us -> 87.9 us  [the longest x1 42.2 us: body(): lax.all_gather(unit_payload, 'ctx').reshape(2, 8, 2, 128, 384).astype(f32)]
    dot_general x103 -> x82, matrix products: 420 us -> 160 us  [the longest x35 73.9 us: ein(): return jnp.einsum(spec, *args, precision=precise)]
    dynamic_slice x62 -> x16, local copies, waits for them, and re-layouts: 187 us -> 16.6 us  [the longest x2 3.7 us: body(): lax.dynamic_index_in_dim(rates_full, head, 1, False)]
    reduce_scatter x6 -> x1, waiting for transfers between devices: 158 us -> 0.02 us  [body(): lax.psum_scatter(g_ff.reshape(1024, 1056), 'ctx', scatter_dimension=0, ti...]
    another operation x9, other arithmetic: 162 us -> 11.4 us  [the longest x4 160 us: span_update(): lax.linalg.triangular_solve(system, right_side, left_side=True, lower=Tru...]
    all_gather x2 -> x0, local copies, waits for them, and re-layouts: 100 us -> none  [carried_in(): pieces = jax.tree.map(lambda part: lax.all_gather(part, axis), value)]
    while x124 -> x32, local copies, waits for them, and re-layouts: 102 us -> 13.5 us
    rev x2 -> x3, local copies, waits for them, and re-layouts: 67.9 us -> 0.14 us  [delta_backward(): d_glog = jnp.flip(jnp.cumsum(jnp.flip(d_total, 1), axis=1), 1)]
  transfers between devices with their start and end apart: 19 -> 52, of which waited for: 10 -> 23; matrix products, arithmetic and copies ran while one was open for 48% -> 46% of each run, Pallas kernels for 0% -> 0%
where the time goes in v1:
time: 854 us; the launch traced here: 842 us
  local copies, waits for them, and re-layouts  186 us (22%)
  matrix products  160 us (19%)
  waiting for transfers between devices  158 us (19%)
  other arithmetic  130 us (15%)
  blocking collectives  116 us (14%)
  starting transfers between devices  73 us (9%)
  between operations  17.8 us (2%)
    psum x1, blocking collectives, body(): lax.psum((spread, rates_spread, head_spread, scale_spread, bias_spread),...  85 us
    dot_general x35, matrix products, ein(): return jnp.einsum(spec, *args, precision=precise)  73.9 us
    ppermute x30, waiting for transfers between devices, along_grp(): lax.ppermute(value, 'grp', [(at, (at + steps) % 4) for at in range(4)])  55.2 us
    unnamed x352, local copies, waits for them, and re-layouts  46.3 us
    all_gather x1, waiting for transfers between devices, body(): lax.all_gather(unit_payload, 'ctx').reshape(2, 8, 2, 128, 384).astype(f32)  42.2 us
    dot_general x15, matrix products, dot(): lax.dot_general(left, right, (dims, ((), ())), precision=precision, prefe...  40.4 us
    ppermute x30, starting transfers between devices, along_grp(): lax.ppermute(value, 'grp', [(at, (at + steps) % 4) for at in range(4)])  34.8 us
    all_gather x1, waiting for transfers between devices, body(): output_all = lax.all_gather(total, 'ctx').reshape(2, 2, 4, 2, 16, 1024)  32.4 us
  transfers between devices with their start and end apart: 52, of which 23 were waited for; matrix products, arithmetic and copies ran while one was open for 46% of the time, Pallas kernels for 0%

profile of v1, /device:TPU:1, one launch (start us, length us, event | category | flops | bytes accessed | tf_op | source)
XLA Modules:
  0.0 841.6 jit_solution(11201969793149576936)
XLA Ops:
  9.0 4.0 concatenate.72
  27.1 6.8 all-to-all-start
  99.1 5.6 collective-permute-done.6
  116.5 4.0 maximum_convert_fusion
  134.3 8.2 fusion.22
  172.8 50.9 %while.31 = (s32[]{:T(128)}, f32[128,128]{1,0:T(8,128)}, f32[16,128,128]{2,1,0:T(8,128)}, f32[16,128,128]{2,1,0:T(8,128)}, f32[16,128,128]{2,1,0:T(8,128)}, /*index=5*/s32[]{:T(128)}, s32[]{:T(128)}) while((s32[]{:T(128)}, f32[128,128]{1,0:T(8,128)}, f32[16,128,128]{2,1,0:T(8,128)}, f32[16,128,128]{2,1,0:T(8,128)}, ...), condition=%wide.region_5.6_spmd.clone, body=%wide.region_4.5_spmd.clone.sunk | while | flops 25214980 | bytes 525923 | solution.py:148
  236.4 7.6 all-to-all-start.1
  249.3 6.3 all-to-all-done.1
  264.0 4.8 collective-permute-done.10
  270.3 6.7 collective-permute-done.8
  298.9 6.5 collective-permute-done.26
  305.6 4.0 collective-permute-done.16
  309.6 7.1 collective-permute-done.18
  318.3 30.6 %all_to_all.20 = bf16[16,64,1024]{2,1,0:T(8,128)(2,1)} all-to-all(bf16[16,64,1024]{2,1,0:T(8,128)(2,1)S(1)} %bitcast.432), channel_id=1, replica_groups={{0,2,4,6,8,10,12,14,16,18,20,22,24,26,28,30},{1,3,5,7,9,11,13,15,17,19,..., dimensions={0} | all-to-all | bytes 4194304 | tf_op jit(solution)/shard_map/all_to_all | solution.py:63
  363.0 5.6 copy.227
  368.7 5.0 copy.228
  379.4 4.0 multiply_reduce_fusion.8
  400.0 29.8 %while.32 = (s32[]{:T(128)}, f32[128,128]{1,0:T(8,128)S(1)}, f32[16,128,128]{2,1,0:T(8,128)}, f32[16,128,128]{2,1,0:T(8,128)}, f32[16,128,128]{2,1,0:T(8,128)}, /*index=5*/s32[]{:T(128)}, s32[]{:T(128)}, s32[]{:T(128)}) while((s32[]{:T(128)}, f32[128,128]{1,0:T(8,128)S(1)}, f32[16,128,128]{2,1,0:T(8,128)}, ...), condition=%wide.region_12.13_spmd.clone, body=%wide.region_11.12_spmd.clone.sunk | while | flops 25214980 | bytes 525943 | solution.py:161
  432.9 4.2 broadcast_multiply_fusion.4
  451.0 3.7 multiply_reduce_fusion.23
  458.4 3.6 multiply_reduce_fusion.6
  467.1 6.9 broadcast_multiply_fusion
  482.7 5.7 fusion.21
  489.3 4.6 fusion.155
  503.1 5.9 collective-permute-done.31
  510.9 3.7 collective-permute-done.33
  514.6 5.1 collective-permute-start.34
  524.1 4.7 fusion.143
  534.1 5.8 convolution_add_fusion.2
  542.2 3.8 collective-permute-done.29
  548.6 5.7 all-to-all-start.3
  556.7 85.0 %all-reduce.12 = (f32[8]{0:T(128)S(1)}, f32[8]{0:T(128)S(1)}, f32[256]{0:T(256)S(1)}) all-reduce(f32[8]{0:T(128)S(1)} %compare_select_fusion.2, f32[8]{0:T(128)S(1)} %compare_select_fusion.1, f32[256]{0:T(256)S(1)} %dynamic_update_slice.32), channel_id=1, replica_groups=mesh['grp'=4,'ctx'=32] {'grp','ctx'}, use_global_device_ids=true, to_apply=%region_37.38 | all-reduce | flops 272 | bytes 2176 | tf_op jit(solution)/shard_map/psum | solution.py:440
  646.1 32.4 %all-gather.11.cloned.1.call-done = bf16[512,1024]{1,0:T(8,128)(2,1)} async-done(((bf16[16,1024]{1,0:T(8,128)(2,1)}), bf16[512,1024]{1,0:T(8,128)(2,1)}) %all-gather.11.cloned.1.call-update) | async-done | bytes 1048592 | tf_op jit(solution)/shard_map/all_gather | solution.py:428
  683.5 42.2 %all-gather.9.cloned.1.call-done = bf16[32,128,384]{2,1,0:T(8,128)(2,1)} async-done(((bf16[1,128,384]{2,1,0:T(8,128)(2,1)}), bf16[32,128,384]{2,1,0:T(8,128)(2,1)}) %all-gather.9.cloned.1.call-update) | async-done | bytes 3145744 | tf_op jit(solution)/shard_map/all_gather | solution.py:403
  728.0 3.5 convert.58
  734.1 3.9 slice_bitcast_fusion.1
  744.0 5.3 copy.222
  749.3 4.1 reshape.670
  761.2 13.2 %all-gather.13.cloned.1.call-done = bf16[128,16,1056]{2,1,0:T(8,128)(2,1)} async-done(((bf16[4,16,1056]{2,1,0:T(8,128)(2,1)}), bf16[128,16,1056]{2,1,0:T(8,128)(2,1)}) %all-gather.13.cloned.1.call-update) | async-done | bytes 4325392 | tf_op jit(solution)/shard_map/all_gather | solution.py:351
  774.4 5.5 slice.292
  780.0 4.9 convert.59
  784.8 9.0 %reshape.681 = f32[16,2,4,16,2,352]{5,4,3,2,1,0:T(2,128)} reshape(f32[16,2,4,16,704]{4,3,2,1,0:T(8,128)} %slice.292) | data formatting | bytes 11534336 | tf_op jit(solution)/shard_map/reshape | solution.py:353
  793.8 10.3 %copy.229 = f32[16,16,2,4,2,352]{5,4,3,2,1,0:T(2,128)} copy(f32[16,16,2,4,2,352]{5,2,1,3,4,0:T(2,128)} %bitcast.422) | data formatting | bytes 11534336 | tf_op jit(solution)/shard_map/transpose | solution.py:353
  804.1 9.5 %reshape.682 = f32[256,5632]{1,0:T(8,128)} reshape(f32[16,16,2,4,2,352]{5,4,3,2,1,0:T(2,128)} %copy.229) | data formatting | bytes 11534336 | tf_op jit(solution)/shard_map/reshape | solution.py:353
  813.6 4.2 multiply_reduce_fusion.1
  821.4 4.1 copy.230
  825.6 5.5 reshape.683
  831.1 3.4 copy.231
  (779 shorter events, 396.3 us)
Async XLA Ops:
  7.2 250.6 %all-gather.7.cloned.1.call-start = ((), (), s32[]{:S(2)}) async-start(), calls=%async_computation.5 | async-start | bytes 5242880 | tf_op jit(solution)/shard_map/all_gather | solution.py:270
  13.1 46.1 %collective-permute-start.2 = (bf16[69,128]{1,0:T(8,128)(2,1)}, bf16[69,128]{1,0:T(8,128)(2,1)}, u32[]{:S(2)}, u32[]{:S(2)}) collective-permute-start(bf16[69,128]{1,0:T(8,128)(2,1)} %bitcast.2), channel_id=1, source_target_pairs={{0,32},{32,64},{64,96},{96,0},{1,33},{33,65},{65,97},{97,1},{2,34}... | collective-permute-start | bytes 53000 | tf_op jit(solution)/shard_map/ppermute | solution.py:49
  15.5 39.6 %collective-permute-start.1 = (bf16[69,128]{1,0:T(8,128)(2,1)}, bf16[69,128]{1,0:T(8,128)(2,1)}, u32[]{:S(2)}, u32[]{:S(2)}) collective-permute-start(bf16[69,128]{1,0:T(8,128)(2,1)} %bitcast.2), channel_id=1, source_target_pairs={{0,64},{32,96},{64,0},{96,32},{1,65},{33,97},{65,1},{97,33},{2,66}... | collective-permute-start | bytes 53000 | tf_op jit(solution)/shard_map/ppermute | solution.py:49
  18.8 35.0 %collective-permute-start = (bf16[69,128]{1,0:T(8,128)(2,1)}, bf16[69,128]{1,0:T(8,128)(2,1)}, u32[]{:S(2)}, u32[]{:S(2)}) collective-permute-start(bf16[69,128]{1,0:T(8,128)(2,1)} %bitcast.2), channel_id=1, source_target_pairs={{0,96},{32,0},{64,32},{96,64},{1,97},{33,1},{65,33},{97,65},{2,98}... | collective-permute-start | bytes 53000 | tf_op jit(solution)/shard_map/ppermute | solution.py:49
  23.0 67.4 %collective-permute-start.21 = (bf16[128,1024]{1,0:T(8,128)(2,1)}, bf16[128,1024]{1,0:T(8,128)(2,1)}, u32[]{:S(2)}, u32[]{:S(2)}) collective-permute-start(bf16[128,1024]{1,0:T(8,128)(2,1)} %get-tuple-element.423), channel_id=1, source_target_pairs={{0,96},{32,0},{64,32},{96,64},{1,97},{33,1},{65,33},{97,65},{2,98}... | collective-permute-start | bytes 786440 | tf_op jit(solution)/shard_map/ppermute | solution.py:49
  23.0 68.2 %collective-permute-start.20 = (bf16[128,1024]{1,0:T(8,128)(2,1)}, bf16[128,1024]{1,0:T(8,128)(2,1)}, u32[]{:S(2)}, u32[]{:S(2)}) collective-permute-start(bf16[128,1024]{1,0:T(8,128)(2,1)} %get-tuple-element.423), channel_id=1, source_target_pairs={{0,64},{32,96},{64,0},{96,32},{1,65},{33,97},{65,1},{97,33},{2,66}... | collective-permute-start | bytes 786440 | tf_op jit(solution)/shard_map/ppermute | solution.py:49
  27.1 44.4 %all-to-all-start = ((bf16[16,64,1024]{2,1,0:T(8,128)(2,1)}), bf16[16,64,1024]{2,1,0:T(8,128)(2,1)S(1)}, u32[]{:S(2)}, u32[]{:S(2)}) async-start(bf16[16,64,1024]{2,1,0:T(8,128)(2,1)} %bitcast.7), calls=%async_computation | async-start | bytes 4194304 | tf_op jit(solution)/shard_map/all_to_all | solution.py:63
  53.8 39.2 %collective-permute-start.19 = (bf16[128,1024]{1,0:T(8,128)(2,1)}, bf16[128,1024]{1,0:T(8,128)(2,1)}, u32[]{:S(2)}, u32[]{:S(2)}) collective-permute-start(bf16[128,1024]{1,0:T(8,128)(2,1)} %get-tuple-element.423), channel_id=1, source_target_pairs={{0,32},{32,64},{64,96},{96,0},{1,33},{33,65},{65,97},{97,1},{2,34}... | collective-permute-start | bytes 786440 | tf_op jit(solution)/shard_map/ppermute | solution.py:49
  55.1 33.5 %collective-permute-start.4 = (bf16[256,512]{1,0:T(8,128)(2,1)}, bf16[256,512]{1,0:T(8,128)(2,1)}, u32[]{:S(2)}, u32[]{:S(2)}) collective-permute-start(bf16[256,512]{1,0:T(8,128)(2,1)} %pad_maximum_fusion.13), channel_id=1, source_target_pairs={{0,96},{32,0},{64,32},{96,64},{1,97},{33,1},{65,33},{97,65},{2,98}... | collective-permute-start | bytes 786440 | tf_op jit(solution)/shard_map/ppermute | solution.py:49
  71.5 41.8 %collective-permute-start.3 = (bf16[16,64,1024]{2,1,0:T(8,128)(2,1)S(1)}, bf16[16,64,1024]{2,1,0:T(8,128)(2,1)}, u32[]{:S(2)}, u32[]{:S(2)}) collective-permute-start(bf16[16,64,1024]{2,1,0:T(8,128)(2,1)S(1)} %all-to-all-done), channel_id=1, source_target_pairs={{0,1},{1,0},{2,3},{3,2},{4,5},{5,4},{6,7},{7,6},{8,9},{9,8},{10,11... | collective-permute-start | bytes 6291464 | tf_op jit(solution)/shard_map/ppermute | solution.py:41
  88.7 9.7 %collective-permute-start.5 = (bf16[256,512]{1,0:T(8,128)(2,1)}, bf16[256,512]{1,0:T(8,128)(2,1)S(1)}, u32[]{:S(2)}, u32[]{:S(2)}) collective-permute-start(bf16[256,512]{1,0:T(8,128)(2,1)} %pad_maximum_fusion.13), channel_id=1, source_target_pairs={{0,64},{32,96},{64,0},{96,32},{1,65},{33,97},{65,1},{97,33},{2,66}... | collective-permute-start | bytes 786440 | tf_op jit(solution)/shard_map/ppermute | solution.py:49
  90.4 14.3 %collective-permute-start.6 = (bf16[256,512]{1,0:T(8,128)(2,1)}, bf16[256,512]{1,0:T(8,128)(2,1)S(1)}, u32[]{:S(2)}, u32[]{:S(2)}) collective-permute-start(bf16[256,512]{1,0:T(8,128)(2,1)} %pad_maximum_fusion.13), channel_id=1, source_target_pairs={{0,32},{32,64},{64,96},{96,0},{1,33},{33,65},{65,97},{97,1},{2,34}... | collective-permute-start | bytes 786440 | tf_op jit(solution)/shard_map/ppermute | solution.py:49
  91.1 154.6 %collective-permute-start.12 = (bf16[256,704]{1,0:T(8,128)(2,1)}, bf16[256,704]{1,0:T(8,128)(2,1)}, u32[]{:S(2)}, u32[]{:S(2)}) collective-permute-start(bf16[256,704]{1,0:T(8,128)(2,1)} %pad_maximum_fusion.10), channel_id=1, source_target_pairs={{0,96},{32,0},{64,32},{96,64},{1,97},{33,1},{65,33},{97,65},{2,98}... | collective-permute-start | bytes 1081352 | tf_op jit(solution)/shard_map/ppermute | solution.py:49
  93.1 154.5 %collective-permute-start.13 = (bf16[256,704]{1,0:T(8,128)(2,1)}, bf16[256,704]{1,0:T(8,128)(2,1)}, u32[]{:S(2)}, u32[]{:S(2)}) collective-permute-start(bf16[256,704]{1,0:T(8,128)(2,1)} %pad_maximum_fusion.11), channel_id=1, source_target_pairs={{0,64},{32,96},{64,0},{96,32},{1,65},{33,97},{65,1},{97,33},{2,66}... | collective-permute-start | bytes 1081352 | tf_op jit(solution)/shard_map/ppermute | solution.py:49
  98.3 164.5 %collective-permute-start.14 = (bf16[256,704]{1,0:T(8,128)(2,1)}, bf16[256,704]{1,0:T(8,128)(2,1)}, u32[]{:S(2)}, u32[]{:S(2)}) collective-permute-start(bf16[256,704]{1,0:T(8,128)(2,1)} %pad_maximum_fusion.12), channel_id=1, source_target_pairs={{0,32},{32,64},{64,96},{96,0},{1,33},{33,65},{65,97},{97,1},{2,34}... | collective-permute-start | bytes 1081352 | tf_op jit(solution)/shard_map/ppermute | solution.py:49
  104.6 175.6 %collective-permute-start.22 = (bf16[512,1024]{1,0:T(8,128)(2,1)}, bf16[512,1024]{1,0:T(8,128)(2,1)}, u32[]{:S(2)}, u32[]{:S(2)}) collective-permute-start(bf16[512,1024]{1,0:T(8,128)(2,1)} %pad_maximum_fusion.7), channel_id=1, source_target_pairs={{0,1},{1,0},{2,3},{3,2},{4,5},{5,4},{6,7},{7,6},{8,9},{9,8},{10,11... | collective-permute-start | bytes 3145736 | tf_op jit(solution)/shard_map/ppermute | solution.py:41
  236.4 19.2 %all-to-all-start.1 = ((bf16[32,64,128]{2,1,0:T(8,128)(2,1)}), bf16[32,64,128]{2,1,0:T(8,128)(2,1)}, u32[]{:S(2)}, u32[]{:S(2)}) async-start(bf16[32,64,128]{2,1,0:T(8,128)(2,1)} %bitcast.433), calls=%async_computation.1 | async-start | bytes 1048576 | tf_op jit(solution)/shard_map/all_to_all | solution.py:303
  244.0 277.4 %reduce-scatter.2.cloned.1.call-start = ((), (), s32[]{:S(2)}) async-start(), calls=%async_computation.7 | async-start | bytes 5013504 | tf_op jit(solution)/shard_map/reduce_scatter | solution.py:343
  261.3 7.5 collective-permute-start.10
  261.7 8.7 %collective-permute-start.9 = (bf16[128,1024]{1,0:T(8,128)(2,1)S(1)}, bf16[128,1024]{1,0:T(8,128)(2,1)S(1)}, u32[]{:S(2)}, u32[]{:S(2)}) collective-permute-start(bf16[128,1024]{1,0:T(8,128)(2,1)S(1)} %get-tuple-element.339), channel_id=1, source_target_pairs={{0,64},{32,96},{64,0},{96,32},{1,65},{33,97},{65,1},{97,33},{2,66}... | collective-permute-start | bytes 786440 | tf_op jit(solution)/shard_map/ppermute | solution.py:49
  261.7 15.3 %collective-permute-start.8 = (bf16[128,1024]{1,0:T(8,128)(2,1)S(1)}, bf16[128,1024]{1,0:T(8,128)(2,1)S(1)}, u32[]{:S(2)}, u32[]{:S(2)}) collective-permute-start(bf16[128,1024]{1,0:T(8,128)(2,1)S(1)} %get-tuple-element.339), channel_id=1, source_target_pairs={{0,32},{32,64},{64,96},{96,0},{1,33},{33,65},{65,97},{97,1},{2,34}... | collective-permute-start | bytes 786440 | tf_op jit(solution)/shard_map/ppermute | solution.py:49
  277.1 4.6 collective-permute-start.11
  290.4 7.8 collective-permute-start.24
  291.1 14.2 %collective-permute-start.26 = (bf16[128,1024]{1,0:T(8,128)(2,1)S(1)}, bf16[128,1024]{1,0:T(8,128)(2,1)S(1)}, u32[]{:S(2)}, u32[]{:S(2)}) collective-permute-start(bf16[128,1024]{1,0:T(8,128)(2,1)S(1)} %get-tuple-element.379), channel_id=1, source_target_pairs={{0,32},{32,64},{64,96},{96,0},{1,33},{33,65},{65,97},{97,1},{2,34}... | collective-permute-start | bytes 786440 | tf_op jit(solution)/shard_map/ppermute | solution.py:49
  292.0 13.4 %collective-permute-start.25 = (bf16[128,1024]{1,0:T(8,128)(2,1)S(1)}, bf16[128,1024]{1,0:T(8,128)(2,1)S(1)}, u32[]{:S(2)}, u32[]{:S(2)}) collective-permute-start(bf16[128,1024]{1,0:T(8,128)(2,1)S(1)} %get-tuple-element.380), channel_id=1, source_target_pairs={{0,64},{32,96},{64,0},{96,32},{1,65},{33,97},{65,1},{97,33},{2,66}... | collective-permute-start | bytes 786440 | tf_op jit(solution)/shard_map/ppermute | solution.py:49
  293.0 16.5 %collective-permute-start.16 = (bf16[128,1024]{1,0:T(8,128)(2,1)S(1)}, bf16[128,1024]{1,0:T(8,128)(2,1)S(1)}, u32[]{:S(2)}, u32[]{:S(2)}) collective-permute-start(bf16[128,1024]{1,0:T(8,128)(2,1)S(1)} %get-tuple-element.381), channel_id=1, source_target_pairs={{0,96},{32,0},{64,32},{96,64},{1,97},{33,1},{65,33},{97,65},{2,98}... | collective-permute-start | bytes 786440 | tf_op jit(solution)/shard_map/ppermute | solution.py:49
  295.1 21.6 %collective-permute-start.18 = (bf16[128,1024]{1,0:T(8,128)(2,1)S(1)}, bf16[128,1024]{1,0:T(8,128)(2,1)S(1)}, u32[]{:S(2)}, u32[]{:S(2)}) collective-permute-start(bf16[128,1024]{1,0:T(8,128)(2,1)S(1)} %get-tuple-element.382), channel_id=1, source_target_pairs={{0,32},{32,64},{64,96},{96,0},{1,33},{33,65},{65,97},{97,1},{2,34}... | collective-permute-start | bytes 786440 | tf_op jit(solution)/shard_map/ppermute | solution.py:49
  298.3 18.4 %collective-permute-start.17 = (bf16[128,1024]{1,0:T(8,128)(2,1)S(1)}, bf16[128,1024]{1,0:T(8,128)(2,1)S(1)}, u32[]{:S(2)}, u32[]{:S(2)}) collective-permute-start(bf16[128,1024]{1,0:T(8,128)(2,1)S(1)} %get-tuple-element.383), channel_id=1, source_target_pairs={{0,64},{32,96},{64,0},{96,32},{1,65},{33,97},{65,1},{97,33},{2,66}... | collective-permute-start | bytes 786440 | tf_op jit(solution)/shard_map/ppermute | solution.py:49
  348.9 24.8 %collective-permute-start.27 = (bf16[16,64,1024]{2,1,0:T(8,128)(2,1)}, bf16[16,64,1024]{2,1,0:T(8,128)(2,1)}, u32[]{:S(2)}, u32[]{:S(2)}) collective-permute-start(bf16[16,64,1024]{2,1,0:T(8,128)(2,1)} %all_to_all.20), channel_id=1, source_target_pairs={{0,1},{1,0},{2,3},{3,2},{4,5},{5,4},{6,7},{7,6},{8,9},{9,8},{10,11... | collective-permute-start | bytes 6291464 | tf_op jit(solution)/shard_map/ppermute | solution.py:41
  373.7 269.7 %all-reduce.16.cloned.1.call-start = ((), (), s32[]{:S(2)}) async-start(), calls=%async_computation.10 | async-start | bytes 262144 | tf_op jit(solution)/shard_map/psum | solution.py:440
  384.8 89.2 %collective-permute-start.35 = (bf16[64,1024]{1,0:T(8,128)(2,1)}, bf16[64,1024]{1,0:T(8,128)(2,1)}, u32[]{:S(2)}, u32[]{:S(2)}) collective-permute-start(bf16[64,1024]{1,0:T(8,128)(2,1)} %fusion.107), channel_id=1, source_target_pairs={{0,16},{1,17},{2,18},{3,19},{4,20},{5,21},{6,22},{7,23},{8,24},{9,... | collective-permute-start | bytes 393224 | tf_op jit(solution)/shard_map/ppermute | solution.py:45
  475.0 4.0 collective-permute-start.36
  475.1 4.0 collective-permute-start.38
  477.7 4.3 collective-permute-start.37
  478.6 199.9 %all-gather.11.cloned.1.call-start = ((), (), s32[]{:S(2)}) async-start(), calls=%async_computation.8 | async-start | bytes 1081344 | tf_op jit(solution)/shard_map/all_gather | solution.py:428
  482.0 6.4 collective-permute-start.39
  489.1 236.7 %all-gather.9.cloned.1.call-start = ((), (), s32[]{:S(2)}) async-start(), calls=%async_computation.6 | async-start | bytes 3244032 | tf_op jit(solution)/shard_map/all_gather | solution.py:403
  494.0 8.8 %collective-permute-start.30 = (bf16[256,512]{1,0:T(8,128)(2,1)S(1)}, bf16[256,512]{1,0:T(8,128)(2,1)S(1)}, u32[]{:S(2)}, u32[]{:S(2)}) collective-permute-start(bf16[256,512]{1,0:T(8,128)(2,1)S(1)} %get-tuple-element.373), channel_id=1, source_target_pairs={{0,32},{32,64},{64,96},{96,0},{1,33},{33,65},{65,97},{97,1},{2,34}... | collective-permute-start | bytes 786440 | tf_op jit(solution)/shard_map/ppermute | solution.py:49
  496.8 6.3 collective-permute-start.32
  498.8 10.2 %collective-permute-start.31 = (bf16[256,512]{1,0:T(8,128)(2,1)S(1)}, bf16[256,512]{1,0:T(8,128)(2,1)S(1)}, u32[]{:S(2)}, u32[]{:S(2)}) collective-permute-start(bf16[256,512]{1,0:T(8,128)(2,1)S(1)} %get-tuple-element.375), channel_id=1, source_target_pairs={{0,64},{32,96},{64,0},{96,32},{1,65},{33,97},{65,1},{97,33},{2,66}... | collective-permute-start | bytes 786440 | tf_op jit(solution)/shard_map/ppermute | solution.py:49
  509.2 5.4 collective-permute-start.33
  514.6 6.0 collective-permute-start.34
  521.3 253.1 %all-gather.13.cloned.1.call-start = ((), (), s32[]{:S(2)}) async-start(), calls=%async_computation.9 | async-start | bytes 4866048 | tf_op jit(solution)/shard_map/all_gather | solution.py:351
  522.4 7.7 collective-permute-start.40
  528.9 4.4 collective-permute-start.42
  529.0 4.3 collective-permute-start.41
  540.2 5.7 collective-permute-start.29
  548.6 132.9 %all-to-all-start.3 = ((bf16[16,64,1024]{2,1,0:T(8,128)(2,1)}), bf16[16,64,1024]{2,1,0:T(8,128)(2,1)S(1)}, u32[]{:S(2)}, u32[]{:S(2)}) async-start(bf16[16,64,1024]{2,1,0:T(8,128)(2,1)} %fusion.18), calls=%async_computation.3 | async-start | bytes 4194304 | tf_op jit(solution)/shard_map/all_to_all | solution.py:63
  (163 other events, 1288.6 us)
Sparse Core Ops, SparseCore 0:
  25.6 55.4 all-gather.6
  373.8 73.5 reduce-scatter.1
  478.7 155.9 all-reduce.15
  637.7 40.8 all-gather.10
  681.5 44.2 all-gather.8
  728.1 46.2 all-gather.12

commit v2 on v1

v2 whole, which is shorter than its diff:
```python
import jax
import jax.numpy as jnp
from jax import lax
from jax.experimental import pallas as pl
from jax.experimental.pallas import tpu as pltpu
from jax.sharding import PartitionSpec as P

f32 = jnp.float32
bf16 = jnp.bfloat16
epsilon = 1e-06
CONV = 4
CHUNK = 128
GROUP = 4
ROWS = CHUNK * GROUP

FF = 2816

CHIPS = [[chip * 2 + core for chip in range(16)] for core in range(2)]
OTHER_CORE = [(place, place ^ 1) for place in range(32)]
OTHER_SEQ = [(place, place ^ 16) for place in range(32)]
OUTPUT_MOVES = [
    (at * 32 + s * 16 + h * 2 + v, (h // 2) * 32 + s * 16 + ((h % 2) * 4 + at) * 2 + v)
    for at in range(4)
    for s in range(2)
    for h in range(8)
    for v in range(2)
]

NN = ((1,), (0,))
NT = ((1,), (1,))
TN = ((0,), (0,))


def raw(left, right, dims):
    return lax.dot_general(left, right, (dims, ((), ())), preferred_element_type=f32)


def split(value):
    high = value.astype(bf16)
    return high, (value - high.astype(f32)).astype(bf16)


def split3(value):
    high = value.astype(bf16)
    rest = value - high.astype(f32)
    mid = rest.astype(bf16)
    return high, mid, (rest - mid.astype(f32)).astype(bf16)


def dot3(left, right, dims):
    lefts = jnp.concatenate([left[0], left[0], left[1]], axis=dims[0][0])
    rights = jnp.concatenate([right[0], right[1], right[0]], axis=dims[1][0])
    return raw(lefts, rights, dims)


def stacked(*pairs, axis=0):
    return tuple(jnp.concatenate([pair[part] for pair in pairs], axis=axis) for part in (0, 1))


def square_iota():
    rows = lax.broadcasted_iota(jnp.int32, (CHUNK, CHUNK), 0)
    cols = lax.broadcasted_iota(jnp.int32, (CHUNK, CHUNK), 1)
    return rows, cols


def inverses(lowers, rows, cols):
    results = [
        jnp.where(rows == cols, 1.0, 0.0) - jnp.where((rows >> 1) == (cols >> 1), lower, 0.0) for lower in lowers
    ]
    level = 1
    while (1 << level) < CHUNK:
        mask = ((rows >> (level + 1)) == (cols >> (level + 1))) & ((rows >> level) != (cols >> level))
        held = [split(result) for result in results]
        parts = [split(jnp.where(mask, lower, 0.0)) for lower in lowers]
        inner = [split(dot3(part, pair, NN)) for part, pair in zip(parts, held)]
        results = [result - dot3(pair, part, NN) for result, pair, part in zip(results, held, inner)]
        level += 1
    return results


def silu(value):
    return value * jax.nn.sigmoid(value)


def softplus(value):
    return jnp.maximum(value, 0.0) + jnp.log1p(jnp.exp(-jnp.abs(value)))


def decay_matrix(total, rows, cols):
    across = total.T[2:3, :]
    return jnp.where(cols <= rows, jnp.exp(jnp.minimum(total[:, 2:3] - across, 0.0)), 0.0)


def unit_norms(active):
    q, k = active[:, :128], active[:, 128:256]
    rq = lax.rsqrt(jnp.sum(q * q, axis=-1, keepdims=True) + epsilon)
    rk = lax.rsqrt(jnp.sum(k * k, axis=-1, keepdims=True) + epsilon)
    return q, k, rq, rk


def forward_kernel(
    numbers, mine, theirs, gain, weight, taps,
    hidden_out, mixed_out, gate_out, conv_out, cols_out, inv_out, from_out, upd_out, score_out, move_out, state_out,
    heads_out, square_out,
    state, ext,
):
    step = pl.program_id(0)
    core, bias, scale = numbers[0], numbers[1], numbers[2]

    @pl.when(step == 0)
    def _():
        state[...] = jnp.zeros_like(state)
        ext[0:8, :] = jnp.zeros((8, 384), f32)

    first = core < 0.5
    for at in range(GROUP):
        one, two = mine[at], theirs[at]
        x = jnp.concatenate([jnp.where(first, one, two), jnp.where(first, two, one)], axis=0).astype(f32)
        rate = lax.rsqrt(jnp.mean(x * x, axis=-1, keepdims=True) + epsilon)
        hidden_out[at * CHUNK : (at + 1) * CHUNK, :] = (x * rate * gain[...]).astype(bf16)
    projected = raw(hidden_out[...], weight[...], NN)
    mixed = projected[:, :384].astype(bf16)
    mixed_out[...] = mixed
    gate_out[...] = projected[:, 384:512]
    rates = projected[:, 512:]
    ext[8 : 8 + ROWS, :] = mixed.astype(f32)
    conv = taps[0:1, :] * ext[5 : 5 + ROWS, :]
    for lag in range(1, CONV):
        conv = conv + taps[lag : lag + 1, :] * ext[5 + lag : 5 + lag + ROWS, :]
    ext[0:8, :] = ext[ROWS : ROWS + 8, :]
    conv_out[...] = conv
    lanes = lax.broadcasted_iota(jnp.int32, (ROWS, 128), 1)
    sums_in = jnp.broadcast_to(rates[:, 1:2], (ROWS, 128)) + bias
    glog = -scale * softplus(sums_in)
    cols_all = jnp.where(lanes == 0, jax.nn.sigmoid(rates), jnp.where(lanes == 3, jax.nn.sigmoid(sums_in), glog))
    rows, cols = square_iota()
    tri = jnp.where(cols <= rows, 1.0, 0.0).astype(bf16)
    tri3 = jnp.concatenate([tri, tri, tri], axis=1)
    lane = lax.broadcasted_iota(jnp.int32, (CHUNK, CHUNK), 1)
    lowers, kept = [], []
    for at in range(GROUP):
        here = slice(at * CHUNK, (at + 1) * CHUNK)
        q, k, rq, rk = unit_norms(silu(conv[here, :256]))
        queries, keys = q * (rq * 128**-0.5), k * rk
        values = silu(conv[here, 256:])
        column = cols_all[here]
        running = raw(tri3, jnp.concatenate(split3(column), axis=0), NN)
        column = jnp.where(lane == 2, running, column)
        cols_out[here, :] = column
        decay = decay_matrix(column, rows, cols)
        beta = column[:, 0:1]
        total = column[:, 2:3]
        growth = jnp.exp(total)
        last = total[CHUNK - 1 : CHUNK, :]
        keys_s = split(keys)
        queries_s = split(queries)
        products = dot3(stacked(keys_s, queries_s), keys_s, NT)
        lowers.append(jnp.where(cols < rows, decay, 0.0) * products[:CHUNK] * beta)
        scores = products[CHUNK:] * decay
        score_out[here, :] = scores
        right = split(jnp.concatenate([(beta * growth) * keys, beta * values], axis=1))
        ends = split(jnp.exp(last - total) * keys)
        kept.append((split(scores), right, ends, split(growth * queries), jnp.exp(last)))
    found = inverses(lowers, rows, cols)
    both = []
    for at in range(GROUP):
        here = slice(at * CHUNK, (at + 1) * CHUNK)
        inv_out[here, :] = found[at]
        both.append(dot3(split(found[at]), kept[at][1], NN))
    maps = []
    for at in range(GROUP):
        here = slice(at * CHUNK, (at + 1) * CHUNK)
        from_out[here, :] = both[at][:, :128]
        ended = dot3(kept[at][2], split(both[at]), TN)
        move = jnp.where(rows == cols, kept[at][4], 0.0) - ended[:, :128]
        move_out[here, :] = move
        maps.append((split(move), ended[:, 128:]))
    current = state[...]
    states = []
    for at in range(GROUP):
        here = slice(at * CHUNK, (at + 1) * CHUNK)
        state_out[here, :] = current
        pair = split(current)
        states.append(pair)
        current = dot3(maps[at][0], pair, NN) + maps[at][1]
    state[...] = current
    ones = jnp.ones((8, 256), bf16)
    for at in range(GROUP):
        here = slice(at * CHUNK, (at + 1) * CHUNK)
        product = dot3(stacked(split(both[at][:, :128]), kept[at][3]), states[at], NN)
        updates = both[at][:, 128:] - product[:CHUNK]
        upd_out[here, :] = updates
        heads = product[CHUNK:] + dot3(kept[at][0], split(updates), NN)
        heads_out[here, :] = heads
        squares = raw(ones, jnp.concatenate(split(heads * heads), axis=1), NT)
        square_out[0, at : at + 1, :] = squares[0:1, :]


def forward_call(numbers, mine, theirs, gain, weight, taps):
    steps = 16 // GROUP
    shape = jax.ShapeDtypeStruct
    blocks = lambda width: pl.BlockSpec((ROWS, width), lambda i: (i, 0))
    whole = lambda *dims: pl.BlockSpec(dims, lambda i: (0,) * len(dims))
    square = shape((2048, 128), f32)
    return pl.pallas_call(
        forward_kernel,
        grid=(steps,),
        in_specs=[
            pl.BlockSpec(memory_space=pltpu.SMEM),
            pl.BlockSpec((GROUP, 64, 1024), lambda i: (i, 0, 0)),
            pl.BlockSpec((GROUP, 64, 1024), lambda i: (i, 0, 0)),
            whole(1, 1024),
            whole(1024, 640),
            whole(4, 384),
        ],
        out_specs=[blocks(1024), blocks(384), blocks(128), blocks(384)]
        + [blocks(128)] * 8
        + [pl.BlockSpec((1, GROUP, 128), lambda i: (i, 0, 0))],
        out_shape=[
            shape((2048, 1024), bf16),
            shape((2048, 384), bf16),
            square,
            shape((2048, 384), f32),
        ]
        + [square] * 8
        + [shape((steps, GROUP, 128), f32)],
        scratch_shapes=[pltpu.VMEM((128, 128), f32), pltpu.VMEM((ROWS + 8, 384), f32)],
        compiler_params=pltpu.CompilerParams(
            dimension_semantics=("arbitrary",), vmem_limit_bytes=52 * 1024 * 1024
        ),
        cost_estimate=cost(30),
        name="delta_forward",
    )(numbers, mine, theirs, gain, weight, taps)


def backward_kernel(
    numbers, taps, conv_in, cols_in, inv_in, from_in, upd_in, score_in, move_in, state_in, mixed_in,
    normed_in, heads_in, sq_mine, sq_theirs, in_mine, in_theirs, hidden_in, gate_in, weight,
    keep_out, give_out, unit_out, logits_out, taps_out, sums_out,
    after, ext, d_all,
):
    step = pl.program_id(0)
    scale = numbers[2]

    @pl.when(step == 0)
    def _():
        after[...] = jnp.zeros_like(after)
        ext[ROWS : ROWS + 8, :] = jnp.zeros((8, 384), f32)
        taps_out[...] = jnp.zeros_like(taps_out)
        sums_out[...] = jnp.zeros_like(sums_out)
        unit_out[...] = jnp.zeros_like(unit_out)
        logits_out[...] = jnp.zeros_like(logits_out)

    rows, cols = square_iota()
    strict = cols < rows
    kept, maps = [], []
    for at in range(GROUP):
        here = slice(at * CHUNK, (at + 1) * CHUNK)
        q, k, rq, rk = unit_norms(silu(conv_in[here, :256]))
        queries, keys = q * (rq * 128**-0.5), k * rk
        column = cols_in[here, :]
        total = column[:, 2:3]
        growth = jnp.exp(total)
        last = total[CHUNK - 1 : CHUNK, :]
        rate = head_rates(sq_mine, sq_theirs, at)
        mean = row_to_square((in_mine[0, at : at + 1, :] + in_theirs[0, at : at + 1, :]) / 256.0)
        grads = split(rate * (normed_in[here, :] - heads_in[here, :] * (rate * rate * mean)))
        passed = dot3(split(score_in[here, :]), grads, TN)
        probe = stacked(split(growth * queries), split(-from_in[here, :]))
        added = dot3(probe, stacked(grads, split(passed)), TN)
        maps.append((split(move_in[here, :]), added))
        kept.append((queries, keys, rq, rk, grads, passed, column, growth, last))
    current = after[...]
    afters = [None] * GROUP
    for at in reversed(range(GROUP)):
        pair = split(current)
        afters[at] = (current, pair)
        current = dot3(maps[at][0], pair, TN) + maps[at][1]
    after[...] = current
    tri = jnp.where(cols >= rows, 1.0, 0.0).astype(bf16)
    tri3 = jnp.concatenate([tri, tri, tri], axis=1)
    scale_sum = jnp.zeros((CHUNK, CHUNK), f32)
    bias_sum = jnp.zeros((CHUNK, CHUNK), f32)
    for at in range(GROUP):
        here = slice(at * CHUNK, (at + 1) * CHUNK)
        queries, keys, rq, rk, grads, passed, column, growth, last = kept[at]
        beta = column[:, 0:1]
        total = column[:, 2:3]
        decay = decay_matrix(column, rows, cols)
        to_end = jnp.exp(last - total)
        keys_s = split(keys)
        state = state_in[here, :]
        state_s = split(state)
        later, later_s = afters[at]
        updates = split(upd_in[here, :])
        d_updates = passed + dot3(split(to_end * keys), later_s, NN)
        right = dot3(split(inv_in[here, :]), split(d_updates), TN)
        right_s = split(right)
        pair = stacked(grads, right_s)
        inner = dot3(pair, updates, NT)
        d_scores = split(inner[:CHUNK] * decay)
        d_lower = split(jnp.where(strict, -inner[CHUNK:] * decay, 0.0))
        through = dot3(pair, state_s, NT)
        k_end = to_end * dot3(updates, later_s, NT)
        d_pair = stacked(d_scores, d_lower)
        on_keys = dot3(d_pair, keys_s, NN)
        k_cols = dot3(d_pair, stacked(split(queries), split(beta * keys)), TN) + k_end
        d_queries = growth * through[:CHUNK] + on_keys[:CHUNK]
        k_rows = on_keys[CHUNK:] - growth * through[CHUNK:]
        k_beta = beta * k_rows
        d_keys = k_beta + k_cols
        values_conv = conv_in[here, 256:]
        values = silu(values_conv)
        d_beta = jnp.sum(keys * k_rows + right * values, axis=-1, keepdims=True)
        d_total = jnp.sum(queries * d_queries + keys * (k_beta - k_cols), axis=-1, keepdims=True)
        ends = jnp.sum(keys * k_end, axis=0, keepdims=True)
        ends = ends + jnp.exp(last) * jnp.sum(state * later, axis=0, keepdims=True)
        d_last = jnp.sum(ends, axis=1, keepdims=True)
        spread = jnp.broadcast_to(d_total, (CHUNK, CHUNK))
        d_glog = raw(tri3, jnp.concatenate(split3(spread), axis=0), NN) + d_last
        d_decay = -scale * d_glog * column[:, 3:4]
        scale_sum = scale_sum + d_glog * column
        bias_sum = bias_sum + d_decay
        d_all[here, 512:] = jnp.where(
            cols == 0, d_beta * beta * (1.0 - beta), jnp.where(cols == 1, d_decay, 0.0)
        ).astype(bf16)
        q_hat, k_hat = queries * 128**0.5, keys
        d_q = (rq * 128**-0.5) * (d_queries - q_hat * jnp.sum(q_hat * d_queries, axis=-1, keepdims=True))
        d_k = rk * (d_keys - k_hat * jnp.sum(k_hat * d_keys, axis=-1, keepdims=True))
        d_v = beta * right
        conv = conv_in[here, :]
        sig = jax.nn.sigmoid(conv)
        ext[here, :] = jnp.concatenate([d_q, d_k, d_v], axis=1) * (sig * (1.0 + conv * (1.0 - sig)))
    sums_out[0:1, :] += jnp.sum(scale_sum, axis=0, keepdims=True)
    sums_out[1:2, :] += jnp.sum(bias_sum, axis=0, keepdims=True)
    mixed = mixed_in[...].astype(f32)
    d_mixed = jnp.zeros((ROWS, 384), f32)
    for lag in range(CONV):
        moved = ext[CONV - 1 - lag : CONV - 1 - lag + ROWS, :]
        d_mixed = d_mixed + taps[lag : lag + 1, :] * moved
        taps_out[lag : lag + 1, :] += jnp.sum(mixed * moved, axis=0, keepdims=True)
    d_all[:, :384] = d_mixed.astype(bf16)
    d_all[:, 384:512] = gate_in[...]
    ext[ROWS : ROWS + 8, :] = ext[0:8, :]
    hidden = hidden_in[...]
    unit_out[...] += raw(hidden, d_all[:, :384], TN)
    logits_out[...] += raw(d_all[:, 512:], hidden, TN)[:8]
    first = numbers[0] < 0.5
    for at in range(GROUP):
        product = raw(d_all[at * CHUNK : (at + 1) * CHUNK, :], weight[...], NT)
        low, high = product[:64], product[64:]
        keep_out[at] = jnp.where(first, low, high)
        give_out[at] = jnp.where(first, high, low).astype(bf16)


def backward_call(numbers, taps, *arrays):
    steps = 16 // GROUP
    shape = jax.ShapeDtypeStruct
    blocks = lambda width: pl.BlockSpec((ROWS, width), lambda i: (steps - 1 - i, 0))
    halves = pl.BlockSpec((GROUP, 64, 1024), lambda i: (steps - 1 - i, 0, 0))
    lines = pl.BlockSpec((1, GROUP, 128), lambda i: (steps - 1 - i, 0, 0))
    whole = lambda *dims: pl.BlockSpec(dims, lambda i: (0,) * len(dims))
    return pl.pallas_call(
        backward_kernel,
        grid=(steps,),
        in_specs=[pl.BlockSpec(memory_space=pltpu.SMEM), whole(4, 384), blocks(384)]
        + [blocks(128)] * 7
        + [blocks(384), blocks(128), blocks(128)]
        + [lines] * 4
        + [blocks(1024), blocks(128), whole(1024, 640)],
        out_specs=[halves, halves, whole(1024, 384), whole(8, 1024), whole(8, 384), whole(8, 128)],
        out_shape=[
            shape((16, 64, 1024), f32),
            shape((16, 64, 1024), bf16),
            shape((1024, 384), f32),
            shape((8, 1024), f32),
            shape((8, 384), f32),
            shape((8, 128), f32),
        ],
        scratch_shapes=[
            pltpu.VMEM((128, 128), f32),
            pltpu.VMEM((ROWS + 8, 384), f32),
            pltpu.VMEM((ROWS, 640), bf16),
        ],
        compiler_params=pltpu.CompilerParams(
            dimension_semantics=("arbitrary",), vmem_limit_bytes=52 * 1024 * 1024
        ),
        cost_estimate=cost(36),
        name="delta_backward",
    )(numbers, taps, *arrays)


def row_to_square(row):
    return jnp.broadcast_to(row, (CHUNK, CHUNK)).T


def head_rates(mine, theirs, at):
    squares = mine[0, at : at + 1, :] + theirs[0, at : at + 1, :]
    return row_to_square(lax.rsqrt(squares / 256.0 + epsilon))


def gate_kernel(heads, gate, mine, theirs, gain, out):
    for at in range(GROUP):
        here = slice(at * CHUNK, (at + 1) * CHUNK)
        normed = heads[here, :] * head_rates(mine, theirs, at)
        out[here, :] = (normed * gain[...] * silu(gate[here, :])).astype(bf16)


def specs(*widths):
    found = []
    for width in widths:
        if width == "rows":
            found.append(pl.BlockSpec((1, GROUP, 128), lambda i: (i, 0, 0)))
        elif width == "tokens":
            found.append(pl.BlockSpec((GROUP, 64, 1024), lambda i: (i, 0, 0)))
        elif width == "smem":
            found.append(pl.BlockSpec(memory_space=pltpu.SMEM))
        elif isinstance(width, tuple):
            found.append(pl.BlockSpec(width, lambda i, dims=len(width): (0,) * dims))
        else:
            found.append(pl.BlockSpec((ROWS, width), lambda i: (i, 0)))
    return found


def cost(microseconds):
    return pl.CostEstimate(flops=microseconds * 10**9, bytes_accessed=microseconds * 3 * 10**6, transcendentals=0)


def params():
    return pltpu.CompilerParams(dimension_semantics=("arbitrary",), vmem_limit_bytes=52 * 1024 * 1024)


def gate_call(heads, gate, mine, theirs, gain):
    return pl.pallas_call(
        gate_kernel,
        grid=(16 // GROUP,),
        in_specs=specs(128, 128, "rows", "rows", (1, 128)),
        out_specs=specs(128)[0],
        out_shape=jax.ShapeDtypeStruct((2048, 128), bf16),
        compiler_params=params(),
        cost_estimate=cost(3),
        name="gate",
    )(heads, gate, mine, theirs, gain)


def middle_kernel(numbers, gated, tokens, mine, theirs, gain, middle_out, hidden_out):
    core = numbers[0]
    for at in range(2):
        line = tokens[at].astype(f32)
        for weight, parity in ((mine, core), (theirs, 1 - core)):
            found = [gated[at * 16 + grp * 4 + parity * 2 + half] for grp in range(4) for half in range(2)]
            line = line + raw(jnp.concatenate(found, axis=1), weight[...], NN)
        rows = slice(at * 64, at * 64 + 64)
        middle_out[rows, :] = line
        rate = lax.rsqrt(jnp.mean(line * line, axis=-1, keepdims=True) + epsilon)
        hidden_out[rows, :] = (line * rate * gain[...]).astype(bf16)


def middle_call(places, gated, tokens, mine, theirs, gain):
    shape = jax.ShapeDtypeStruct
    return pl.pallas_call(
        middle_kernel,
        in_specs=[pl.BlockSpec(memory_space=pltpu.SMEM)] + [pl.BlockSpec(memory_space=pltpu.VMEM)] * 5,
        out_shape=[shape((128, 1024), f32), shape((128, 1024), bf16)],
        compiler_params=pltpu.CompilerParams(vmem_limit_bytes=52 * 1024 * 1024),
        cost_estimate=cost(4),
        name="middle",
    )(places, gated, tokens, mine, theirs, gain)


def gate_back_kernel(
    numbers, mine, theirs, weight, heads, gate, sq_mine, sq_theirs, gain, gated, hidden,
    normed_out, gate_out, inner_out, early_out, head_out,
    output_sum, gate_sum,
):
    @pl.when(pl.program_id(0) == 0)
    def _():
        output_sum[...] = jnp.zeros_like(output_sum)
        gate_sum[...] = jnp.zeros_like(gate_sum)
        head_out[...] = jnp.zeros_like(head_out)

    first = numbers[0] < 0.5
    ones = jnp.ones((8, 256), bf16)
    for at in range(GROUP):
        here = slice(at * CHUNK, (at + 1) * CHUNK)
        one, two = mine[at], theirs[at]
        grads = jnp.concatenate([jnp.where(first, one, two), jnp.where(first, two, one)], axis=0)
        d_gated = raw(grads, weight[...], NT)
        output_sum[...] += raw(gated[here, :], grads, TN)
        value = heads[here, :]
        normed = value * head_rates(sq_mine, sq_theirs, at)
        logits = gate[here, :]
        sig = jax.nn.sigmoid(logits)
        active = logits * sig
        head_out[0:1, :] += jnp.sum(d_gated * normed * active, axis=0, keepdims=True)
        gained = d_gated * gain[...]
        gate_out[here, :] = (gained * normed * (sig * (1.0 + logits * (1.0 - sig)))).astype(bf16)
        d_normed = gained * active
        normed_out[here, :] = d_normed
        product = raw(ones, jnp.concatenate(split(d_normed * value), axis=1), NT)
        inner_out[0, at : at + 1, :] = product[0:1, :]
    gate_sum[...] += raw(hidden[...], gate_out[...], TN)

    @pl.when(pl.program_id(0) == 16 // GROUP - 1)
    def _():
        for grp in range(4):
            early_out[grp, :256, :] = gate_sum[grp * 256 : grp * 256 + 256, :]
            for part in range(8):
                block = output_sum[grp * 32 : grp * 32 + 32, part * 128 : part * 128 + 128]
                early_out[grp, 256 + part * 32 : 288 + part * 32, :] = block


def gate_back_call(numbers, mine, theirs, weight, *arrays):
    shape = jax.ShapeDtypeStruct
    return pl.pallas_call(
        gate_back_kernel,
        grid=(16 // GROUP,),
        in_specs=specs(
            "smem", "tokens", "tokens", (128, 1024), 128, 128, "rows", "rows", (1, 128), 128, 1024
        ),
        out_specs=specs(128, 128, "rows", (4, 512, 128), (8, 128)),
        out_shape=[
            shape((2048, 128), f32),
            shape((2048, 128), bf16),
            shape((16 // GROUP, GROUP, 128), f32),
            shape((4, 512, 128), f32),
            shape((8, 128), f32),
        ],
        scratch_shapes=[pltpu.VMEM((128, 1024), f32), pltpu.VMEM((1024, 128), f32)],
        compiler_params=params(),
        cost_estimate=cost(9),
        name="gate_back",
    )(numbers, mine, theirs, weight, *arrays)


def ff_weights_kernel(two, grads, swi, dy, out):
    grp = pl.program_id(0)
    found = raw(two[...], grads[...], TN).astype(bf16)
    for chip in range(16):
        for part in range(6):
            at = pl.multiple_of(grp * 96 + part * 16, 16)
            block = found[chip * 16 : chip * 16 + 16, part * 128 : part * 128 + 128]
            out[chip, pl.ds(at, 16), :] = block
    found = raw(swi[...], dy[...], TN).astype(bf16)
    for chip in range(16):
        for part in range(2):
            at = pl.multiple_of(384 + grp * 64 + part * 32, 32)
            if chip < 11:
                block = found[chip * 32 : chip * 32 + 32, part * 128 : part * 128 + 128]
            else:
                block = jnp.zeros((32, 128), bf16)
            out[chip, pl.ds(at, 32), :] = block


def ff_weights_call(two, grads, swi, dy):
    return pl.pallas_call(
        ff_weights_kernel,
        grid=(4,),
        in_specs=[
            pl.BlockSpec((1024, 256), lambda i: (0, i)),
            pl.BlockSpec((1024, 768), lambda i: (0, 0)),
            pl.BlockSpec((1024, 384), lambda i: (0, 0)),
            pl.BlockSpec((1024, 256), lambda i: (0, i)),
        ],
        out_specs=pl.BlockSpec((16, 640, 128), lambda i: (0, 0, 0)),
        out_shape=jax.ShapeDtypeStruct((16, 640, 128), bf16),
        compiler_params=params(),
        cost_estimate=cost(7),
        name="ff_weights",
    )(two, grads, swi, dy)


def ff_grads_kernel(numbers, mine, theirs, weight, gain, gateup_out, down_out, gain_out):
    step = pl.program_id(0)
    first = numbers[0] < 0.5

    def piece(core, chip, at, size):
        one, two = mine[chip, at : at + size, :], theirs[chip, at : at + size, :]
        return (jnp.where(first, one, two) if core == 0 else jnp.where(first, two, one)).astype(f32)

    for chip in range(4):
        rows = slice(chip * 16, chip * 16 + 16)
        total = jnp.zeros((16, 128), f32)
        for half in range(2):
            found = []
            for grp in range(4):
                for core in range(2):
                    at = (grp * 6 + half * 3) * 16
                    for part in range(3):
                        block = piece(core, chip, at + part * 16, 16)
                        found.append(block if part < 2 else block[:, :96])
            line = jnp.concatenate(found, axis=1)
            gateup_out[rows, half * FF : (half + 1) * FF] = line
            product = line * weight[rows, half * FF : (half + 1) * FF].astype(f32)
            for part in range(FF // 128):
                total = total + product[:, part * 128 : part * 128 + 128]
        total = jnp.sum(total, axis=1, keepdims=True)
        gain_out[rows, :] = jnp.broadcast_to(total, (16, 128)) / gain[rows, :].astype(f32)

        @pl.when(step * 4 + chip < 11)
        def _():
            for core in range(2):
                at = pl.multiple_of(core * 352 + (step * 4 + chip) * 32, 8)
                for part in range(8):
                    down_out[pl.ds(at, 32), part * 128 : part * 128 + 128] = piece(core, chip, 384 + part * 32, 32)


def ff_grads_call(numbers, mine, theirs, weight, gain):
    shape = jax.ShapeDtypeStruct
    return pl.pallas_call(
        ff_grads_kernel,
        grid=(4,),
        in_specs=[
            pl.BlockSpec(memory_space=pltpu.SMEM),
            pl.BlockSpec((4, 640, 128), lambda i: (i, 0, 0)),
            pl.BlockSpec((4, 640, 128), lambda i: (i, 0, 0)),
            pl.BlockSpec((64, 2 * FF), lambda i: (i, 0)),
            pl.BlockSpec((64, 128), lambda i: (i, 0)),
        ],
        out_specs=[
            pl.BlockSpec((64, 2 * FF), lambda i: (i, 0)),
            pl.BlockSpec((704, 1024), lambda i: (0, 0)),
            pl.BlockSpec((64, 128), lambda i: (i, 0)),
        ],
        out_shape=[shape((256, 2 * FF), f32), shape((704, 1024), f32), shape((256, 128), f32)],
        compiler_params=params(),
        cost_estimate=cost(8),
        name="ff_grads",
    )(numbers, mine, theirs, weight, gain)


def out_grads_kernel(numbers, mine, theirs, weight, gate_out, output_out, sum_out):
    first = numbers[0] < 0.5
    for chip in range(16):
        seq, head = chip // 8, chip % 8
        one, two = mine[chip], theirs[chip]
        for core in range(2):
            piece = (jnp.where(first, one, two) if core == 0 else jnp.where(first, two, one)).astype(f32)
            to = head * 256 + core * 128
            gate_out[seq * 128 : seq * 128 + 128, to : to + 128] = piece[:128]
            at = head // 4 * 256 + core * 128 + head % 4 * 32 + seq * 16
            for part in range(8):
                block = piece[128 + part * 16 : 144 + part * 16]
                output_out[at : at + 16, part * 128 : part * 128 + 128] = block
    for rows in (slice(0, 128), slice(128, 256)):
        total = jnp.sum(gate_out[rows, :] * weight[rows, :].astype(f32), axis=1, keepdims=True)
        sum_out[rows, :] = jnp.broadcast_to(total, (128, 128))


def out_grads_call(numbers, mine, theirs, weight):
    shape = jax.ShapeDtypeStruct
    return pl.pallas_call(
        out_grads_kernel,
        grid=(1,),
        in_specs=[
            pl.BlockSpec(memory_space=pltpu.SMEM),
            pl.BlockSpec((16, 256, 128), lambda i: (0, 0, 0)),
            pl.BlockSpec((16, 256, 128), lambda i: (0, 0, 0)),
            pl.BlockSpec((256, 2048), lambda i: (0, 0)),
        ],
        out_specs=[
            pl.BlockSpec((256, 2048), lambda i: (0, 0)),
            pl.BlockSpec((512, 1024), lambda i: (0, 0)),
            pl.BlockSpec((256, 128), lambda i: (0, 0)),
        ],
        out_shape=[shape((256, 2048), f32), shape((512, 1024), f32), shape((256, 128), f32)],
        compiler_params=params(),
        cost_estimate=cost(4),
        name="out_grads",
    )(numbers, mine, theirs, weight)


def mixer_grads_kernel(numbers, mine, theirs, weight, mixer_out, sum_out):
    first = numbers[0] < 0.5
    for head in range(8):
        one, two = mine[head], theirs[head]
        for core in range(2):
            piece = jnp.where(first, one, two) if core == 0 else jnp.where(first, two, one)
            piece = piece.astype(f32)
            rows = slice(core * 64, core * 64 + 64)
            mixer_out[rows, head * 128 : head * 128 + 128] = piece[:64]
            mixer_out[rows, 1024 + head * 128 : 1152 + head * 128] = piece[64:128]
            to = 2048 + head * 256 + core * 128
            mixer_out[:, to : to + 128] = piece[128:256]
    total = jnp.sum(mixer_out[...] * weight[...].astype(f32), axis=1, keepdims=True)
    sum_out[...] = jnp.broadcast_to(total, (128, 128))


def mixer_grads_call(numbers, mine, theirs, weight):
    shape = jax.ShapeDtypeStruct
    return pl.pallas_call(
        mixer_grads_kernel,
        grid=(2,),
        in_specs=[
            pl.BlockSpec(memory_space=pltpu.SMEM),
            pl.BlockSpec((8, 256, 128), lambda i: (i, 0, 0)),
            pl.BlockSpec((8, 256, 128), lambda i: (i, 0, 0)),
            pl.BlockSpec((128, 4096), lambda i: (i, 0)),
        ],
        out_specs=[
            pl.BlockSpec((128, 4096), lambda i: (i, 0)),
            pl.BlockSpec((128, 128), lambda i: (i, 0)),
        ],
        out_shape=[shape((256, 4096), f32), shape((256, 128), f32)],
        compiler_params=params(),
        cost_estimate=cost(4),
        name="mixer_grads",
    )(numbers, mine, theirs, weight)


def mm(left, right):
    return raw(left, right, NN)


def mm_t(left, right):
    return raw(left, right, NT)


def t_mm(left, right):
    return raw(left, right, TN)


def other_core(value):
    return lax.ppermute(value, "ctx", OTHER_CORE)


def other_seq(value):
    return lax.ppermute(value, "ctx", OTHER_SEQ)


def along_grp(value, steps):
    return lax.ppermute(value, "grp", [(at, (at + steps) % 4) for at in range(4)])


def from_grp(value):
    return [value] + [along_grp(value, steps) for steps in (1, 2, 3)]


def in_grp_order(pieces, place):
    turned = [pieces[0], pieces[3], pieces[2], pieces[1]]
    doubled = jnp.stack(turned + turned[:3])
    return lax.dynamic_slice_in_dim(doubled, (4 - place) % 4, 4, axis=0)


def exchange_grp(value, place):
    part = lambda steps: lax.dynamic_index_in_dim(value, (place + steps) % 4, 0, False)
    return [part(0)] + [along_grp(part(steps), steps) for steps in (1, 2, 3)]


def sum_grp(value, place):
    mine, *others = exchange_grp(value.astype(bf16), place)
    total = lax.dynamic_index_in_dim(value, place, 0, False)
    for other in others:
        total = total + other.astype(f32)
    return total


def after(value, *others):
    return lax.optimization_barrier((value,) + others)[0]


def over_chips(value):
    return lax.all_to_all(value, "ctx", 0, 0, axis_index_groups=CHIPS)


def to_units(tokens):
    mine = over_chips(jnp.repeat(tokens, 8, axis=0))
    return mine, other_core(mine)


def wide_columns(value, width):
    return jnp.concatenate([value[:, at * 128 : at * 128 + 128] for at in range(width // 128)], axis=0)


def body(
    block_input,
    seq_lengths,
    in_gain,
    w_mixer,
    conv_weight,
    w_rates,
    decay_scale,
    decay_bias,
    w_outgate,
    head_gain,
    w_output,
    mlp_gain,
    w_gateup,
    w_down,
    cotangent,
):
    place = lax.axis_index("ctx")
    grp = lax.axis_index("grp")
    core = place % 2
    head = (place % 16) // 2
    seq = place // 16
    unit = place % 16

    x_all = jnp.repeat(block_input, 8, axis=0)
    x_mine = over_chips(x_all)
    w_mixer_one, w_output_one, conv_one = lax.optimization_barrier((w_mixer, w_output, conv_weight, x_all))[:3]

    small = jnp.concatenate(
        [
            conv_one.reshape(-1),
            in_gain,
            mlp_gain,
            head_gain,
            decay_scale,
            decay_bias,
            jnp.zeros((60,), bf16),
        ]
    ).reshape(-1, 128)
    small = in_grp_order(from_grp(small), grp).reshape(4, -1)
    conv_full = small[:, :4096].reshape(4, 4, 1024).transpose(1, 0, 2).reshape(4, 4096).astype(f32)
    gain_one = small[:, 4096:4352].reshape(1, 1024).astype(f32)
    gain_two = small[:, 4352:4608].reshape(1, 1024).astype(f32)
    head_full = small[:, 4608:4672].reshape(1, 256).astype(f32)
    scale_full = small[:, 4672:4674].reshape(8).astype(f32)
    bias_full = small[:, 4674:4676].reshape(8).astype(f32)

    def unit_columns(value):
        q_part = lax.dynamic_slice_in_dim(value, head * 128, 128, axis=1)
        k_part = lax.dynamic_slice_in_dim(value, 1024 + head * 128, 128, axis=1)
        v_part = lax.dynamic_slice_in_dim(value, 2048 + unit * 128, 128, axis=1)
        return [q_part, k_part, v_part]

    unit_part = jnp.concatenate(
        unit_columns(w_mixer_one)
        + [
            lax.dynamic_slice_in_dim(w_outgate, unit * 128, 128, axis=1),
            lax.dynamic_slice_in_dim(w_rates, head, 1, axis=1),
            lax.dynamic_slice_in_dim(w_rates, 8 + head, 1, axis=1),
            jnp.zeros((256, 126), bf16),
        ],
        axis=1,
    )
    w_unit = in_grp_order(from_grp(unit_part), grp).reshape(1024, 640)
    taps = jnp.concatenate(unit_columns(conv_full), axis=1)
    scale = lax.dynamic_index_in_dim(scale_full, head, 0, False)
    bias = lax.dynamic_index_in_dim(bias_full, head, 0, False)
    head_half = lax.dynamic_slice_in_dim(head_full, core * 128, 128, axis=1)
    numbers = jnp.stack([core.astype(f32), bias, jnp.exp(scale), jnp.zeros((), f32)])

    def ff_columns(owner):
        at = owner * 704 + core * 352
        gate = lax.dynamic_slice_in_dim(w_gateup, at, 352, axis=1)
        up = lax.dynamic_slice_in_dim(w_gateup, FF + at, 352, axis=1)
        fill = jnp.zeros((256, 32), bf16)
        return jnp.concatenate([gate, fill, up, fill], axis=1)

    gateup_pieces = [ff_columns((grp + steps) % 4) for steps in range(4)]
    w_dn = jnp.concatenate(
        [lax.dynamic_slice_in_dim(w_down, core * 352, 352, axis=0), jnp.zeros((32, 1024), bf16)], axis=0
    )
    output_half = lax.dynamic_slice_in_dim(w_output_one, core * 256, 256, axis=0)
    output_mine = lax.all_gather(output_half, "grp", axis=0, tiled=True)

    positions = place * 64 + lax.broadcasted_iota(jnp.int32, (2, 64), 1)
    valid = (positions < seq_lengths[:, None]).astype(f32)[..., None]
    inputs_rows = block_input.astype(f32).reshape(128, 1024)
    r_one = lax.rsqrt(jnp.mean(inputs_rows * inputs_rows, axis=-1, keepdims=True) + epsilon)
    dy = (cotangent.astype(f32) * valid).reshape(128, 1024)
    dy_low = dy.astype(bf16)

    def to_wide(tokens):
        mine = jnp.concatenate(from_grp(tokens), axis=0)
        return jnp.concatenate([mine, other_core(mine)], axis=0)

    def from_wide(left, right, dims, sent):
        theirs = other_core(raw(left[512:], right, dims).astype(sent))
        mine = raw(left[:512], right, dims) + theirs.astype(f32)
        low = mine.reshape(4, 128, 1024).astype(sent)
        total = mine[:128]
        for steps in (1, 2, 3):
            total = total + along_grp(low[steps], -steps).astype(f32)
        return total

    places = jnp.stack([core, head])
    gateup_pieces, dy_sent, x_mine = lax.optimization_barrier((gateup_pieces, dy_low, x_mine))
    x_theirs = other_core(x_mine)
    dy_pieces = from_grp(dy_sent)
    gateup_pieces = gateup_pieces[:1] + [along_grp(gateup_pieces[steps], steps) for steps in (1, 2, 3)]

    (
        hidden_one, mixed_in, outgate, conv, columns, inverse, from_state, updates, scores, moves, states, heads_out,
        squares,
    ) = forward_call(numbers, x_mine, x_theirs, gain_one, w_unit, taps)
    output_theirs = other_core(output_mine)
    unit_at = head // 2 * 256 + core * 128
    output_unit = jnp.where(
        head % 2 == core,
        lax.dynamic_slice_in_dim(output_mine, unit_at, 128, axis=0),
        lax.dynamic_slice_in_dim(output_theirs, unit_at, 128, axis=0),
    )
    squares_theirs = other_core(squares)
    heads_out, gateup_pieces, dy_pieces = lax.optimization_barrier((heads_out, gateup_pieces, dy_pieces))
    gated = gate_call(heads_out, outgate, squares, squares_theirs, head_half)

    gated_tokens = lax.all_to_all(gated.reshape(32, 64, 128), "ctx", 0, 0)
    middle, hidden_two = middle_call(places, gated_tokens, block_input, output_mine, output_theirs, gain_two)
    r_two = lax.rsqrt(jnp.mean(middle * middle, axis=-1, keepdims=True) + epsilon)
    gateup_pieces, dy_pieces = lax.optimization_barrier((gateup_pieces, dy_pieces, hidden_two))[:2]
    w_gu = in_grp_order(gateup_pieces, grp).reshape(1024, 768)
    dy_wide = jnp.concatenate(dy_pieces, axis=0)
    dy_wide = jnp.concatenate([dy_wide, other_core(dy_wide)], axis=0)
    two_wide = to_wide(hidden_two)
    gateup = mm(two_wide, w_gu)
    gate, up = gateup[:, :384], gateup[:, 384:]
    sig = jax.nn.sigmoid(gate)
    silu_gate = gate * sig
    swi = (silu_gate * up).astype(bf16)
    dswi = mm_t(dy_wide, w_dn)
    dgate = dswi * up * (sig * (1.0 + gate * (1.0 - sig)))
    dgateup = jnp.concatenate([dgate, dswi * silu_gate], axis=1).astype(bf16)
    g_ff = ff_weights_call(two_wide, dgateup, swi, dy_wide)
    dhidden_two = from_wide(dgateup, w_gu, NT, f32)
    scaled = dhidden_two * gain_two
    dmiddle = dy + r_two * scaled - middle * r_two**3 * jnp.mean(scaled * middle, axis=-1, keepdims=True)
    dmix = dmiddle.astype(bf16)
    dmix, g_ff = lax.optimization_barrier((dmix, g_ff))
    dmix_mine, dmix_theirs = to_units(dmix.reshape(2, 64, 1024))

    d_normed, d_outgate, inner, g_early, g_head = gate_back_call(
        numbers, dmix_mine, dmix_theirs, output_unit, heads_out, outgate, squares, squares_theirs, head_half, gated,
        hidden_one,
    )
    inner_theirs = other_core(inner)
    g_ff, g_early, inner, d_normed = lax.optimization_barrier((g_ff, g_early, inner, d_normed))
    g_ff = over_chips(g_ff)
    early_mine, *early_others = exchange_grp(g_early.astype(bf16), grp)
    early_mine = lax.dynamic_index_in_dim(g_early, grp, 0, False)
    keep, give, g_unit, g_rates, g_taps, g_sums = backward_call(
        numbers, taps, conv, columns, inverse, from_state, updates, scores, moves, states, mixed_in,
        d_normed, heads_out, squares, squares_theirs, inner, inner_theirs, hidden_one, d_outgate, w_unit,
    )

    give_theirs = other_core(give)
    d_sent = (keep + give_theirs.astype(f32)).astype(bf16)
    d_tokens = over_chips(d_sent)

    g_rates = g_rates[:2].reshape(2, 4, 2, 128).transpose(1, 0, 2, 3).reshape(4, 4, 128)
    shared = jnp.concatenate(
        [g_taps[:4].reshape(12, 128), g_head[:1], g_sums[:2], jnp.zeros((5, 128), f32)], axis=0
    )
    g_small = jnp.concatenate([jnp.broadcast_to(shared, (4, 20, 128)), g_rates], axis=1)

    g_ff, early_others, give_theirs = lax.optimization_barrier((g_ff, early_others, give_theirs))
    g_ff = g_ff.astype(f32).sum(axis=0).astype(bf16)
    g_gu = in_grp_order(exchange_grp(g_ff[:384].reshape(4, 96, 128), grp), grp).reshape(384, 128)
    g_early = early_mine + sum(other.astype(f32) for other in early_others)
    g_early = jnp.concatenate(
        [g_early[:256].reshape(2, 128, 128), g_early[256:].reshape(8, 2, 16, 128).transpose(1, 0, 2, 3).reshape(2, 128, 128)],
        axis=1,
    )
    early_mine = lax.dynamic_index_in_dim(g_early, seq, 0, False)
    early_given = lax.dynamic_index_in_dim(g_early, 1 - seq, 0, False).astype(bf16)
    early_mine = (early_mine + other_seq(early_given).astype(f32)).astype(bf16)
    early_output = lax.ppermute(early_mine[128:], ("grp", "ctx"), OUTPUT_MOVES)
    early = jnp.concatenate([g_gu, g_ff[384:], early_mine[:128], early_output], axis=0)
    early_mine = lax.all_gather(early, "ctx", axis_index_groups=CHIPS)
    early_theirs = other_core(early_mine)
    grad_gateup, grad_down, mlp_sums = ff_grads_call(
        numbers, early_mine, early_theirs, w_gateup, jnp.broadcast_to(mlp_gain[:, None], (256, 128))
    )
    grad_outgate, grad_output, gate_sums = out_grads_call(
        numbers, early_mine[:, 640:], early_theirs[:, 640:], w_outgate
    )

    swi, g_unit, g_small = lax.optimization_barrier((swi, g_unit, g_small, d_sent))[:3]
    g_small = sum(exchange_grp(g_small, grp))
    g_sum = sum_grp(g_unit.reshape(4, 256, 384), grp).reshape(2, 128, 384)

    dhidden_one = d_tokens.astype(f32)
    dhidden_one = dhidden_one.reshape(2, 8, 64, 1024).sum(axis=1).reshape(128, 1024)
    scaled = dhidden_one * gain_one
    input_grad = (
        dmiddle + r_one * scaled - inputs_rows * r_one**3 * jnp.mean(scaled * inputs_rows, axis=-1, keepdims=True)
    )

    mine = lax.dynamic_index_in_dim(g_sum, seq, 0, False)
    given = lax.dynamic_index_in_dim(g_sum, 1 - seq, 0, False).astype(bf16)
    mine = mine + other_seq(given).astype(f32)
    halves = mine[:, :256].reshape(2, 64, 256)
    qk_mine = lax.dynamic_index_in_dim(halves, core, 0, False)
    qk_given = lax.dynamic_index_in_dim(halves, 1 - core, 0, False).astype(bf16)
    qk_mine = qk_mine + other_core(qk_given).astype(f32)
    late = jnp.concatenate([qk_mine[:, :128], qk_mine[:, 128:], mine[:, 256:]], axis=0).astype(bf16)
    small_high = lax.optimization_barrier(g_small.astype(bf16))
    small_low = (g_small - small_high.astype(f32)).astype(bf16)
    late = jnp.concatenate([late, small_high, small_low], axis=0)
    late, d_tokens = lax.optimization_barrier((late, d_tokens))
    late_mine = over_chips(jnp.broadcast_to(late, (16,) + late.shape))
    late_theirs = other_core(late_mine)
    grad_mixer, mixer_sums = mixer_grads_call(numbers, late_mine, late_theirs, w_mixer)
    small_one = (late_mine[:, 256:280].astype(f32) + late_mine[:, 280:].astype(f32)).reshape(2, 8, 24, 128)
    small_two = (late_theirs[:, 256:280].astype(f32) + late_theirs[:, 280:].astype(f32)).reshape(2, 8, 24, 128)
    small_one, small_two = small_one.sum(axis=0), small_two.sum(axis=0)
    both = small_one + small_two
    g_low = jnp.where(core == 0, small_one, small_two)
    g_high = jnp.where(core == 0, small_two, small_one)
    taps_at = lambda value, at: value[:, :12].reshape(8, 4, 3, 128)[:, :, at].transpose(1, 0, 2).reshape(4, 1024)
    taps_v = jnp.stack([g_low[:, :12], g_high[:, :12]], axis=1).reshape(8, 2, 4, 3, 128)[:, :, :, 2]
    taps_v = taps_v.transpose(2, 0, 1, 3).reshape(4, 2048)
    grad_conv = jnp.concatenate([taps_at(both, 0), taps_at(both, 1), taps_v], axis=1)
    grad_conv = lax.dynamic_slice_in_dim(grad_conv, grp * 1024, 1024, axis=1)
    grad_head = jnp.concatenate([g_low[:, 12].sum(axis=0), g_high[:, 12].sum(axis=0)])
    grad_head = lax.dynamic_slice_in_dim(grad_head, grp * 64, 64, axis=0)
    grad_scale = lax.dynamic_slice_in_dim(both[:, 13, 1], grp * 2, 2, axis=0)
    grad_bias = lax.dynamic_slice_in_dim(both[:, 14, 1], grp * 2, 2, axis=0)
    grad_rates = both[:, 20:].reshape(8, 2, 256).transpose(1, 0, 2).reshape(16, 256).T
    grad_in_gain = (
        mixer_sums[:, 0]
        + gate_sums[:, 0]
        + jnp.sum(grad_rates * w_rates.astype(f32), axis=1)
    ) / in_gain.astype(f32)

    block_out = middle + from_wide(swi, w_dn, NN, bf16)
    block_output = (block_out.reshape(2, 64, 1024) * valid).astype(bf16)

    return (
        block_output,
        input_grad.reshape(2, 64, 1024),
        grad_in_gain,
        grad_mixer,
        grad_conv,
        grad_rates,
        grad_scale,
        grad_bias,
        grad_outgate,
        grad_head,
        grad_output,
        mlp_sums[:, 0],
        grad_gateup,
        grad_down,
    )


def solution(mesh):
    tokens = P("grp", "ctx", None)
    rows = P("grp", None)
    one = P("grp")
    taps = P(None, "grp")
    return jax.shard_map(
        body,
        mesh=mesh,
        in_specs=(tokens, one, one, rows, taps, rows, one, one, rows, one, rows, one, rows, rows, tokens),
        out_specs=(tokens, tokens, one, rows, taps, rows, one, one, rows, one, rows, one, rows, rows),
        check_vma=False,
    )
```

time: 854 us -> 448 us (0.52)
  matrix products: 160 us -> 8.74 us
  local copies, waits for them, and re-layouts: 186 us -> 41.9 us
  Pallas kernels: 0 us -> 108 us
  other arithmetic: 130 us -> 26.5 us
  blocking collectives: 116 us -> 30.4 us
  waiting for transfers between devices: 158 us -> 100 us
  starting transfers between devices: 73 us -> 108 us
    dot_general x82 -> x6, matrix products: 160 us -> 8.74 us  [raw(): lax.dot_general(left, right, (dims, ((), ())), preferred_element_type=f32)]
    pallas_call x0 -> x9, Pallas kernels: none -> 108 us  [the longest x1 36.7 us: backward_call(): pl.pallas_call(backward_kernel, grid=(steps,), in_specs=[pl.BlockSpec(mem...]
    psum x1 -> x0, blocking collectives: 85 us -> none  [body(): lax.psum((spread, rates_spread, head_spread, scale_spread, bias_spread),...]
    all_gather x4 -> x2, waiting for transfers between devices: 87.9 us -> 3.46 us  [the longest x1 3.46 us: body(): early_mine = lax.all_gather(early, 'ctx', axis_index_groups=CHIPS)]
    transpose x9 -> x2, local copies, waits for them, and re-layouts: 38 us -> 0.04 us  [the longest x1 0.03 us: body(): taps_v = taps_v.transpose(2, 0, 1, 3).reshape(4, 2048)]
    reshape x12 -> x5, local copies, waits for them, and re-layouts: 34.4 us -> 0.09 us  [the longest x1 0.04 us: body(): taps_v = taps_v.transpose(2, 0, 1, 3).reshape(4, 2048)]
    unnamed x352 -> x116, local copies, waits for them, and re-layouts: 46.3 us -> 15 us
    convert_element_type x18 -> x9, other arithmetic: 30.9 us -> 6.62 us  [the longest x1 5.08 us: body(): d_sent = (keep + give_theirs.astype(f32)).astype(bf16)]
  transfers between devices with their start and end apart: 52 -> 56, of which waited for: 23 -> 25; matrix products, arithmetic and copies ran while one was open for 46% -> 12% of each run, Pallas kernels for 0% -> 19%
where the time goes in v2:
time: 448 us; the launch traced here: 441 us
  starting transfers between devices  108 us (24%)
  Pallas kernels  108 us (24%)
  waiting for transfers between devices  100 us (22%)
  local copies, waits for them, and re-layouts  41.9 us (9%)
  blocking collectives  30.4 us (7%)
  other arithmetic  26.5 us (6%)
  between operations  16.5 us (4%)
  matrix products  8.74 us (2%)
    ppermute x33, starting transfers between devices, along_grp(): lax.ppermute(value, 'grp', [(at, (at + steps) % 4) for at in range(4)])  52.5 us
    ppermute x33, waiting for transfers between devices, along_grp(): lax.ppermute(value, 'grp', [(at, (at + steps) % 4) for at in range(4)])  49.8 us
    pallas_call x1, Pallas kernels, backward_call(): pl.pallas_call(backward_kernel, grid=(steps,), in_specs=[pl.BlockSpec(mem...  36.7 us
    pallas_call x1, Pallas kernels, forward_call(): pl.pallas_call(forward_kernel, grid=(steps,), in_specs=[pl.BlockSpec(memo...  30.8 us
    all_to_all x1, blocking collectives, over_chips(): return lax.all_to_all(value, 'ctx', 0, 0, axis_index_groups=CHIPS)  30.4 us
    all_to_all x4, starting transfers between devices, over_chips(): return lax.all_to_all(value, 'ctx', 0, 0, axis_index_groups=CHIPS)  22.7 us
    ppermute x13, starting transfers between devices, other_core(): return lax.ppermute(value, 'ctx', OTHER_CORE)  18.8 us
    unnamed x116, local copies, waits for them, and re-layouts  15 us
  transfers between devices with their start and end apart: 56, of which 25 were waited for; matrix products, arithmetic and copies ran while one was open for 12% of the time, Pallas kernels for 19%

profile of v2, /device:TPU:1, one launch (start us, length us, event | category | flops | bytes accessed | tf_op | source)
XLA Modules:
  0.0 440.7 jit_solution(15658836177817230209)
XLA Ops:
  7.2 2.6 broadcast_in_dim.16
  9.9 7.8 %all-to-all-start = ((bf16[16,64,1024]{2,1,0:T(8,128)(2,1)}), bf16[16,64,1024]{2,1,0:T(8,128)(2,1)}, u32[]{:S(2)}, u32[]{:S(2)}) async-start(bf16[16,64,1024]{2,1,0:T(8,128)(2,1)} %bitcast.3), calls=%async_computation | async-start | bytes 4194304 | tf_op jit(solution)/shard_map/all_to_all | solution.py:763
  19.6 3.3 collective-permute-start.1
  30.1 2.4 constant_dynamic-slice_fusion.22
  38.3 9.9 %all-to-all-done.mine = bf16[16,64,1024]{2,1,0:T(8,128)(2,1)} async-done(((bf16[16,64,1024]{2,1,0:T(8,128)(2,1)}), bf16[16,64,1024]{2,1,0:T(8,128)(2,1)}, u32[]{:S(2)}, u32[]{:S(2)}) %all-to-all-start) | async-done | bytes 2097184 | tf_op jit(solution)/shard_map/all_to_all | solution.py:763
  55.9 3.8 collective-permute-start.12
  60.4 2.5 constant_dynamic-slice_fusion.14
  67.5 2.5 collective-permute-start.8
  70.8 5.5 %collective-permute-start.9 = (bf16[256,768]{1,0:T(8,128)(2,1)}, bf16[256,768]{1,0:T(8,128)(2,1)}, u32[]{:S(2)}, u32[]{:S(2)}) collective-permute-start(bf16[256,768]{1,0:T(8,128)(2,1)} %get-tuple-element.95), channel_id=1, source_target_pairs={{0,96},{32,0},{64,32},{96,64},{1,97},{33,1},{65,33},{97,65},{2,98}... | collective-permute-start | bytes 1179656 | tf_op jit(solution)/shard_map/ppermute | solution.py:732
  77.6 30.8 %delta_forward.1 = (bf16[2048,1024]{1,0:T(8,128)(2,1)}, bf16[2048,384]{1,0:T(8,128)(2,1)}, f32[2048,128]{1,0:T(8,128)S(1)}, f32[2048,384]{1,0:T(8,128)}, f32[204...) custom-call(f32[4]{0:T(128)S(1)} %pad_maximum_fusion.16.numbers, ...), custom_call_target="tpu_custom_call" | custom-call | flops 30000001024 | bytes 90000000 | tf_op jit(solution)/shard_map/delta_forward/pallas_call | solution.py:205
  111.7 3.5 gate.1.gated
  115.3 7.2 %all-to-all-start.1 = ((bf16[32,64,128]{2,1,0:T(8,128)(2,1)}), bf16[32,64,128]{2,1,0:T(8,128)(2,1)S(1)}, u32[]{:S(2)}, u32[]{:S(2)}) async-start(bf16[32,64,128]{2,1,0:T(8,128)(2,1)} %bitcast.17), calls=%async_computation.1 | async-start | bytes 1048576 | tf_op jit(solution)/shard_map/all_to_all | solution.py:900
  122.6 11.4 %all-to-all-done.1.gated = bf16[32,64,128]{2,1,0:T(8,128)(2,1)S(1)} async-done(((bf16[32,64,128]{2,1,0:T(8,128)(2,1)}), bf16[32,64,128]{2,1,0:T(8,128)(2,1)S(1)}, u32[]{:S(2)}, u32[]{:S(2)}) %all-to-all-start.1) | async-done | bytes 524320 | tf_op jit(solution)/shard_map/all_to_all | solution.py:900
  134.1 4.0 middle.1
  147.2 6.4 %collective-permute-done.15 = bf16[128,1024]{1,0:T(8,128)(2,1)S(1)} collective-permute-done((bf16[128,1024]{1,0:T(8,128)(2,1)S(1)}, bf16[128,1024]{1,0:T(8,128)(2,1)S(1)}, u32[]{:S(2)}, u32[]{:S(2)}) %collective-permute-start.15) | collective-permute-done | bytes 262176 | tf_op jit(solution)/shard_map/ppermute | solution.py:732
  163.1 2.5 collective-permute-done.20
  169.8 7.0 %ff_weights.1 = bf16[16,640,128]{2,1,0:T(8,128)(2,1)} custom-call(bf16[1024,1024]{1,0:T(8,128)(2,1)} %copy-done.23, bf16[1024,768]{1,0:T(8,128)(2,1)} %pad_maximum_fusion.grads, bf16[1024,384]{1,0:T(8,128)(2,1)S(1)} %get-tuple-element.144.swi, bf16[1024,1024]{1,0:T(8,128)(2,1)} %copy-done.24), custom_call_target="tpu_custom_call" | custom-call | flops 7000000000 | bytes 21000000 | tf_op jit(solution)/shard_map/ff_weights/pallas_call | solution.py:556
  176.9 3.2 collective-permute-done.21
  182.3 10.1 %collective-permute-done.22 = f32[128,1024]{1,0:T(8,128)S(1)} collective-permute-done((f32[128,1024]{1,0:T(8,128)S(1)}, f32[128,1024]{1,0:T(8,128)S(1)}, u32[]{:S(2)}, u32[]{:S(2)}) %collective-permute-start.22) | collective-permute-done | bytes 524320 | tf_op jit(solution)/shard_map/ppermute | solution.py:732
  193.2 30.4 %all_to_all.30.mine = bf16[16,64,1024]{2,1,0:T(8,128)(2,1)} all-to-all(bf16[16,64,1024]{2,1,0:T(8,128)(2,1)S(1)} %bitcast.216), channel_id=1, replica_groups={{0,2,4,6,8,10,12,14,16,18,20,22,24,26,28,30},{1,3,5,7,9,11,13,15,17,19,..., dimensions={0} | all-to-all | bytes 4194304 | tf_op jit(solution)/shard_map/all_to_all | solution.py:763
  223.6 2.8 collective-permute-start.24
  227.5 3.0 collective-permute-done.24.theirs
  230.6 9.7 %gate_back.1 = (f32[2048,128]{1,0:T(8,128)}, bf16[2048,128]{1,0:T(8,128)(2,1)S(1)}, f32[4,4,128]{2,1,0:T(4,128)S(1)}, f32[4,512,128]{2,1,0:T(8,128)}, f32[8,128]{1,0:T(8,128)S(1)}) custom-call(f32[4]{0:T(128)S(1)} %pad_maximum_fusion.16.numbers, bf16[16,64,1024]{2,1,0:T(8,128)(2,1)} %all_to_all.30.mine, ...), custom_call_target="tpu_custom_call" | custom-call | flops 8999999488 | bytes 27000000 | tf_op jit(solution)/shard_map/gate_back/pallas_call | solution.py:515
  240.7 4.5 %all-to-all-start.5 = ((bf16[16,640,128]{2,1,0:T(8,128)(2,1)}), bf16[16,640,128]{2,1,0:T(8,128)(2,1)}, u32[]{:S(2)}, u32[]{:S(2)}) async-start(bf16[16,640,128]{2,1,0:T(8,128)(2,1)} %ff_weights.1), calls=%async_computation.5 | async-start | bytes 5242880 | tf_op jit(solution)/shard_map/all_to_all | solution.py:763
  246.7 36.7 %delta_backward.1 = (f32[16,64,1024]{2,1,0:T(8,128)}, bf16[16,64,1024]{2,1,0:T(8,128)(2,1)}, f32[1024,384]{1,0:T(8,128)}, f32[8,1024]{1,0:T(8,128)S(1)}, f32[8,384]{1,0:T(8,128)S(1)}, /*index=5*/f32[8,128]{1,0:T(8,128)S(1)}) custom-call(f32[4]{0:T(128)S(1)} %pad_maximum_fusion.16.numbers, f32[4,384]{1,0:T(4,128)S(1)} %pad_maximum_fusion.14.taps, ...), custom_call_target="tpu_custom_call" | custom-call | flops 35999997952 | bytes 108000000 | tf_op jit(solution)/shard_map/delta_backward/pallas_call | solution.py:363
  287.6 3.0 collective-permute-done.42
  292.4 3.8 collective-permute-done.40
  296.9 2.8 reduce_sum.107
  301.9 3.1 collective-permute-start.46
  306.9 3.8 collective-permute-done.44
  312.5 5.1 %add_convert_fusion = bf16[16,64,1024]{2,1,0:T(8,128)(2,1)} fusion(f32[16,64,1024]{2,1,0:T(8,128)} %get-tuple-element.142, bf16[16,64,1024]{2,1,0:T(8,128)(2,1)} %collective-permute-done.26), kind=kLoop, calls=%fused_computation.1 | loop fusion | flops 3145728 | bytes 8388608 | tf_op jit(solution)/shard_map/convert_element_type | solution.py:939
  318.5 6.5 %collective-permute-start.31 = (bf16[256,384]{1,0:T(8,128)(2,1)}, bf16[256,384]{1,0:T(8,128)(2,1)S(1)}, u32[]{:S(2)}, u32[]{:S(2)}) collective-permute-start(bf16[256,384]{1,0:T(8,128)(2,1)} %get-tuple-element.193), channel_id=1, source_target_pairs={{0,32},{32,64},{64,96},{96,0},{1,33},{33,65},{65,97},{97,1},{2,34}... | collective-permute-start | bytes 589832 | tf_op jit(solution)/shard_map/ppermute | solution.py:732
  325.0 3.4 collective-permute-start.33
  329.7 4.7 %all-to-all-start.3 = ((bf16[16,64,1024]{2,1,0:T(8,128)(2,1)}), bf16[16,64,1024]{2,1,0:T(8,128)(2,1)}, u32[]{:S(2)}, u32[]{:S(2)}) async-start(bf16[16,64,1024]{2,1,0:T(8,128)(2,1)} %add_convert_fusion), calls=%async_computation.3 | async-start | bytes 4194304 | tf_op jit(solution)/shard_map/all_to_all | solution.py:763
  340.4 2.9 collective-permute-start.34
  344.0 6.1 %collective-permute-start.27 = (bf16[512,1024]{1,0:T(8,128)(2,1)S(1)}, bf16[512,1024]{1,0:T(8,128)(2,1)S(1)}, u32[]{:S(2)}, u32[]{:S(2)}) collective-permute-start(bf16[512,1024]{1,0:T(8,128)(2,1)S(1)} %convolution_convert_fusion), channel_id=1, source_target_pairs={{0,1},{1,0},{2,3},{3,2},{4,5},{5,4},{6,7},{7,6},{8,9},{9,8},{10,11... | collective-permute-start | bytes 3145736 | tf_op jit(solution)/shard_map/ppermute | solution.py:724
  350.1 13.1 %collective-permute-done.34 = bf16[128,384]{1,0:T(8,128)(2,1)S(1)} collective-permute-done((bf16[128,384]{1,0:T(8,128)(2,1)S(1)}, bf16[128,384]{1,0:T(8,128)(2,1)S(1)}, u32[]{:S(2)}, u32[]{:S(2)}) %collective-permute-start.34) | collective-permute-done | bytes 98336 | tf_op jit(solution)/shard_map/ppermute | solution.py:728
  365.8 2.4 fusion.69
  369.4 5.8 %all-to-all-start.4 = ((bf16[16,304,128]{2,1,0:T(8,128)(2,1)}), bf16[16,304,128]{2,1,0:T(8,128)(2,1)S(1)}, u32[]{:S(2)}, u32[]{:S(2)}) async-start(bf16[16,304,128]{2,1,0:T(8,128)(2,1)} %broadcast_in_dim.40), calls=%async_computation.4 | async-start | bytes 2490368 | tf_op jit(solution)/shard_map/all_to_all | solution.py:763
  378.7 2.9 collective-permute-start.29
  381.6 3.2 collective-permute-done.28
  384.8 2.3 collective-permute-done.30
  387.2 5.7 %collective-permute-done.29 = bf16[128,1024]{1,0:T(8,128)(2,1)S(1)} collective-permute-done((bf16[128,1024]{1,0:T(8,128)(2,1)}, bf16[128,1024]{1,0:T(8,128)(2,1)S(1)}, u32[]{:S(2)}, u32[]{:S(2)}) %collective-permute-start.29) | collective-permute-done | bytes 262176 | tf_op jit(solution)/shard_map/ppermute | solution.py:732
  394.9 3.5 all-gather.6.cloned.1.call-done
  404.6 2.5 collective-permute-done.39.theirs
  411.6 3.9 mixer_grads.1
  417.0 8.7 %ff_grads.1 = (f32[256,5632]{1,0:T(8,128)}, f32[704,1024]{1,0:T(8,128)}, f32[256,128]{1,0:T(8,128)S(1)}) custom-call(f32[4]{0:T(128)S(1)} %pad_maximum_fusion.16.numbers, bf16[16,896,128]{2,1,0:T(8,128)(2,1)} %bitcast.243, bf16[16,896,128]{2,1,0:T(8,128)(2,1)} %collective-permute-done.48.theirs, bf16[256,5632]{1,0:T(8,128)(2,1)} %weight.5, ...), custom_call_target="tpu_custom_call" | custom-call | flops 8000000000 | bytes 24000000 | tf_op jit(solution)/shard_map/ff_grads/pallas_call | solution.py:610
  428.7 4.1 out_grads.1
  (329 shorter events, 107.4 us)
Async XLA Ops:
  9.9 38.3 %all-to-all-start = ((bf16[16,64,1024]{2,1,0:T(8,128)(2,1)}), bf16[16,64,1024]{2,1,0:T(8,128)(2,1)}, u32[]{:S(2)}, u32[]{:S(2)}) async-start(bf16[16,64,1024]{2,1,0:T(8,128)(2,1)} %bitcast.3), calls=%async_computation | async-start | bytes 4194304 | tf_op jit(solution)/shard_map/all_to_all | solution.py:763
  17.7 58.5 %all-gather.4.cloned.1.call-start = ((), (), s32[]{:S(2)}) async-start(), calls=%async_computation.6 | async-start | bytes 2621440 | tf_op jit(solution)/shard_map/all_gather | solution.py:857
  17.9 18.1 %collective-permute-start.2 = (bf16[37,128]{1,0:T(8,128)(2,1)S(1)}, bf16[37,128]{1,0:T(8,128)(2,1)S(1)}, u32[]{:S(2)}, u32[]{:S(2)}) collective-permute-start(bf16[37,128]{1,0:T(8,128)(2,1)S(1)} %bitcast.252), channel_id=1, source_target_pairs={{0,32},{32,64},{64,96},{96,0},{1,33},{33,65},{65,97},{97,1},{2,34}... | collective-permute-start | bytes 28424 | tf_op jit(solution)/shard_map/ppermute | solution.py:732
  19.6 16.4 %collective-permute-start.1 = (bf16[37,128]{1,0:T(8,128)(2,1)S(1)}, bf16[37,128]{1,0:T(8,128)(2,1)S(1)}, u32[]{:S(2)}, u32[]{:S(2)}) collective-permute-start(bf16[37,128]{1,0:T(8,128)(2,1)S(1)} %bitcast.253), channel_id=1, source_target_pairs={{0,64},{32,96},{64,0},{96,32},{1,65},{33,97},{65,1},{97,33},{2,66}... | collective-permute-start | bytes 28424 | tf_op jit(solution)/shard_map/ppermute | solution.py:732
  22.9 11.0 %collective-permute-start = (bf16[37,128]{1,0:T(8,128)(2,1)S(1)}, bf16[37,128]{1,0:T(8,128)(2,1)S(1)}, u32[]{:S(2)}, u32[]{:S(2)}) collective-permute-start(bf16[37,128]{1,0:T(8,128)(2,1)S(1)} %bitcast.254), channel_id=1, source_target_pairs={{0,96},{32,0},{64,32},{96,64},{1,97},{33,1},{65,33},{97,65},{2,98}... | collective-permute-start | bytes 28424 | tf_op jit(solution)/shard_map/ppermute | solution.py:732
  25.9 26.8 %collective-permute-start.6 = (bf16[256,640]{1,0:T(8,128)(2,1)S(1)}, bf16[256,640]{1,0:T(8,128)(2,1)}, u32[]{:S(2)}, u32[]{:S(2)}) collective-permute-start(bf16[256,640]{1,0:T(8,128)(2,1)S(1)} %concatenate.72), channel_id=1, source_target_pairs={{0,32},{32,64},{64,96},{96,0},{1,33},{33,65},{65,97},{97,1},{2,34}... | collective-permute-start | bytes 983048 | tf_op jit(solution)/shard_map/ppermute | solution.py:732
  26.7 25.2 %collective-permute-start.5 = (bf16[256,640]{1,0:T(8,128)(2,1)S(1)}, bf16[256,640]{1,0:T(8,128)(2,1)S(1)}, u32[]{:S(2)}, u32[]{:S(2)}) collective-permute-start(bf16[256,640]{1,0:T(8,128)(2,1)S(1)} %concatenate.72), channel_id=1, source_target_pairs={{0,64},{32,96},{64,0},{96,32},{1,65},{33,97},{65,1},{97,33},{2,66}... | collective-permute-start | bytes 983048 | tf_op jit(solution)/shard_map/ppermute | solution.py:732
  33.9 17.2 %collective-permute-start.4 = (bf16[256,640]{1,0:T(8,128)(2,1)S(1)}, bf16[256,640]{1,0:T(8,128)(2,1)S(1)}, u32[]{:S(2)}, u32[]{:S(2)}) collective-permute-start(bf16[256,640]{1,0:T(8,128)(2,1)S(1)} %concatenate.72), channel_id=1, source_target_pairs={{0,96},{32,0},{64,32},{96,64},{1,97},{33,1},{65,33},{97,65},{2,98}... | collective-permute-start | bytes 983048 | tf_op jit(solution)/shard_map/ppermute | solution.py:732
  48.2 28.0 %collective-permute-start.3 = (bf16[16,64,1024]{2,1,0:T(8,128)(2,1)}, bf16[16,64,1024]{2,1,0:T(8,128)(2,1)}, u32[]{:S(2)}, u32[]{:S(2)}) collective-permute-start(bf16[16,64,1024]{2,1,0:T(8,128)(2,1)} %all-to-all-done.mine), channel_id=1, source_target_pairs={{0,1},{1,0},{2,3},{3,2},{4,5},{5,4},{6,7},{7,6},{8,9},{9,8},{10,11... | collective-permute-start | bytes 6291464 | tf_op jit(solution)/shard_map/ppermute | solution.py:724
  55.9 11.6 %collective-permute-start.12 = (bf16[128,1024]{1,0:T(8,128)(2,1)S(1)}, bf16[128,1024]{1,0:T(8,128)(2,1)S(1)}, u32[]{:S(2)}, u32[]{:S(2)}) collective-permute-start(bf16[128,1024]{1,0:T(8,128)(2,1)S(1)} %bitcast_convert_fusion), channel_id=1, source_target_pairs={{0,96},{32,0},{64,32},{96,64},{1,97},{33,1},{65,33},{97,65},{2,98}... | collective-permute-start | bytes 786440 | tf_op jit(solution)/shard_map/ppermute | solution.py:732
  59.7 10.4 %collective-permute-start.11 = (bf16[128,1024]{1,0:T(8,128)(2,1)S(1)}, bf16[128,1024]{1,0:T(8,128)(2,1)S(1)}, u32[]{:S(2)}, u32[]{:S(2)}) collective-permute-start(bf16[128,1024]{1,0:T(8,128)(2,1)S(1)} %bitcast_convert_fusion), channel_id=1, source_target_pairs={{0,64},{32,96},{64,0},{96,32},{1,65},{33,97},{65,1},{97,33},{2,66}... | collective-permute-start | bytes 786440 | tf_op jit(solution)/shard_map/ppermute | solution.py:732
  62.9 46.4 %collective-permute-start.10 = (bf16[128,1024]{1,0:T(8,128)(2,1)S(1)}, bf16[128,1024]{1,0:T(8,128)(2,1)S(1)}, u32[]{:S(2)}, u32[]{:S(2)}) collective-permute-start(bf16[128,1024]{1,0:T(8,128)(2,1)S(1)} %bitcast_convert_fusion), channel_id=1, source_target_pairs={{0,32},{32,64},{64,96},{96,0},{1,33},{33,65},{65,97},{97,1},{2,34}... | collective-permute-start | bytes 786440 | tf_op jit(solution)/shard_map/ppermute | solution.py:732
  63.6 45.8 %collective-permute-start.7 = (bf16[256,768]{1,0:T(8,128)(2,1)}, bf16[256,768]{1,0:T(8,128)(2,1)}, u32[]{:S(2)}, u32[]{:S(2)}) collective-permute-start(bf16[256,768]{1,0:T(8,128)(2,1)} %get-tuple-element.93), channel_id=1, source_target_pairs={{0,32},{32,64},{64,96},{96,0},{1,33},{33,65},{65,97},{97,1},{2,34}... | collective-permute-start | bytes 1179656 | tf_op jit(solution)/shard_map/ppermute | solution.py:732
  67.5 41.9 %collective-permute-start.8 = (bf16[256,768]{1,0:T(8,128)(2,1)}, bf16[256,768]{1,0:T(8,128)(2,1)S(1)}, u32[]{:S(2)}, u32[]{:S(2)}) collective-permute-start(bf16[256,768]{1,0:T(8,128)(2,1)} %get-tuple-element.94), channel_id=1, source_target_pairs={{0,64},{32,96},{64,0},{96,32},{1,65},{33,97},{65,1},{97,33},{2,66}... | collective-permute-start | bytes 1179656 | tf_op jit(solution)/shard_map/ppermute | solution.py:732
  70.8 38.7 %collective-permute-start.9 = (bf16[256,768]{1,0:T(8,128)(2,1)}, bf16[256,768]{1,0:T(8,128)(2,1)}, u32[]{:S(2)}, u32[]{:S(2)}) collective-permute-start(bf16[256,768]{1,0:T(8,128)(2,1)} %get-tuple-element.95), channel_id=1, source_target_pairs={{0,96},{32,0},{64,32},{96,64},{1,97},{33,1},{65,33},{97,65},{2,98}... | collective-permute-start | bytes 1179656 | tf_op jit(solution)/shard_map/ppermute | solution.py:732
  76.2 57.8 %collective-permute-start.14 = (bf16[1024,1024]{1,0:T(8,128)(2,1)}, bf16[1024,1024]{1,0:T(8,128)(2,1)}, u32[]{:S(2)}, u32[]{:S(2)}) collective-permute-start(bf16[1024,1024]{1,0:T(8,128)(2,1)} %all-gather.4.cloned.1.call-done.mine), channel_id=1, source_target_pairs={{0,1},{1,0},{2,3},{3,2},{4,5},{5,4},{6,7},{7,6},{8,9},{9,8},{10,11... | collective-permute-start | bytes 6291464 | tf_op jit(solution)/shard_map/ppermute | solution.py:724
  115.3 18.7 %all-to-all-start.1 = ((bf16[32,64,128]{2,1,0:T(8,128)(2,1)}), bf16[32,64,128]{2,1,0:T(8,128)(2,1)S(1)}, u32[]{:S(2)}, u32[]{:S(2)}) async-start(bf16[32,64,128]{2,1,0:T(8,128)(2,1)} %bitcast.17), calls=%async_computation.1 | async-start | bytes 1048576 | tf_op jit(solution)/shard_map/all_to_all | solution.py:900
  138.1 7.5 %collective-permute-start.17 = (bf16[128,1024]{1,0:T(8,128)(2,1)S(1)}, bf16[128,1024]{1,0:T(8,128)(2,1)S(1)}, u32[]{:S(2)}, u32[]{:S(2)}) collective-permute-start(bf16[128,1024]{1,0:T(8,128)(2,1)S(1)} %get-tuple-element.102), channel_id=1, source_target_pairs={{0,96},{32,0},{64,32},{96,64},{1,97},{33,1},{65,33},{97,65},{2,98}... | collective-permute-start | bytes 786440 | tf_op jit(solution)/shard_map/ppermute | solution.py:732
  138.1 9.0 %collective-permute-start.16 = (bf16[128,1024]{1,0:T(8,128)(2,1)S(1)}, bf16[128,1024]{1,0:T(8,128)(2,1)S(1)}, u32[]{:S(2)}, u32[]{:S(2)}) collective-permute-start(bf16[128,1024]{1,0:T(8,128)(2,1)S(1)} %get-tuple-element.102), channel_id=1, source_target_pairs={{0,64},{32,96},{64,0},{96,32},{1,65},{33,97},{65,1},{97,33},{2,66}... | collective-permute-start | bytes 786440 | tf_op jit(solution)/shard_map/ppermute | solution.py:732
  139.7 13.9 %collective-permute-start.15 = (bf16[128,1024]{1,0:T(8,128)(2,1)S(1)}, bf16[128,1024]{1,0:T(8,128)(2,1)S(1)}, u32[]{:S(2)}, u32[]{:S(2)}) collective-permute-start(bf16[128,1024]{1,0:T(8,128)(2,1)S(1)} %get-tuple-element.102), channel_id=1, source_target_pairs={{0,32},{32,64},{64,96},{96,0},{1,33},{33,65},{65,97},{97,1},{2,34}... | collective-permute-start | bytes 786440 | tf_op jit(solution)/shard_map/ppermute | solution.py:732
  140.6 14.1 %collective-permute-start.19 = (bf16[512,1024]{1,0:T(8,128)(2,1)S(1)}, bf16[512,1024]{1,0:T(8,128)(2,1)S(1)}, u32[]{:S(2)}, u32[]{:S(2)}) collective-permute-start(bf16[512,1024]{1,0:T(8,128)(2,1)S(1)} %pad_maximum_fusion.2), channel_id=1, source_target_pairs={{0,1},{1,0},{2,3},{3,2},{4,5},{5,4},{6,7},{7,6},{8,9},{9,8},{10,11... | collective-permute-start | bytes 3145736 | tf_op jit(solution)/shard_map/ppermute | solution.py:724
  166.9 13.2 %collective-permute-start.21 = (f32[128,1024]{1,0:T(8,128)S(1)}, f32[128,1024]{1,0:T(8,128)S(1)}, u32[]{:S(2)}, u32[]{:S(2)}) collective-permute-start(f32[128,1024]{1,0:T(8,128)S(1)} %get-tuple-element.184), channel_id=1, source_target_pairs={{0,96},{32,0},{64,32},{96,64},{1,97},{33,1},{65,33},{97,65},{2,98}... | collective-permute-start | bytes 1572872 | tf_op jit(solution)/shard_map/ppermute | solution.py:732
  167.7 14.6 %collective-permute-start.23 = (f32[128,1024]{1,0:T(8,128)S(1)}, f32[128,1024]{1,0:T(8,128)S(1)}, u32[]{:S(2)}, u32[]{:S(2)}) collective-permute-start(f32[128,1024]{1,0:T(8,128)S(1)} %get-tuple-element.185), channel_id=1, source_target_pairs={{0,32},{32,64},{64,96},{96,0},{1,33},{33,65},{65,97},{97,1},{2,34}... | collective-permute-start | bytes 1572872 | tf_op jit(solution)/shard_map/ppermute | solution.py:732
  168.4 24.1 %collective-permute-start.22 = (f32[128,1024]{1,0:T(8,128)S(1)}, f32[128,1024]{1,0:T(8,128)S(1)}, u32[]{:S(2)}, u32[]{:S(2)}) collective-permute-start(f32[128,1024]{1,0:T(8,128)S(1)} %get-tuple-element.186), channel_id=1, source_target_pairs={{0,64},{32,96},{64,0},{96,32},{1,65},{33,97},{65,1},{97,33},{2,66}... | collective-permute-start | bytes 1572872 | tf_op jit(solution)/shard_map/ppermute | solution.py:732
  223.6 6.9 %collective-permute-start.24 = (bf16[16,64,1024]{2,1,0:T(8,128)(2,1)}, bf16[16,64,1024]{2,1,0:T(8,128)(2,1)}, u32[]{:S(2)}, u32[]{:S(2)}) collective-permute-start(bf16[16,64,1024]{2,1,0:T(8,128)(2,1)} %all_to_all.30.mine), channel_id=1, source_target_pairs={{0,1},{1,0},{2,3},{3,2},{4,5},{5,4},{6,7},{7,6},{8,9},{9,8},{10,11... | collective-permute-start | bytes 6291464 | tf_op jit(solution)/shard_map/ppermute | solution.py:724
  240.2 5.2 %collective-permute-start.25 = (f32[4,4,128]{2,1,0:T(4,128)S(1)}, f32[4,4,128]{2,1,0:T(4,128)S(1)}, u32[]{:S(2)}, u32[]{:S(2)}) collective-permute-start(f32[4,4,128]{2,1,0:T(4,128)S(1)} %get-tuple-element.135.in_mine), channel_id=1, source_target_pairs={{0,1},{1,0},{2,3},{3,2},{4,5},{5,4},{6,7},{7,6},{8,9},{9,8},{10,11... | collective-permute-start | bytes 24584 | tf_op jit(solution)/shard_map/ppermute | solution.py:724
  240.7 55.6 %all-to-all-start.5 = ((bf16[16,640,128]{2,1,0:T(8,128)(2,1)}), bf16[16,640,128]{2,1,0:T(8,128)(2,1)}, u32[]{:S(2)}, u32[]{:S(2)}) async-start(bf16[16,640,128]{2,1,0:T(8,128)(2,1)} %ff_weights.1), calls=%async_computation.5 | async-start | bytes 5242880 | tf_op jit(solution)/shard_map/all_to_all | solution.py:763
  245.2 153.2 %all-gather.6.cloned.1.call-start = ((), (), s32[]{:S(2)}) async-start(), calls=%async_computation.7 | async-start | bytes 3899392 | tf_op jit(solution)/shard_map/all_gather | solution.py:961
  283.4 12.9 %collective-permute-start.26 = (bf16[16,64,1024]{2,1,0:T(8,128)(2,1)}, bf16[16,64,1024]{2,1,0:T(8,128)(2,1)}, u32[]{:S(2)}, u32[]{:S(2)}) collective-permute-start(bf16[16,64,1024]{2,1,0:T(8,128)(2,1)} %get-tuple-element.143), channel_id=1, source_target_pairs={{0,1},{1,0},{2,3},{3,2},{4,5},{5,4},{6,7},{7,6},{8,9},{9,8},{10,11... | collective-permute-start | bytes 6291464 | tf_op jit(solution)/shard_map/ppermute | solution.py:724
  286.3 6.1 %collective-permute-start.41 = (bf16[512,128]{1,0:T(8,128)(2,1)}, bf16[512,128]{1,0:T(8,128)(2,1)S(1)}, u32[]{:S(2)}, u32[]{:S(2)}) collective-permute-start(bf16[512,128]{1,0:T(8,128)(2,1)} %get-tuple-element.197), channel_id=1, source_target_pairs={{0,64},{32,96},{64,0},{96,32},{1,65},{33,97},{65,1},{97,33},{2,66}... | collective-permute-start | bytes 393224 | tf_op jit(solution)/shard_map/ppermute | solution.py:732
  286.7 9.5 %collective-permute-start.40 = (bf16[512,128]{1,0:T(8,128)(2,1)}, bf16[512,128]{1,0:T(8,128)(2,1)S(1)}, u32[]{:S(2)}, u32[]{:S(2)}) collective-permute-start(bf16[512,128]{1,0:T(8,128)(2,1)} %get-tuple-element.198), channel_id=1, source_target_pairs={{0,32},{32,64},{64,96},{96,0},{1,33},{33,65},{65,97},{97,1},{2,34}... | collective-permute-start | bytes 393224 | tf_op jit(solution)/shard_map/ppermute | solution.py:732
  301.8 5.1 %collective-permute-start.43 = (bf16[96,128]{1,0:T(8,128)(2,1)S(1)}, bf16[96,128]{1,0:T(8,128)(2,1)S(1)}, u32[]{:S(2)}, u32[]{:S(2)}) collective-permute-start(bf16[96,128]{1,0:T(8,128)(2,1)S(1)} %get-tuple-element.209), channel_id=1, source_target_pairs={{0,96},{32,0},{64,32},{96,64},{1,97},{33,1},{65,33},{97,65},{2,98}... | collective-permute-start | bytes 73736 | tf_op jit(solution)/shard_map/ppermute | solution.py:732
  301.9 8.9 %collective-permute-start.46 = (bf16[256,128]{1,0:T(8,128)(2,1)S(1)}, bf16[256,128]{1,0:T(8,128)(2,1)S(1)}, u32[]{:S(2)}, u32[]{:S(2)}) collective-permute-start(bf16[256,128]{1,0:T(8,128)(2,1)S(1)} %fusion.39), channel_id=1, source_target_pairs={{0,16},{1,17},{2,18},{3,19},{4,20},{5,21},{6,22},{7,23},{8,24},{9,... | collective-permute-start | bytes 196616 | tf_op jit(solution)/shard_map/ppermute | solution.py:728
  305.1 5.7 %collective-permute-start.45 = (bf16[96,128]{1,0:T(8,128)(2,1)S(1)}, bf16[96,128]{1,0:T(8,128)(2,1)S(1)}, u32[]{:S(2)}, u32[]{:S(2)}) collective-permute-start(bf16[96,128]{1,0:T(8,128)(2,1)S(1)} %get-tuple-element.206), channel_id=1, source_target_pairs={{0,32},{32,64},{64,96},{96,0},{1,33},{33,65},{65,97},{97,1},{2,34}... | collective-permute-start | bytes 73736 | tf_op jit(solution)/shard_map/ppermute | solution.py:732
  318.5 18.7 %collective-permute-start.31 = (bf16[256,384]{1,0:T(8,128)(2,1)}, bf16[256,384]{1,0:T(8,128)(2,1)S(1)}, u32[]{:S(2)}, u32[]{:S(2)}) collective-permute-start(bf16[256,384]{1,0:T(8,128)(2,1)} %get-tuple-element.193), channel_id=1, source_target_pairs={{0,32},{32,64},{64,96},{96,0},{1,33},{33,65},{65,97},{97,1},{2,34}... | collective-permute-start | bytes 589832 | tf_op jit(solution)/shard_map/ppermute | solution.py:732
  325.0 14.0 %collective-permute-start.33 = (bf16[256,384]{1,0:T(8,128)(2,1)}, bf16[256,384]{1,0:T(8,128)(2,1)}, u32[]{:S(2)}, u32[]{:S(2)}) collective-permute-start(bf16[256,384]{1,0:T(8,128)(2,1)} %get-tuple-element.194), channel_id=1, source_target_pairs={{0,96},{32,0},{64,32},{96,64},{1,97},{33,1},{65,33},{97,65},{2,98}... | collective-permute-start | bytes 589832 | tf_op jit(solution)/shard_map/ppermute | solution.py:732
  328.4 10.5 %collective-permute-start.32 = (bf16[256,384]{1,0:T(8,128)(2,1)S(1)}, bf16[256,384]{1,0:T(8,128)(2,1)}, u32[]{:S(2)}, u32[]{:S(2)}) collective-permute-start(bf16[256,384]{1,0:T(8,128)(2,1)S(1)} %get-tuple-element.195), channel_id=1, source_target_pairs={{0,64},{32,96},{64,0},{96,32},{1,65},{33,97},{65,1},{97,33},{2,66}... | collective-permute-start | bytes 589832 | tf_op jit(solution)/shard_map/ppermute | solution.py:732
  329.7 38.5 %all-to-all-start.3 = ((bf16[16,64,1024]{2,1,0:T(8,128)(2,1)}), bf16[16,64,1024]{2,1,0:T(8,128)(2,1)}, u32[]{:S(2)}, u32[]{:S(2)}) async-start(bf16[16,64,1024]{2,1,0:T(8,128)(2,1)} %add_convert_fusion), calls=%async_computation.3 | async-start | bytes 4194304 | tf_op jit(solution)/shard_map/all_to_all | solution.py:763
  334.5 30.4 %collective-permute-start.36 = (f32[24,128]{1,0:T(8,128)S(1)}, f32[24,128]{1,0:T(8,128)S(1)}, u32[]{:S(2)}, u32[]{:S(2)}) collective-permute-start(f32[24,128]{1,0:T(8,128)S(1)} %get-tuple-element.221), channel_id=1, source_target_pairs={{0,32},{32,64},{64,96},{96,0},{1,33},{33,65},{65,97},{97,1},{2,34}... | collective-permute-start | bytes 36872 | tf_op jit(solution)/shard_map/ppermute | solution.py:732
  335.2 29.7 %collective-permute-start.38 = (f32[24,128]{1,0:T(8,128)S(1)}, f32[24,128]{1,0:T(8,128)S(1)}, u32[]{:S(2)}, u32[]{:S(2)}) collective-permute-start(f32[24,128]{1,0:T(8,128)S(1)} %get-tuple-element.222), channel_id=1, source_target_pairs={{0,96},{32,0},{64,32},{96,64},{1,97},{33,1},{65,33},{97,65},{2,98}... | collective-permute-start | bytes 36872 | tf_op jit(solution)/shard_map/ppermute | solution.py:732
  337.2 27.7 %collective-permute-start.37 = (f32[24,128]{1,0:T(8,128)S(1)}, f32[24,128]{1,0:T(8,128)S(1)}, u32[]{:S(2)}, u32[]{:S(2)}) collective-permute-start(f32[24,128]{1,0:T(8,128)S(1)} %get-tuple-element.223), channel_id=1, source_target_pairs={{0,64},{32,96},{64,0},{96,32},{1,65},{33,97},{65,1},{97,33},{2,66}... | collective-permute-start | bytes 36872 | tf_op jit(solution)/shard_map/ppermute | solution.py:732
  340.4 22.8 %collective-permute-start.34 = (bf16[128,384]{1,0:T(8,128)(2,1)S(1)}, bf16[128,384]{1,0:T(8,128)(2,1)S(1)}, u32[]{:S(2)}, u32[]{:S(2)}) collective-permute-start(bf16[128,384]{1,0:T(8,128)(2,1)S(1)} %fusion.38), channel_id=1, source_target_pairs={{0,16},{1,17},{2,18},{3,19},{4,20},{5,21},{6,22},{7,23},{8,24},{9,... | collective-permute-start | bytes 294920 | tf_op jit(solution)/shard_map/ppermute | solution.py:728
  344.0 21.8 %collective-permute-start.27 = (bf16[512,1024]{1,0:T(8,128)(2,1)S(1)}, bf16[512,1024]{1,0:T(8,128)(2,1)S(1)}, u32[]{:S(2)}, u32[]{:S(2)}) collective-permute-start(bf16[512,1024]{1,0:T(8,128)(2,1)S(1)} %convolution_convert_fusion), channel_id=1, source_target_pairs={{0,1},{1,0},{2,3},{3,2},{4,5},{5,4},{6,7},{7,6},{8,9},{9,8},{10,11... | collective-permute-start | bytes 3145736 | tf_op jit(solution)/shard_map/ppermute | solution.py:724
  369.4 33.0 %all-to-all-start.4 = ((bf16[16,304,128]{2,1,0:T(8,128)(2,1)}), bf16[16,304,128]{2,1,0:T(8,128)(2,1)S(1)}, u32[]{:S(2)}, u32[]{:S(2)}) async-start(bf16[16,304,128]{2,1,0:T(8,128)(2,1)} %broadcast_in_dim.40), calls=%async_computation.4 | async-start | bytes 2490368 | tf_op jit(solution)/shard_map/all_to_all | solution.py:763
  377.3 7.6 %collective-permute-start.28 = (bf16[128,1024]{1,0:T(8,128)(2,1)}, bf16[128,1024]{1,0:T(8,128)(2,1)S(1)}, u32[]{:S(2)}, u32[]{:S(2)}) collective-permute-start(bf16[128,1024]{1,0:T(8,128)(2,1)} %get-tuple-element.190), channel_id=1, source_target_pairs={{0,96},{32,0},{64,32},{96,64},{1,97},{33,1},{65,33},{97,65},{2,98}... | collective-permute-start | bytes 786440 | tf_op jit(solution)/shard_map/ppermute | solution.py:732
  378.7 8.5 %collective-permute-start.30 = (bf16[128,1024]{1,0:T(8,128)(2,1)}, bf16[128,1024]{1,0:T(8,128)(2,1)S(1)}, u32[]{:S(2)}, u32[]{:S(2)}) collective-permute-start(bf16[128,1024]{1,0:T(8,128)(2,1)} %get-tuple-element.191), channel_id=1, source_target_pairs={{0,32},{32,64},{64,96},{96,0},{1,33},{33,65},{65,97},{97,1},{2,34}... | collective-permute-start | bytes 786440 | tf_op jit(solution)/shard_map/ppermute | solution.py:732
  378.7 14.2 %collective-permute-start.29 = (bf16[128,1024]{1,0:T(8,128)(2,1)}, bf16[128,1024]{1,0:T(8,128)(2,1)S(1)}, u32[]{:S(2)}, u32[]{:S(2)}) collective-permute-start(bf16[128,1024]{1,0:T(8,128)(2,1)} %get-tuple-element.192), channel_id=1, source_target_pairs={{0,64},{32,96},{64,0},{96,32},{1,65},{33,97},{65,1},{97,33},{2,66}... | collective-permute-start | bytes 786440 | tf_op jit(solution)/shard_map/ppermute | solution.py:732
  398.4 18.5 %collective-permute-start.48 = (bf16[16,896,128]{2,1,0:T(8,128)(2,1)}, bf16[16,896,128]{2,1,0:T(8,128)(2,1)}, u32[]{:S(2)}, u32[]{:S(2)}) collective-permute-start(bf16[16,896,128]{2,1,0:T(8,128)(2,1)} %bitcast.241), channel_id=1, source_target_pairs={{0,1},{1,0},{2,3},{3,2},{4,5},{5,4},{6,7},{7,6},{8,9},{9,8},{10,11... | collective-permute-start | bytes 11010056 | tf_op jit(solution)/shard_map/ppermute | solution.py:724
  (43 other events, 407.7 us)
Sparse Core Ops, SparseCore 0:
  29.1 35.7 all-gather.3
  312.4 85.9 all-gather.5

commit v3 on v2

--- a/solution.py
+++ b/solution.py
@@ -18,13 +18,6 @@
 CHIPS = [[chip * 2 + core for chip in range(16)] for core in range(2)]
 OTHER_CORE = [(place, place ^ 1) for place in range(32)]
 OTHER_SEQ = [(place, place ^ 16) for place in range(32)]
-OUTPUT_MOVES = [
-    (at * 32 + s * 16 + h * 2 + v, (h // 2) * 32 + s * 16 + ((h % 2) * 4 + at) * 2 + v)
-    for at in range(4)
-    for s in range(2)
-    for h in range(8)
-    for v in range(2)
-]
 
 NN = ((1,), (0,))
 NT = ((1,), (1,))
@@ -98,11 +91,15 @@
     return q, k, rq, rk
 
 
+def block_of(places, steps):
+    return pl.ds(pl.multiple_of(places[2 + steps] * 256, 256), 256)
+
+
 def forward_kernel(
-    numbers, mine, theirs, gain, weight, taps,
+    numbers, places, mine, theirs, gain, weight_0, weight_1, weight_2, weight_3, taps,
     hidden_out, mixed_out, gate_out, conv_out, cols_out, inv_out, from_out, upd_out, score_out, move_out, state_out,
     heads_out, square_out,
-    state, ext,
+    state, ext, held,
 ):
     step = pl.program_id(0)
     core, bias, scale = numbers[0], numbers[1], numbers[2]
@@ -111,6 +108,8 @@
     def _():
         state[...] = jnp.zeros_like(state)
         ext[0:8, :] = jnp.zeros((8, 384), f32)
+        for steps, weight in enumerate((weight_0, weight_1, weight_2, weight_3)):
+            held[block_of(places, steps), :] = weight[...]
 
     first = core < 0.5
     for at in range(GROUP):
@@ -118,7 +117,7 @@
         x = jnp.concatenate([jnp.where(first, one, two), jnp.where(first, two, one)], axis=0).astype(f32)
         rate = lax.rsqrt(jnp.mean(x * x, axis=-1, keepdims=True) + epsilon)
         hidden_out[at * CHUNK : (at + 1) * CHUNK, :] = (x * rate * gain[...]).astype(bf16)
-    projected = raw(hidden_out[...], weight[...], NN)
+    projected = raw(hidden_out[...], held[...], NN)
     mixed = projected[:, :384].astype(bf16)
     mixed_out[...] = mixed
     gate_out[...] = projected[:, 384:512]
@@ -196,7 +195,7 @@
         square_out[0, at : at + 1, :] = squares[0:1, :]
 
 
-def forward_call(numbers, mine, theirs, gain, weight, taps):
+def forward_call(numbers, places, mine, theirs, gain, weights, taps):
     steps = 16 // GROUP
     shape = jax.ShapeDtypeStruct
     blocks = lambda width: pl.BlockSpec((ROWS, width), lambda i: (i, 0))
@@ -207,12 +206,13 @@
         grid=(steps,),
         in_specs=[
             pl.BlockSpec(memory_space=pltpu.SMEM),
+            pl.BlockSpec(memory_space=pltpu.SMEM),
             pl.BlockSpec((GROUP, 64, 1024), lambda i: (i, 0, 0)),
             pl.BlockSpec((GROUP, 64, 1024), lambda i: (i, 0, 0)),
             whole(1, 1024),
-            whole(1024, 640),
-            whole(4, 384),
-        ],
+        ]
+        + [whole(256, 640)] * 4
+        + [whole(4, 384)],
         out_specs=[blocks(1024), blocks(384), blocks(128), blocks(384)]
         + [blocks(128)] * 8
         + [pl.BlockSpec((1, GROUP, 128), lambda i: (i, 0, 0))],
@@ -224,20 +224,25 @@
         ]
         + [square] * 8
         + [shape((steps, GROUP, 128), f32)],
-        scratch_shapes=[pltpu.VMEM((128, 128), f32), pltpu.VMEM((ROWS + 8, 384), f32)],
+        scratch_shapes=[
+            pltpu.VMEM((128, 128), f32),
+            pltpu.VMEM((ROWS + 8, 384), f32),
+            pltpu.VMEM((1024, 640), bf16),
+        ],
         compiler_params=pltpu.CompilerParams(
             dimension_semantics=("arbitrary",), vmem_limit_bytes=52 * 1024 * 1024
         ),
         cost_estimate=cost(30),
         name="delta_forward",
-    )(numbers, mine, theirs, gain, weight, taps)
+    )(numbers, places, mine, theirs, gain, *weights, taps)
 
 
 def backward_kernel(
-    numbers, taps, conv_in, cols_in, inv_in, from_in, upd_in, score_in, move_in, state_in, mixed_in,
-    normed_in, heads_in, sq_mine, sq_theirs, in_mine, in_theirs, hidden_in, gate_in, weight,
-    keep_out, give_out, unit_out, logits_out, taps_out, sums_out,
-    after, ext, d_all,
+    numbers, places, taps, conv_in, cols_in, inv_in, from_in, upd_in, score_in, move_in, state_in, mixed_in,
+    normed_in, heads_in, sq_mine, sq_theirs, in_mine, in_theirs, hidden_in, gate_in,
+    weight_0, weight_1, weight_2, weight_3,
+    keep_out, give_out, unit_out, low_out, logits_out, taps_out, sums_out,
+    after, ext, d_all, held,
 ):
     step = pl.program_id(0)
     scale = numbers[2]
@@ -250,6 +255,8 @@
         sums_out[...] = jnp.zeros_like(sums_out)
         unit_out[...] = jnp.zeros_like(unit_out)
         logits_out[...] = jnp.zeros_like(logits_out)
+        for steps, weight in enumerate((weight_0, weight_1, weight_2, weight_3)):
+            held[block_of(places, steps), :] = weight[...]
 
     rows, cols = square_iota()
     strict = cols < rows
@@ -343,17 +350,21 @@
     d_all[:, 384:512] = gate_in[...]
     ext[ROWS : ROWS + 8, :] = ext[0:8, :]
     hidden = hidden_in[...]
-    unit_out[...] += raw(hidden, d_all[:, :384], TN)
+    unit_out[...] += raw(hidden, d_all[:, :512], TN)
     logits_out[...] += raw(d_all[:, 512:], hidden, TN)[:8]
     first = numbers[0] < 0.5
     for at in range(GROUP):
-        product = raw(d_all[at * CHUNK : (at + 1) * CHUNK, :], weight[...], NT)
+        product = raw(d_all[at * CHUNK : (at + 1) * CHUNK, :], held[...], NT)
         low, high = product[:64], product[64:]
         keep_out[at] = jnp.where(first, low, high)
         give_out[at] = jnp.where(first, high, low).astype(bf16)
 
-
-def backward_call(numbers, taps, *arrays):
+    @pl.when(step == 16 // GROUP - 1)
+    def _():
+        low_out[...] = unit_out[...].astype(bf16)
+
+
+def backward_call(numbers, places, taps, *arrays):
     steps = 16 // GROUP
     shape = jax.ShapeDtypeStruct
     blocks = lambda width: pl.BlockSpec((ROWS, width), lambda i: (steps - 1 - i, 0))
@@ -363,16 +374,19 @@
     return pl.pallas_call(
         backward_kernel,
         grid=(steps,),
-        in_specs=[pl.BlockSpec(memory_space=pltpu.SMEM), whole(4, 384), blocks(384)]
+        in_specs=[pl.BlockSpec(memory_space=pltpu.SMEM)] * 2
+        + [whole(4, 384), blocks(384)]
         + [blocks(128)] * 7
         + [blocks(384), blocks(128), blocks(128)]
         + [lines] * 4
-        + [blocks(1024), blocks(128), whole(1024, 640)],
-        out_specs=[halves, halves, whole(1024, 384), whole(8, 1024), whole(8, 384), whole(8, 128)],
+        + [blocks(1024), blocks(128)]
+        + [whole(256, 640)] * 4,
+        out_specs=[halves, halves, whole(1024, 512), whole(1024, 512), whole(8, 1024), whole(8, 384), whole(8, 128)],
         out_shape=[
             shape((16, 64, 1024), f32),
             shape((16, 64, 1024), bf16),
-            shape((1024, 384), f32),
+            shape((1024, 512), f32),
+            shape((1024, 512), bf16),
             shape((8, 1024), f32),
             shape((8, 384), f32),
             shape((8, 128), f32),
@@ -381,13 +395,14 @@
             pltpu.VMEM((128, 128), f32),
             pltpu.VMEM((ROWS + 8, 384), f32),
             pltpu.VMEM((ROWS, 640), bf16),
+            pltpu.VMEM((1024, 640), bf16),
         ],
         compiler_params=pltpu.CompilerParams(
             dimension_semantics=("arbitrary",), vmem_limit_bytes=52 * 1024 * 1024
         ),
         cost_estimate=cost(36),
         name="delta_backward",
-    )(numbers, taps, *arrays)
+    )(numbers, places, taps, *arrays)
 
 
 def row_to_square(row):
@@ -448,7 +463,7 @@
     for at in range(2):
         line = tokens[at].astype(f32)
         for weight, parity in ((mine, core), (theirs, 1 - core)):
-            found = [gated[at * 16 + grp * 4 + parity * 2 + half] for grp in range(4) for half in range(2)]
+            found = [gated[at * 16 + numbers[2 + grp] * 4 + parity * 2 + half] for grp in range(4) for half in range(2)]
             line = line + raw(jnp.concatenate(found, axis=1), weight[...], NN)
         rows = slice(at * 64, at * 64 + 64)
         middle_out[rows, :] = line
@@ -468,114 +483,200 @@
     )(places, gated, tokens, mine, theirs, gain)
 
 
+def d_gated_kernel(places, grads, mine, theirs, out):
+    core = places[0]
+    for weight, parity in ((mine, core), (theirs, 1 - core)):
+        found = raw(grads[...], weight[...], NT)
+        for seq in range(2):
+            for grp in range(4):
+                for half in range(2):
+                    at = (grp * 2 + half) * 128
+                    to = seq * 16 + places[2 + grp] * 4 + parity * 2 + half
+                    out[to] = found[seq * 64 : seq * 64 + 64, at : at + 128]
+
+
+def d_gated_call(places, grads, mine, theirs):
+    return pl.pallas_call(
+        d_gated_kernel,
+        in_specs=[pl.BlockSpec(memory_space=pltpu.SMEM)] + [pl.BlockSpec(memory_space=pltpu.VMEM)] * 3,
+        out_shape=jax.ShapeDtypeStruct((32, 64, 128), f32),
+        compiler_params=pltpu.CompilerParams(vmem_limit_bytes=52 * 1024 * 1024),
+        cost_estimate=cost(3),
+        name="d_gated",
+    )(places, grads, mine, theirs)
+
+
+def output_weights_kernel(
+    left_0, left_1, left_2, left_3, grads_0, grads_1, grads_2, grads_3, out
+):
+    grads = jnp.concatenate([grads_0[...], grads_1[...], grads_2[...], grads_3[...]], axis=0)
+    for parity in range(2):
+        for half in range(2):
+            left = [side[seq, parity, half] for side in (left_0, left_1, left_2, left_3) for seq in range(2)]
+            found = raw(jnp.concatenate(left, axis=0), grads, TN).astype(bf16)
+            for part in range(8):
+                for block in range(8):
+                    piece = found[part * 16 : part * 16 + 16, block * 128 : block * 128 + 128]
+                    at = parity * 128 + block * 16
+                    out[half * 8 + part, at : at + 16, :] = piece
+
+
+def output_weights_call(*arrays):
+    return pl.pallas_call(
+        output_weights_kernel,
+        in_specs=[pl.BlockSpec(memory_space=pltpu.VMEM)] * 8,
+        out_shape=jax.ShapeDtypeStruct((16, 256, 128), bf16),
+        compiler_params=pltpu.CompilerParams(vmem_limit_bytes=52 * 1024 * 1024),
+        cost_estimate=cost(3),
+        name="output_weights",
+    )(*arrays)
+
+
+def ff_kernel(two, dy, weight, down, swi_out, grads_out, part_out):
+    gateup = raw(two[...], weight[...], NN)
+    d_swi = raw(dy[...], down[...], NT)
+    gate, up = gateup[:, :384], gateup[:, 384:]
+    sig = jax.nn.sigmoid(gate)
+    active = gate * sig
+    swi_out[...] = (active * up).astype(bf16)
+    grads_out[:, :384] = (d_swi * up * (sig * (1.0 + gate * (1.0 - sig)))).astype(bf16)
+    grads_out[:, 384:] = (d_swi * active).astype(bf16)
+    part_out[...] = raw(grads_out[...], weight[...], NT)
+
+
+def ff_call(two, dy, weight, down):
+    shape = jax.ShapeDtypeStruct
+    rows = lambda width: pl.BlockSpec((256, width), lambda i: (i, 0))
+    whole = lambda *dims: pl.BlockSpec(dims, lambda i: (0, 0))
+    return pl.pallas_call(
+        ff_kernel,
+        grid=(2,),
+        in_specs=[rows(1024), rows(1024), whole(1024, 768), whole(384, 1024)],
+        out_specs=[rows(384), rows(768), rows(1024)],
+        out_shape=[shape((512, 384), bf16), shape((512, 768), bf16), shape((512, 1024), f32)],
+        compiler_params=params(),
+        cost_estimate=cost(5),
+        name="ff",
+    )(two, dy, weight, down)
+
+
+def ff_sum_kernel(two, dy, weight, down, added, swi_out, grads_out, low_out, own_out, part):
+    ff_kernel(two, dy, weight, down, swi_out, grads_out, part)
+    total = part[...] + added[...]
+    low_out[...] = total.astype(bf16)
+
+    @pl.when(pl.program_id(0) == 0)
+    def _():
+        own_out[...] = total[:128]
+
+
+def ff_sum_call(two, dy, weight, down, added):
+    shape = jax.ShapeDtypeStruct
+    rows = lambda width: pl.BlockSpec((256, width), lambda i: (i, 0))
+    whole = lambda *dims: pl.BlockSpec(dims, lambda i: (0, 0))
+    return pl.pallas_call(
+        ff_sum_kernel,
+        grid=(2,),
+        in_specs=[rows(1024), rows(1024), whole(1024, 768), whole(384, 1024), rows(1024)],
+        out_specs=[rows(384), rows(768), rows(1024), whole(128, 1024)],
+        out_shape=[
+            shape((512, 384), bf16),
+            shape((512, 768), bf16),
+            shape((512, 1024), bf16),
+            shape((128, 1024), f32),
+        ],
+        scratch_shapes=[pltpu.VMEM((256, 1024), f32)],
+        compiler_params=params(),
+        cost_estimate=cost(5),
+        name="ff_sum",
+    )(two, dy, weight, down, added)
+
+
 def gate_back_kernel(
-    numbers, mine, theirs, weight, heads, gate, sq_mine, sq_theirs, gain, gated, hidden,
-    normed_out, gate_out, inner_out, early_out, head_out,
-    output_sum, gate_sum,
+    d_gated, heads, gate, sq_mine, sq_theirs, gain,
+    normed_out, gate_out, inner_out, head_out,
 ):
     @pl.when(pl.program_id(0) == 0)
     def _():
-        output_sum[...] = jnp.zeros_like(output_sum)
-        gate_sum[...] = jnp.zeros_like(gate_sum)
         head_out[...] = jnp.zeros_like(head_out)
 
-    first = numbers[0] < 0.5
     ones = jnp.ones((8, 256), bf16)
     for at in range(GROUP):
         here = slice(at * CHUNK, (at + 1) * CHUNK)
-        one, two = mine[at], theirs[at]
-        grads = jnp.concatenate([jnp.where(first, one, two), jnp.where(first, two, one)], axis=0)
-        d_gated = raw(grads, weight[...], NT)
-        output_sum[...] += raw(gated[here, :], grads, TN)
+        grads = d_gated[here, :]
         value = heads[here, :]
         normed = value * head_rates(sq_mine, sq_theirs, at)
         logits = gate[here, :]
         sig = jax.nn.sigmoid(logits)
         active = logits * sig
-        head_out[0:1, :] += jnp.sum(d_gated * normed * active, axis=0, keepdims=True)
-        gained = d_gated * gain[...]
+        head_out[0:1, :] += jnp.sum(grads * normed * active, axis=0, keepdims=True)
+        gained = grads * gain[...]
         gate_out[here, :] = (gained * normed * (sig * (1.0 + logits * (1.0 - sig)))).astype(bf16)
         d_normed = gained * active
         normed_out[here, :] = d_normed
         product = raw(ones, jnp.concatenate(split(d_normed * value), axis=1), NT)
         inner_out[0, at : at + 1, :] = product[0:1, :]
-    gate_sum[...] += raw(hidden[...], gate_out[...], TN)
-
-    @pl.when(pl.program_id(0) == 16 // GROUP - 1)
-    def _():
-        for grp in range(4):
-            early_out[grp, :256, :] = gate_sum[grp * 256 : grp * 256 + 256, :]
-            for part in range(8):
-                block = output_sum[grp * 32 : grp * 32 + 32, part * 128 : part * 128 + 128]
-                early_out[grp, 256 + part * 32 : 288 + part * 32, :] = block
-
-
-def gate_back_call(numbers, mine, theirs, weight, *arrays):
+
+
+def gate_back_call(*arrays):
     shape = jax.ShapeDtypeStruct
     return pl.pallas_call(
         gate_back_kernel,
         grid=(16 // GROUP,),
-        in_specs=specs(
-            "smem", "tokens", "tokens", (128, 1024), 128, 128, "rows", "rows", (1, 128), 128, 1024
-        ),
-        out_specs=specs(128, 128, "rows", (4, 512, 128), (8, 128)),
+        in_specs=specs(128, 128, 128, "rows", "rows", (1, 128)),
+        out_specs=specs(128, 128, "rows", (8, 128)),
         out_shape=[
             shape((2048, 128), f32),
             shape((2048, 128), bf16),
             shape((16 // GROUP, GROUP, 128), f32),
-            shape((4, 512, 128), f32),
             shape((8, 128), f32),
         ],
-        scratch_shapes=[pltpu.VMEM((128, 1024), f32), pltpu.VMEM((1024, 128), f32)],
         compiler_params=params(),
-        cost_estimate=cost(9),
+        cost_estimate=cost(4),
         name="gate_back",
-    )(numbers, mine, theirs, weight, *arrays)
-
-
-def ff_weights_kernel(two, grads, swi, dy, out):
+    )(*arrays)
+
+
+def ff_weights_kernel(two_0, two_1, grads_0, grads_1, swi_0, swi_1, dy_0, dy_1, out):
     grp = pl.program_id(0)
-    found = raw(two[...], grads[...], TN).astype(bf16)
+    found = raw(two_0[...], grads_0[...], TN) + raw(two_1[...], grads_1[...], TN)
     for chip in range(16):
         for part in range(6):
             at = pl.multiple_of(grp * 96 + part * 16, 16)
             block = found[chip * 16 : chip * 16 + 16, part * 128 : part * 128 + 128]
             out[chip, pl.ds(at, 16), :] = block
-    found = raw(swi[...], dy[...], TN).astype(bf16)
+    found = raw(swi_0[...], dy_0[...], TN) + raw(swi_1[...], dy_1[...], TN)
     for chip in range(16):
         for part in range(2):
             at = pl.multiple_of(384 + grp * 64 + part * 32, 32)
             if chip < 11:
                 block = found[chip * 32 : chip * 32 + 32, part * 128 : part * 128 + 128]
             else:
-                block = jnp.zeros((32, 128), bf16)
+                block = jnp.zeros((32, 128), f32)
             out[chip, pl.ds(at, 32), :] = block
 
 
-def ff_weights_call(two, grads, swi, dy):
+def ff_weights_call(*arrays):
+    columns = pl.BlockSpec((512, 256), lambda i: (0, i))
+    whole = lambda width: pl.BlockSpec((512, width), lambda i: (0, 0))
     return pl.pallas_call(
         ff_weights_kernel,
         grid=(4,),
-        in_specs=[
-            pl.BlockSpec((1024, 256), lambda i: (0, i)),
-            pl.BlockSpec((1024, 768), lambda i: (0, 0)),
-            pl.BlockSpec((1024, 384), lambda i: (0, 0)),
-            pl.BlockSpec((1024, 256), lambda i: (0, i)),
-        ],
+        in_specs=[columns] * 2 + [whole(768)] * 2 + [whole(384)] * 2 + [columns] * 2,
         out_specs=pl.BlockSpec((16, 640, 128), lambda i: (0, 0, 0)),
-        out_shape=jax.ShapeDtypeStruct((16, 640, 128), bf16),
+        out_shape=jax.ShapeDtypeStruct((16, 640, 128), f32),
         compiler_params=params(),
         cost_estimate=cost(7),
         name="ff_weights",
-    )(two, grads, swi, dy)
-
-
-def ff_grads_kernel(numbers, mine, theirs, weight, gain, gateup_out, down_out, gain_out):
+    )(*arrays)
+
+
+def ff_grads_kernel(numbers, places, mine, theirs, weight, gain, gateup_out, down_out, output_out, gain_out):
     step = pl.program_id(0)
     first = numbers[0] < 0.5
 
     def piece(core, chip, at, size):
-        one, two = mine[chip, at : at + size, :], theirs[chip, at : at + size, :]
+        one, two = mine[chip, pl.ds(at, size), :], theirs[chip, pl.ds(at, size), :]
         return (jnp.where(first, one, two) if core == 0 else jnp.where(first, two, one)).astype(f32)
 
     for chip in range(4):
@@ -585,9 +686,9 @@
             found = []
             for grp in range(4):
                 for core in range(2):
-                    at = (grp * 6 + half * 3) * 16
                     for part in range(3):
-                        block = piece(core, chip, at + part * 16, 16)
+                        at = pl.multiple_of(places[2 + grp] * 96 + half * 48 + part * 16, 16)
+                        block = piece(core, chip, at, 16)
                         found.append(block if part < 2 else block[:, :96])
             line = jnp.concatenate(found, axis=1)
             gateup_out[rows, half * FF : (half + 1) * FF] = line
@@ -597,6 +698,11 @@
         total = jnp.sum(total, axis=1, keepdims=True)
         gain_out[rows, :] = jnp.broadcast_to(total, (16, 128)) / gain[rows, :].astype(f32)
 
+        for core in range(2):
+            at = pl.multiple_of(core * 256 + (step * 4 + chip) * 16, 16)
+            for part in range(8):
+                output_out[pl.ds(at, 16), part * 128 : part * 128 + 128] = piece(core, chip, 640 + part * 16, 16)
+
         @pl.when(step * 4 + chip < 11)
         def _():
             for core in range(2):
@@ -605,72 +711,38 @@
                     down_out[pl.ds(at, 32), part * 128 : part * 128 + 128] = piece(core, chip, 384 + part * 32, 32)
 
 
-def ff_grads_call(numbers, mine, theirs, weight, gain):
+def ff_grads_call(numbers, places, mine, theirs, weight, gain):
     shape = jax.ShapeDtypeStruct
     return pl.pallas_call(
         ff_grads_kernel,
         grid=(4,),
         in_specs=[
             pl.BlockSpec(memory_space=pltpu.SMEM),
-            pl.BlockSpec((4, 640, 128), lambda i: (i, 0, 0)),
-            pl.BlockSpec((4, 640, 128), lambda i: (i, 0, 0)),
+            pl.BlockSpec(memory_space=pltpu.SMEM),
+            pl.BlockSpec((4, 768, 128), lambda i: (i, 0, 0)),
+            pl.BlockSpec((4, 768, 128), lambda i: (i, 0, 0)),
             pl.BlockSpec((64, 2 * FF), lambda i: (i, 0)),
             pl.BlockSpec((64, 128), lambda i: (i, 0)),
         ],
         out_specs=[
             pl.BlockSpec((64, 2 * FF), lambda i: (i, 0)),
             pl.BlockSpec((704, 1024), lambda i: (0, 0)),
+            pl.BlockSpec((512, 1024), lambda i: (0, 0)),
             pl.BlockSpec((64, 128), lambda i: (i, 0)),
         ],
-        out_shape=[shape((256, 2 * FF), f32), shape((704, 1024), f32), shape((256, 128), f32)],
+        out_shape=[
+            shape((256, 2 * FF), f32),
+            shape((704, 1024), f32),
+            shape((512, 1024), f32),
+            shape((256, 128), f32),
+        ],
         compiler_params=params(),
         cost_estimate=cost(8),
         name="ff_grads",
-    )(numbers, mine, theirs, weight, gain)
-
-
-def out_grads_kernel(numbers, mine, theirs, weight, gate_out, output_out, sum_out):
-    first = numbers[0] < 0.5
-    for chip in range(16):
-        seq, head = chip // 8, chip % 8
-        one, two = mine[chip], theirs[chip]
-        for core in range(2):
-            piece = (jnp.where(first, one, two) if core == 0 else jnp.where(first, two, one)).astype(f32)
-            to = head * 256 + core * 128
-            gate_out[seq * 128 : seq * 128 + 128, to : to + 128] = piece[:128]
-            at = head // 4 * 256 + core * 128 + head % 4 * 32 + seq * 16
-            for part in range(8):
-                block = piece[128 + part * 16 : 144 + part * 16]
-                output_out[at : at + 16, part * 128 : part * 128 + 128] = block
-    for rows in (slice(0, 128), slice(128, 256)):
-        total = jnp.sum(gate_out[rows, :] * weight[rows, :].astype(f32), axis=1, keepdims=True)
-        sum_out[rows, :] = jnp.broadcast_to(total, (128, 128))
-
-
-def out_grads_call(numbers, mine, theirs, weight):
-    shape = jax.ShapeDtypeStruct
-    return pl.pallas_call(
-        out_grads_kernel,
-        grid=(1,),
-        in_specs=[
-            pl.BlockSpec(memory_space=pltpu.SMEM),
-            pl.BlockSpec((16, 256, 128), lambda i: (0, 0, 0)),
-            pl.BlockSpec((16, 256, 128), lambda i: (0, 0, 0)),
-            pl.BlockSpec((256, 2048), lambda i: (0, 0)),
-        ],
-        out_specs=[
-            pl.BlockSpec((256, 2048), lambda i: (0, 0)),
-            pl.BlockSpec((512, 1024), lambda i: (0, 0)),
-            pl.BlockSpec((256, 128), lambda i: (0, 0)),
-        ],
-        out_shape=[shape((256, 2048), f32), shape((512, 1024), f32), shape((256, 128), f32)],
-        compiler_params=params(),
-        cost_estimate=cost(4),
-        name="out_grads",
-    )(numbers, mine, theirs, weight)
-
-
-def mixer_grads_kernel(numbers, mine, theirs, weight, mixer_out, sum_out):
+    )(numbers, places, mine, theirs, weight, gain)
+
+
+def mixer_grads_kernel(numbers, mine, theirs, weight, gate_weight, mixer_out, gate_out, sum_out):
     first = numbers[0] < 0.5
     for head in range(8):
         one, two = mine[head], theirs[head]
@@ -682,30 +754,35 @@
             mixer_out[rows, 1024 + head * 128 : 1152 + head * 128] = piece[64:128]
             to = 2048 + head * 256 + core * 128
             mixer_out[:, to : to + 128] = piece[128:256]
+            to = head * 256 + core * 128
+            gate_out[:, to : to + 128] = piece[256:384]
     total = jnp.sum(mixer_out[...] * weight[...].astype(f32), axis=1, keepdims=True)
+    total = total + jnp.sum(gate_out[...] * gate_weight[...].astype(f32), axis=1, keepdims=True)
     sum_out[...] = jnp.broadcast_to(total, (128, 128))
 
 
-def mixer_grads_call(numbers, mine, theirs, weight):
+def mixer_grads_call(numbers, mine, theirs, weight, gate_weight):
     shape = jax.ShapeDtypeStruct
     return pl.pallas_call(
         mixer_grads_kernel,
         grid=(2,),
         in_specs=[
             pl.BlockSpec(memory_space=pltpu.SMEM),
-            pl.BlockSpec((8, 256, 128), lambda i: (i, 0, 0)),
-            pl.BlockSpec((8, 256, 128), lambda i: (i, 0, 0)),
+            pl.BlockSpec((8, 384, 128), lambda i: (i, 0, 0)),
+            pl.BlockSpec((8, 384, 128), lambda i: (i, 0, 0)),
             pl.BlockSpec((128, 4096), lambda i: (i, 0)),
+            pl.BlockSpec((128, 2048), lambda i: (i, 0)),
         ],
         out_specs=[
             pl.BlockSpec((128, 4096), lambda i: (i, 0)),
+            pl.BlockSpec((128, 2048), lambda i: (i, 0)),
             pl.BlockSpec((128, 128), lambda i: (i, 0)),
         ],
-        out_shape=[shape((256, 4096), f32), shape((256, 128), f32)],
+        out_shape=[shape((256, 4096), f32), shape((256, 2048), f32), shape((256, 128), f32)],
         compiler_params=params(),
         cost_estimate=cost(4),
         name="mixer_grads",
-    )(numbers, mine, theirs, weight)
+    )(numbers, mine, theirs, weight, gate_weight)
 
 
 def mm(left, right):
@@ -755,21 +832,13 @@
     return total
 
 
-def after(value, *others):
-    return lax.optimization_barrier((value,) + others)[0]
+def sum_chips(value):
+    flat = value.reshape(-1, 128)
+    return lax.psum_scatter(flat, "ctx", scatter_dimension=0, tiled=True, axis_index_groups=CHIPS)
 
 
 def over_chips(value):
     return lax.all_to_all(value, "ctx", 0, 0, axis_index_groups=CHIPS)
-
-
-def to_units(tokens):
-    mine = over_chips(jnp.repeat(tokens, 8, axis=0))
-    return mine, other_core(mine)
-
-
-def wide_columns(value, width):
-    return jnp.concatenate([value[:, at * 128 : at * 128 + 128] for at in range(width // 128)], axis=0)
 
 
 def body(
@@ -797,21 +866,39 @@
     unit = place % 16
 
     x_all = jnp.repeat(block_input, 8, axis=0)
+    w_mixer_one, w_output_one, x_all = lax.optimization_barrier((w_mixer, w_output, x_all))
     x_mine = over_chips(x_all)
-    w_mixer_one, w_output_one, conv_one = lax.optimization_barrier((w_mixer, w_output, conv_weight, x_all))[:3]
+
+    def unit_columns(value):
+        q_part = lax.dynamic_slice_in_dim(value, head * 128, 128, axis=1)
+        k_part = lax.dynamic_slice_in_dim(value, 1024 + head * 128, 128, axis=1)
+        v_part = lax.dynamic_slice_in_dim(value, 2048 + unit * 128, 128, axis=1)
+        return [q_part, k_part, v_part]
 
     small = jnp.concatenate(
         [
-            conv_one.reshape(-1),
+            conv_weight.reshape(-1),
             in_gain,
             mlp_gain,
             head_gain,
             decay_scale,
             decay_bias,
-            jnp.zeros((60,), bf16),
+            jnp.zeros((188,), bf16),
         ]
-    ).reshape(-1, 128)
-    small = in_grp_order(from_grp(small), grp).reshape(4, -1)
+    ).reshape(256, 19)
+    unit_part = jnp.concatenate(
+        unit_columns(w_mixer_one)
+        + [
+            lax.dynamic_slice_in_dim(w_outgate, unit * 128, 128, axis=1),
+            lax.dynamic_slice_in_dim(w_rates, head, 1, axis=1),
+            lax.dynamic_slice_in_dim(w_rates, 8 + head, 1, axis=1),
+            small,
+            jnp.zeros((256, 107), bf16),
+        ],
+        axis=1,
+    )
+    w_unit = from_grp(unit_part)
+    small = in_grp_order([piece[:, 514:533] for piece in w_unit], grp).reshape(4, -1)
     conv_full = small[:, :4096].reshape(4, 4, 1024).transpose(1, 0, 2).reshape(4, 4096).astype(f32)
     gain_one = small[:, 4096:4352].reshape(1, 1024).astype(f32)
     gain_two = small[:, 4352:4608].reshape(1, 1024).astype(f32)
@@ -819,23 +906,6 @@
     scale_full = small[:, 4672:4674].reshape(8).astype(f32)
     bias_full = small[:, 4674:4676].reshape(8).astype(f32)
 
-    def unit_columns(value):
-        q_part = lax.dynamic_slice_in_dim(value, head * 128, 128, axis=1)
-        k_part = lax.dynamic_slice_in_dim(value, 1024 + head * 128, 128, axis=1)
-        v_part = lax.dynamic_slice_in_dim(value, 2048 + unit * 128, 128, axis=1)
-        return [q_part, k_part, v_part]
-
-    unit_part = jnp.concatenate(
-        unit_columns(w_mixer_one)
-        + [
-            lax.dynamic_slice_in_dim(w_outgate, unit * 128, 128, axis=1),
-            lax.dynamic_slice_in_dim(w_rates, head, 1, axis=1),
-            lax.dynamic_slice_in_dim(w_rates, 8 + head, 1, axis=1),
-            jnp.zeros((256, 126), bf16),
-        ],
-        axis=1,
-    )
-    w_unit = in_grp_order(from_grp(unit_part), grp).reshape(1024, 640)
     taps = jnp.concatenate(unit_columns(conv_full), axis=1)
     scale = lax.dynamic_index_in_dim(scale_full, head, 0, False)
     bias = lax.dynamic_index_in_dim(bias_full, head, 0, False)
@@ -849,12 +919,11 @@
         fill = jnp.zeros((256, 32), bf16)
         return jnp.concatenate([gate, fill, up, fill], axis=1)
 
-    gateup_pieces = [ff_columns((grp + steps) % 4) for steps in range(4)]
+    gateup_pieces = jnp.stack([ff_columns(owner) for owner in range(4)])
     w_dn = jnp.concatenate(
         [lax.dynamic_slice_in_dim(w_down, core * 352, 352, axis=0), jnp.zeros((32, 1024), bf16)], axis=0
     )
     output_half = lax.dynamic_slice_in_dim(w_output_one, core * 256, 256, axis=0)
-    output_mine = lax.all_gather(output_half, "grp", axis=0, tiled=True)
 
     positions = place * 64 + lax.broadcasted_iota(jnp.int32, (2, 64), 1)
     valid = (positions < seq_lengths[:, None]).astype(f32)[..., None]
@@ -865,111 +934,105 @@
 
     def to_wide(tokens):
         mine = jnp.concatenate(from_grp(tokens), axis=0)
-        return jnp.concatenate([mine, other_core(mine)], axis=0)
-
-    def from_wide(left, right, dims, sent):
-        theirs = other_core(raw(left[512:], right, dims).astype(sent))
-        mine = raw(left[:512], right, dims) + theirs.astype(f32)
-        low = mine.reshape(4, 128, 1024).astype(sent)
-        total = mine[:128]
+        return mine, other_core(mine)
+
+    def over_cores(mine, theirs, sent):
+        mine = mine + other_core(theirs.astype(sent)).astype(f32)
+        return mine[:128], mine.reshape(4, 128, 1024).astype(bf16)
+
+    def over_grp(total, low):
         for steps in (1, 2, 3):
             total = total + along_grp(low[steps], -steps).astype(f32)
         return total
 
-    places = jnp.stack([core, head])
-    gateup_pieces, dy_sent, x_mine = lax.optimization_barrier((gateup_pieces, dy_low, x_mine))
+    places = jnp.stack([core, head] + [(grp - steps) % 4 for steps in range(4)])
+    output_pieces = from_grp(output_half)
+    gateup_pieces, w_dn, w_unit, output_pieces, numbers, places, gain_one, taps, x_mine = lax.optimization_barrier(
+        (gateup_pieces, w_dn, w_unit, output_pieces, numbers, places, gain_one, taps, x_mine)
+    )
     x_theirs = other_core(x_mine)
-    dy_pieces = from_grp(dy_sent)
-    gateup_pieces = gateup_pieces[:1] + [along_grp(gateup_pieces[steps], steps) for steps in (1, 2, 3)]
-
+    gateup_pieces = lax.all_to_all(gateup_pieces, "grp", 0, 0)
     (
         hidden_one, mixed_in, outgate, conv, columns, inverse, from_state, updates, scores, moves, states, heads_out,
         squares,
-    ) = forward_call(numbers, x_mine, x_theirs, gain_one, w_unit, taps)
+    ) = forward_call(numbers, places, x_mine, x_theirs, gain_one, w_unit, taps)
+    heads_out, squares, gateup_pieces = lax.optimization_barrier((heads_out, squares, gateup_pieces))
+    squares_theirs = other_core(squares)
+    gated = gate_call(heads_out, outgate, squares, squares_theirs, head_half)
+
+    dy_low, output_pieces, gated = lax.optimization_barrier((dy_low, output_pieces, gated))
+    gated_tokens = lax.all_to_all(gated.reshape(32, 64, 128), "ctx", 0, 0)
+    dy_mine = jnp.concatenate(from_grp(dy_low), axis=0)
+    output_mine = jnp.concatenate(output_pieces, axis=0)
     output_theirs = other_core(output_mine)
-    unit_at = head // 2 * 256 + core * 128
-    output_unit = jnp.where(
-        head % 2 == core,
-        lax.dynamic_slice_in_dim(output_mine, unit_at, 128, axis=0),
-        lax.dynamic_slice_in_dim(output_theirs, unit_at, 128, axis=0),
-    )
-    squares_theirs = other_core(squares)
-    heads_out, gateup_pieces, dy_pieces = lax.optimization_barrier((heads_out, gateup_pieces, dy_pieces))
-    gated = gate_call(heads_out, outgate, squares, squares_theirs, head_half)
-
-    gated_tokens = lax.all_to_all(gated.reshape(32, 64, 128), "ctx", 0, 0)
+    gated_tokens, dy_mine = lax.optimization_barrier((gated_tokens, dy_mine))
+    dy_theirs = other_core(dy_mine)
     middle, hidden_two = middle_call(places, gated_tokens, block_input, output_mine, output_theirs, gain_two)
     r_two = lax.rsqrt(jnp.mean(middle * middle, axis=-1, keepdims=True) + epsilon)
-    gateup_pieces, dy_pieces = lax.optimization_barrier((gateup_pieces, dy_pieces, hidden_two))[:2]
-    w_gu = in_grp_order(gateup_pieces, grp).reshape(1024, 768)
-    dy_wide = jnp.concatenate(dy_pieces, axis=0)
-    dy_wide = jnp.concatenate([dy_wide, other_core(dy_wide)], axis=0)
-    two_wide = to_wide(hidden_two)
-    gateup = mm(two_wide, w_gu)
-    gate, up = gateup[:, :384], gateup[:, 384:]
-    sig = jax.nn.sigmoid(gate)
-    silu_gate = gate * sig
-    swi = (silu_gate * up).astype(bf16)
-    dswi = mm_t(dy_wide, w_dn)
-    dgate = dswi * up * (sig * (1.0 + gate * (1.0 - sig)))
-    dgateup = jnp.concatenate([dgate, dswi * silu_gate], axis=1).astype(bf16)
-    g_ff = ff_weights_call(two_wide, dgateup, swi, dy_wide)
-    dhidden_two = from_wide(dgateup, w_gu, NT, f32)
+    two_mine, two_theirs = to_wide(hidden_two)
+    w_gu = gateup_pieces.reshape(1024, 768)
+    swi_theirs, grads_theirs, part_theirs = ff_call(two_theirs, dy_theirs, w_gu, w_dn)
+    by_grp = exchange_grp(gated_tokens.reshape(2, 4, 2, 2, 64, 128).transpose(1, 0, 2, 3, 4, 5), grp)
+    swi_mine, grads_mine, part_low, part_own = ff_sum_call(two_mine, dy_mine, w_gu, w_dn, other_core(part_theirs))
+    part_low, part_own, swi_mine, grads_mine, by_grp = lax.optimization_barrier(
+        (part_low, part_own, swi_mine, grads_mine, by_grp)
+    )
+    g_ff = ff_weights_call(
+        two_mine, two_theirs, grads_mine, grads_theirs, swi_mine, swi_theirs, dy_mine, dy_theirs
+    )
+    dhidden_two = over_grp(part_own, part_low.reshape(4, 128, 1024))
     scaled = dhidden_two * gain_two
     dmiddle = dy + r_two * scaled - middle * r_two**3 * jnp.mean(scaled * middle, axis=-1, keepdims=True)
     dmix = dmiddle.astype(bf16)
     dmix, g_ff = lax.optimization_barrier((dmix, g_ff))
-    dmix_mine, dmix_theirs = to_units(dmix.reshape(2, 64, 1024))
-
-    d_normed, d_outgate, inner, g_early, g_head = gate_back_call(
-        numbers, dmix_mine, dmix_theirs, output_unit, heads_out, outgate, squares, squares_theirs, head_half, gated,
-        hidden_one,
+    g_ff = sum_chips(g_ff)
+    d_gated = d_gated_call(places, dmix, output_mine, output_theirs)
+    dmix, d_gated = lax.optimization_barrier((dmix, d_gated))
+    d_gated = lax.all_to_all(d_gated, "ctx", 0, 0)
+
+    dmix_pieces, d_gated = lax.optimization_barrier((from_grp(dmix), d_gated))
+    g_output = output_weights_call(*by_grp, *dmix_pieces)
+    d_gated, g_output = lax.optimization_barrier((d_gated, g_output))
+    g_output = over_chips(g_output)
+
+    d_normed, d_outgate, inner, g_head = gate_back_call(
+        d_gated.reshape(2048, 128), heads_out, outgate, squares, squares_theirs, head_half
     )
     inner_theirs = other_core(inner)
-    g_ff, g_early, inner, d_normed = lax.optimization_barrier((g_ff, g_early, inner, d_normed))
-    g_ff = over_chips(g_ff)
-    early_mine, *early_others = exchange_grp(g_early.astype(bf16), grp)
-    early_mine = lax.dynamic_index_in_dim(g_early, grp, 0, False)
-    keep, give, g_unit, g_rates, g_taps, g_sums = backward_call(
-        numbers, taps, conv, columns, inverse, from_state, updates, scores, moves, states, mixed_in,
-        d_normed, heads_out, squares, squares_theirs, inner, inner_theirs, hidden_one, d_outgate, w_unit,
+    keep, give, g_unit, g_unit_low, g_rates, g_taps, g_sums = backward_call(
+        numbers, places, taps, conv, columns, inverse, from_state, updates, scores, moves, states, mixed_in,
+        d_normed, heads_out, squares, squares_theirs, inner, inner_theirs, hidden_one, d_outgate, *w_unit,
     )
 
+    give, g_output = lax.optimization_barrier((give, g_output))
     give_theirs = other_core(give)
     d_sent = (keep + give_theirs.astype(f32)).astype(bf16)
+    g_ff, g_output, g_unit_low, d_sent = lax.optimization_barrier((g_ff, g_output, g_unit_low, d_sent))
     d_tokens = over_chips(d_sent)
-
+    g_unit_pieces = exchange_grp(g_unit_low.reshape(4, 256, 512), grp)[1:]
+    g_output = g_output.astype(f32).sum(axis=0).reshape(2, 128, 128)
+    g_output_theirs = other_core(lax.dynamic_index_in_dim(g_output, 1 - core, 0, False).astype(bf16))
+    g_output = lax.dynamic_index_in_dim(g_output, core, 0, False) + g_output_theirs.astype(f32)
+    g_gu = exchange_grp(g_ff[:384].astype(bf16).reshape(4, 96, 128), grp)
+    early = jnp.concatenate(g_gu + [g_ff[384:].astype(bf16), g_output.astype(bf16)], axis=0)
     g_rates = g_rates[:2].reshape(2, 4, 2, 128).transpose(1, 0, 2, 3).reshape(4, 4, 128)
     shared = jnp.concatenate(
         [g_taps[:4].reshape(12, 128), g_head[:1], g_sums[:2], jnp.zeros((5, 128), f32)], axis=0
     )
     g_small = jnp.concatenate([jnp.broadcast_to(shared, (4, 20, 128)), g_rates], axis=1)
-
-    g_ff, early_others, give_theirs = lax.optimization_barrier((g_ff, early_others, give_theirs))
-    g_ff = g_ff.astype(f32).sum(axis=0).astype(bf16)
-    g_gu = in_grp_order(exchange_grp(g_ff[:384].reshape(4, 96, 128), grp), grp).reshape(384, 128)
-    g_early = early_mine + sum(other.astype(f32) for other in early_others)
-    g_early = jnp.concatenate(
-        [g_early[:256].reshape(2, 128, 128), g_early[256:].reshape(8, 2, 16, 128).transpose(1, 0, 2, 3).reshape(2, 128, 128)],
-        axis=1,
-    )
-    early_mine = lax.dynamic_index_in_dim(g_early, seq, 0, False)
-    early_given = lax.dynamic_index_in_dim(g_early, 1 - seq, 0, False).astype(bf16)
-    early_mine = (early_mine + other_seq(early_given).astype(f32)).astype(bf16)
-    early_output = lax.ppermute(early_mine[128:], ("grp", "ctx"), OUTPUT_MOVES)
-    early = jnp.concatenate([g_gu, g_ff[384:], early_mine[:128], early_output], axis=0)
+    g_small = exchange_grp(g_small, grp)
+    g_unit_pieces, g_small, d_tokens = lax.optimization_barrier((g_unit_pieces, g_small, d_tokens))
     early_mine = lax.all_gather(early, "ctx", axis_index_groups=CHIPS)
     early_theirs = other_core(early_mine)
-    grad_gateup, grad_down, mlp_sums = ff_grads_call(
-        numbers, early_mine, early_theirs, w_gateup, jnp.broadcast_to(mlp_gain[:, None], (256, 128))
+    grad_gateup, grad_down, grad_output, mlp_sums = ff_grads_call(
+        numbers, places, early_mine, early_theirs, w_gateup, jnp.broadcast_to(mlp_gain[:, None], (256, 128))
     )
-    grad_outgate, grad_output, gate_sums = out_grads_call(
-        numbers, early_mine[:, 640:], early_theirs[:, 640:], w_outgate
-    )
-
-    swi, g_unit, g_small = lax.optimization_barrier((swi, g_unit, g_small, d_sent))[:3]
-    g_small = sum(exchange_grp(g_small, grp))
-    g_sum = sum_grp(g_unit.reshape(4, 256, 384), grp).reshape(2, 128, 384)
+
+    g_small = sum(g_small)
+    g_sum = lax.dynamic_index_in_dim(g_unit.reshape(4, 256, 512), grp, 0, False)
+    for other in g_unit_pieces:
+        g_sum = g_sum + other.astype(f32)
+    g_sum = g_sum.reshape(2, 128, 512)
 
     dhidden_one = d_tokens.astype(f32)
     dhidden_one = dhidden_one.reshape(2, 8, 64, 1024).sum(axis=1).reshape(128, 1024)
@@ -985,16 +1048,20 @@
     qk_mine = lax.dynamic_index_in_dim(halves, core, 0, False)
     qk_given = lax.dynamic_index_in_dim(halves, 1 - core, 0, False).astype(bf16)
     qk_mine = qk_mine + other_core(qk_given).astype(f32)
-    late = jnp.concatenate([qk_mine[:, :128], qk_mine[:, 128:], mine[:, 256:]], axis=0).astype(bf16)
+    late = [qk_mine[:, :128], qk_mine[:, 128:], mine[:, 256:384], mine[:, 384:]]
+    late = jnp.concatenate(late, axis=0).astype(bf16)
     small_high = lax.optimization_barrier(g_small.astype(bf16))
     small_low = (g_small - small_high.astype(f32)).astype(bf16)
     late = jnp.concatenate([late, small_high, small_low], axis=0)
-    late, d_tokens = lax.optimization_barrier((late, d_tokens))
+    late, swi_mine, swi_theirs = lax.optimization_barrier((late, swi_mine, swi_theirs))
     late_mine = over_chips(jnp.broadcast_to(late, (16,) + late.shape))
+    block_out = middle + over_grp(*over_cores(mm(swi_mine, w_dn), mm(swi_theirs, w_dn), bf16))
+    block_output = (block_out.reshape(2, 64, 1024) * valid).astype(bf16)
+    late_mine, block_output, input_grad = lax.optimization_barrier((late_mine, block_output, input_grad))
     late_theirs = other_core(late_mine)
-    grad_mixer, mixer_sums = mixer_grads_call(numbers, late_mine, late_theirs, w_mixer)
-    small_one = (late_mine[:, 256:280].astype(f32) + late_mine[:, 280:].astype(f32)).reshape(2, 8, 24, 128)
-    small_two = (late_theirs[:, 256:280].astype(f32) + late_theirs[:, 280:].astype(f32)).reshape(2, 8, 24, 128)
+    grad_mixer, grad_outgate, mixer_sums = mixer_grads_call(numbers, late_mine, late_theirs, w_mixer, w_outgate)
+    small_one = (late_mine[:, 384:408].astype(f32) + late_mine[:, 408:].astype(f32)).reshape(2, 8, 24, 128)
+    small_two = (late_theirs[:, 384:408].astype(f32) + late_theirs[:, 408:].astype(f32)).reshape(2, 8, 24, 128)
     small_one, small_two = small_one.sum(axis=0), small_two.sum(axis=0)
     both = small_one + small_two
     g_low = jnp.where(core == 0, small_one, small_two)
@@ -1011,12 +1078,8 @@
     grad_rates = both[:, 20:].reshape(8, 2, 256).transpose(1, 0, 2).reshape(16, 256).T
     grad_in_gain = (
         mixer_sums[:, 0]
-        + gate_sums[:, 0]
         + jnp.sum(grad_rates * w_rates.astype(f32), axis=1)
     ) / in_gain.astype(f32)
-
-    block_out = middle + from_wide(swi, w_dn, NN, bf16)
-    block_output = (block_out.reshape(2, 64, 1024) * valid).astype(bf16)
 
     return (
         block_output,

time: 448 us -> 431 us (0.962)
  blocking collectives: 30.4 us -> 0 us
  waiting for transfers between devices: 100 us -> 116 us
  Pallas kernels: 108 us -> 120 us
  matrix products: 8.74 us -> 3.68 us
    ppermute x33, waiting for transfers between devices: 49.8 us -> 82.2 us  [along_grp(): lax.ppermute(value, 'grp', [(at, (at + steps) % 4) for at in range(4)])]
    all_to_all x1 -> x0, blocking collectives: 30.4 us -> none  [over_chips(): return lax.all_to_all(value, 'ctx', 0, 0, axis_index_groups=CHIPS)]
    ppermute x33, starting transfers between devices: 52.5 us -> 37.7 us  [along_grp(): lax.ppermute(value, 'grp', [(at, (at + steps) % 4) for at in range(4)])]
    all_to_all x0 -> x2, starting transfers between devices: none -> 13.1 us  [the longest x1 8.27 us: body(): d_gated = lax.all_to_all(d_gated, 'ctx', 0, 0)]
    all_to_all x1, waiting for transfers between devices: 11.4 us -> 0.01 us  [body(): gated_tokens = lax.all_to_all(gated.reshape(32, 64, 128), 'ctx', 0, 0)]
    ppermute x2 -> x1, waiting for transfers between devices: 13.1 us -> 2.35 us  [other_seq(): return lax.ppermute(value, 'ctx', OTHER_SEQ)]
    pallas_call x3 -> x6, Pallas kernels: 20.8 us -> 30 us  [the longest x1 7.74 us: ff_weights_call(): pl.pallas_call(ff_weights_kernel, grid=(4,), in_specs=[columns] * 2 + [wh...]
    slice x9 -> x4, local copies, waits for them, and re-layouts: 6.75 us -> 1.37 us  [the longest x2 1.26 us: over_grp(): total = total + along_grp(low[steps], -steps).astype(f32)]
  transfers between devices with their start and end apart: 56 -> 56, of which waited for: 25 -> 25; matrix products, arithmetic and copies ran while one was open for 12% -> 9% of each run, Pallas kernels for 19% -> 23%
where the time goes in v3:
time: 431 us; the launch traced here: 425 us
  Pallas kernels  120 us (28%)
  waiting for transfers between devices  116 us (27%)
  starting transfers between devices  106 us (25%)
  local copies, waits for them, and re-layouts  38.4 us (9%)
  other arithmetic  24.5 us (6%)
  between operations  16.5 us (4%)
    ppermute x33, waiting for transfers between devices, along_grp(): lax.ppermute(value, 'grp', [(at, (at + steps) % 4) for at in range(4)])  82.2 us
    ppermute x33, starting transfers between devices, along_grp(): lax.ppermute(value, 'grp', [(at, (at + steps) % 4) for at in range(4)])  37.7 us
    pallas_call x1, Pallas kernels, backward_call(): pl.pallas_call(backward_kernel, grid=(steps,), in_specs=[pl.BlockSpec(mem...  37.2 us
    pallas_call x1, Pallas kernels, forward_call(): pl.pallas_call(forward_kernel, grid=(steps,), in_specs=[pl.BlockSpec(memo...  30.6 us
    all_to_all x4, starting transfers between devices, over_chips(): return lax.all_to_all(value, 'ctx', 0, 0, axis_index_groups=CHIPS)  24.8 us
    ppermute x13, starting transfers between devices, other_core(): return lax.ppermute(value, 'ctx', OTHER_CORE)  23.8 us
    unnamed x110, local copies, waits for them, and re-layouts  18.6 us
    all_to_all x4, waiting for transfers between devices, over_chips(): return lax.all_to_all(value, 'ctx', 0, 0, axis_index_groups=CHIPS)  12.9 us
  transfers between devices with their start and end apart: 56, of which 25 were waited for; matrix products, arithmetic and copies ran while one was open for 9% of the time, Pallas kernels for 23%

profile of v3, /device:TPU:1, one launch (start us, length us, event | category | flops | bytes accessed | tf_op | source)
XLA Modules:
  0.0 424.5 jit_solution(4331737334194077875)
XLA Ops:
  7.3 2.6 broadcast_in_dim.14
  14.4 3.3 collective-permute-start.1
  21.5 6.8 %all-to-all-start = ((bf16[16,64,1024]{2,1,0:T(8,128)(2,1)}), bf16[16,64,1024]{2,1,0:T(8,128)(2,1)}, u32[]{:S(2)}, u32[]{:S(2)}) async-start(bf16[16,64,1024]{2,1,0:T(8,128)(2,1)} %bitcast.187), calls=%async_computation | async-start | bytes 4194304 | tf_op jit(solution)/shard_map/all_to_all | solution.py:841
  32.7 2.7 pad_maximum_fusion
  42.2 12.2 %collective-permute-done.4 = bf16[256,1024]{1,0:T(8,128)(2,1)} collective-permute-done((bf16[256,1024]{1,0:T(8,128)(2,1)}, bf16[256,1024]{1,0:T(8,128)(2,1)}, u32[]{:S(2)}, u32[]{:S(2)}) %collective-permute-start.4) | collective-permute-done | bytes 524320 | tf_op jit(solution)/shard_map/ppermute | solution.py:809
  55.3 4.6 %collective-permute-start.6 = (bf16[16,64,1024]{2,1,0:T(8,128)(2,1)}, bf16[16,64,1024]{2,1,0:T(8,128)(2,1)}, u32[]{:S(2)}, u32[]{:S(2)}) collective-permute-start(bf16[16,64,1024]{2,1,0:T(8,128)(2,1)} %all-to-all-done.mine), channel_id=1, source_target_pairs={{0,1},{1,0},{2,3},{3,2},{4,5},{5,4},{6,7},{7,6},{8,9},{9,8},{10,11... | collective-permute-start | bytes 6291464 | tf_op jit(solution)/shard_map/ppermute | solution.py:801
  61.1 4.9 %all-to-all-start.1 = ((bf16[4,256,768]{2,1,0:T(8,128)(2,1)}), bf16[4,256,768]{2,1,0:T(8,128)(2,1)}, u32[]{:S(2)}, u32[]{:S(2)}) async-start(bf16[4,256,768]{2,1,0:T(8,128)(2,1)} %pad_maximum_fusion), calls=%async_computation.1 | async-start | bytes 3145728 | tf_op jit(solution)/shard_map/all_to_all | solution.py:954
  66.0 30.6 %delta_forward.1 = (bf16[2048,1024]{1,0:T(8,128)(2,1)}, bf16[2048,384]{1,0:T(8,128)(2,1)}, f32[2048,128]{1,0:T(8,128)}, f32[2048,384]{1,0:T(8,128)}, f32[2048,12...) custom-call(f32[4]{0:T(128)S(1)} %pad_maximum_fusion.13.numbers, ...), custom_call_target="tpu_custom_call" | custom-call | flops 30000001024 | bytes 90000000 | tf_op jit(solution)/shard_map/delta_forward/pallas_call | solution.py:204
  99.1 3.5 gate.1
  109.3 3.9 all-to-all-start.2
  113.3 3.0 collective-permute-start.10
  117.4 9.8 %collective-permute-done.10 = bf16[128,1024]{1,0:T(8,128)(2,1)S(1)} collective-permute-done((bf16[128,1024]{1,0:T(8,128)(2,1)S(1)}, bf16[128,1024]{1,0:T(8,128)(2,1)S(1)}, u32[]{:S(2)}, u32[]{:S(2)}) %collective-permute-start.10) | collective-permute-done | bytes 262176 | tf_op jit(solution)/shard_map/ppermute | solution.py:809
  127.2 4.4 %collective-permute-done.8 = bf16[128,1024]{1,0:T(8,128)(2,1)S(1)} collective-permute-done((bf16[128,1024]{1,0:T(8,128)(2,1)S(1)}, bf16[128,1024]{1,0:T(8,128)(2,1)S(1)}, u32[]{:S(2)}, u32[]{:S(2)}) %collective-permute-start.8) | collective-permute-done | bytes 262176 | tf_op jit(solution)/shard_map/ppermute | solution.py:809
  132.7 4.0 middle.1
  140.6 10.3 %collective-permute-done.12 = bf16[128,1024]{1,0:T(8,128)(2,1)S(1)} collective-permute-done((bf16[128,1024]{1,0:T(8,128)(2,1)S(1)}, bf16[128,1024]{1,0:T(8,128)(2,1)S(1)}, u32[]{:S(2)}, u32[]{:S(2)}) %collective-permute-start.12) | collective-permute-done | bytes 262176 | tf_op jit(solution)/shard_map/ppermute | solution.py:809
  156.5 6.1 %ff.1 = (bf16[512,384]{1,0:T(8,128)(2,1)S(1)}, bf16[512,768]{1,0:T(8,128)(2,1)S(1)}, f32[512,1024]{1,0:T(8,128)}) custom-call(bf16[512,1024]{1,0:T(8,128)(2,1)} %copy-done.41, bf16[512,1024]{1,0:T(8,128)(2,1)} %copy-done.40, bf16[1024,768]{1,0:T(8,128)(2,1)} %bitcast.19.weight, bf16[384,1024]{1,0:T(8,128)(2,1)S(1)} %concatenate.59.down), custom_call_target="tpu_custom_call" | custom-call | flops 5000000000 | bytes 15000000 | tf_op jit(solution)/shard_map/ff/pallas_call | solution.py:551
  164.1 3.5 collective-permute-start.19
  168.0 6.6 %ff_sum.1 = (bf16[512,384]{1,0:T(8,128)(2,1)S(1)}, bf16[512,768]{1,0:T(8,128)(2,1)S(1)}, bf16[512,1024]{1,0:T(8,128)(2,1)}, f32[128,1024]{1,0:T(8,128)S(1)}) custom-call(bf16[512,1024]{1,0:T(8,128)(2,1)} %copy-done.30, bf16[512,1024]{1,0:T(8,128)(2,1)} %pad_maximum_fusion.1.dy.dy_0, bf16[1024,768]{1,0:T(8,128)(2,1)} %bitcast.19.weight, ...), custom_call_target="tpu_custom_call" | custom-call | flops 5000000000 | bytes 15000000 | tf_op jit(solution)/shard_map/ff_sum/pallas_call | solution.py:577
  177.0 2.5 collective-permute-start.22
  179.5 7.7 %ff_weights.1 = f32[16,640,128]{2,1,0:T(8,128)} custom-call(bf16[512,1024]{1,0:T(8,128)(2,1)} %copy-done.30, bf16[512,1024]{1,0:T(8,128)(2,1)} %copy-done.41, bf16[512,768]{1,0:T(8,128)(2,1)S(1)} %get-tuple-element.172.grads_0, bf16[512,768]{1,0:T(8,128)(2,1)} %copy-done.16, bf16[512,384]{1,0:T(8,128)(2,1)S(1)} %get-tuple-element.215.swi_0, ...), custom_call_target="tpu_custom_call" | custom-call | flops 7000000000 | bytes 21000000 | tf_op jit(solution)/shard_map/ff_weights/pallas_call | solution.py:662
  187.3 3.9 collective-permute-done.22
  192.6 4.7 %d_gated.1 = f32[32,64,128]{2,1,0:T(8,128)} custom-call(s32[6]{0:T(128)S(1)} %stack.84.places.numbers, bf16[128,1024]{1,0:T(8,128)(2,1)S(1)} %get-tuple-element.184.grads.grads_0, bf16[1024,1024]{1,0:T(8,128)(2,1)} %constant_dynamic-update-slice_fusion.mine, bf16[1024,1024]{1,0:T(8,128)(2,1)} %collective-permute-done.11.theirs), custom_call_target="tpu_custom_call" | custom-call | flops 3000000000 | bytes 9000000 | tf_op jit(solution)/shard_map/d_gated/pallas_call | solution.py:499
  197.3 8.3 %all-to-all-start.3 = ((f32[32,64,128]{2,1,0:T(8,128)}), f32[32,64,128]{2,1,0:T(8,128)}, u32[]{:S(2)}, u32[]{:S(2)}) async-start(f32[32,64,128]{2,1,0:T(8,128)} %d_gated.1), calls=%async_computation.3 | async-start | bytes 2097152 | tf_op jit(solution)/shard_map/all_to_all | solution.py:991
  206.1 2.8 collective-permute-start.25
  208.9 5.6 %collective-permute-done.24.grads_1 = bf16[128,1024]{1,0:T(8,128)(2,1)S(1)} collective-permute-done((bf16[128,1024]{1,0:T(8,128)(2,1)S(1)}, bf16[128,1024]{1,0:T(8,128)(2,1)S(1)}, u32[]{:S(2)}, u32[]{:S(2)}) %collective-permute-start.24) | collective-permute-done | bytes 262176 | tf_op jit(solution)/shard_map/ppermute | solution.py:809
  214.5 6.2 %collective-permute-done.25.grads_2 = bf16[128,1024]{1,0:T(8,128)(2,1)S(1)} collective-permute-done((bf16[128,1024]{1,0:T(8,128)(2,1)S(1)}, bf16[128,1024]{1,0:T(8,128)(2,1)S(1)}, u32[]{:S(2)}, u32[]{:S(2)}) %collective-permute-start.25) | collective-permute-done | bytes 262176 | tf_op jit(solution)/shard_map/ppermute | solution.py:809
  222.2 3.5 all-to-all-done.3
  230.3 3.1 gate_back.1
  237.1 4.5 %all-to-all-start.4 = ((bf16[16,256,128]{2,1,0:T(8,128)(2,1)}), bf16[16,256,128]{2,1,0:T(8,128)(2,1)}, u32[]{:S(2)}, u32[]{:S(2)}) async-start(bf16[16,256,128]{2,1,0:T(8,128)(2,1)} %output_weights.1), calls=%async_computation.5 | async-start | bytes 2097152 | tf_op jit(solution)/shard_map/all_to_all | solution.py:841
  242.7 37.2 %delta_backward.1 = (f32[16,64,1024]{2,1,0:T(8,128)}, bf16[16,64,1024]{2,1,0:T(8,128)(2,1)}, f32[1024,512]{1,0:T(8,128)}, bf16[1024,512]{1,0:T(8,128)(2,1)}, f32...) custom-call(f32[4]{0:T(128)S(1)} %pad_maximum_fusion.13.numbers, s32[6]{0:T(128)S(1)} %stack.84.places.numbers, ...), custom_call_target="tpu_custom_call" | custom-call | flops 35999997952 | bytes 108000000 | tf_op jit(solution)/shard_map/delta_backward/pallas_call | solution.py:374
  280.0 4.3 %collective-permute-done.28 = bf16[16,64,1024]{2,1,0:T(8,128)(2,1)S(1)} collective-permute-done((bf16[16,64,1024]{2,1,0:T(8,128)(2,1)}, bf16[16,64,1024]{2,1,0:T(8,128)(2,1)S(1)}, u32[]{:S(2)}, u32[]{:S(2)}) %collective-permute-start.28) | collective-permute-done | bytes 2097184 | tf_op jit(solution)/shard_map/ppermute | solution.py:801
  284.3 4.4 %add_convert_fusion = bf16[16,64,1024]{2,1,0:T(8,128)(2,1)} fusion(f32[16,64,1024]{2,1,0:T(8,128)} %get-tuple-element.199, bf16[16,64,1024]{2,1,0:T(8,128)(2,1)S(1)} %collective-permute-done.28), kind=kLoop, calls=%fused_computation.1 | loop fusion | flops 3145728 | bytes 8388608 | tf_op jit(solution)/shard_map/convert_element_type | solution.py:1009
  288.8 6.8 %all-to-all-start.5 = ((bf16[16,64,1024]{2,1,0:T(8,128)(2,1)}), bf16[16,64,1024]{2,1,0:T(8,128)(2,1)}, u32[]{:S(2)}, u32[]{:S(2)}) async-start(bf16[16,64,1024]{2,1,0:T(8,128)(2,1)} %add_convert_fusion), calls=%async_computation.6 | async-start | bytes 4194304 | tf_op jit(solution)/shard_map/all_to_all | solution.py:841
  296.4 2.8 collective-permute-start.33
  305.2 9.5 %collective-permute-done.42 = bf16[96,128]{1,0:T(8,128)(2,1)S(1)} collective-permute-done((bf16[96,128]{1,0:T(8,128)(2,1)S(1)}, bf16[96,128]{1,0:T(8,128)(2,1)S(1)}, u32[]{:S(2)}, u32[]{:S(2)}) %collective-permute-start.42) | collective-permute-done | bytes 24608 | tf_op jit(solution)/shard_map/ppermute | solution.py:809
  314.7 4.6 %collective-permute-done.43 = bf16[96,128]{1,0:T(8,128)(2,1)S(1)} collective-permute-done((bf16[96,128]{1,0:T(8,128)(2,1)S(1)}, bf16[96,128]{1,0:T(8,128)(2,1)S(1)}, u32[]{:S(2)}, u32[]{:S(2)}) %collective-permute-start.43) | collective-permute-done | bytes 24608 | tf_op jit(solution)/shard_map/ppermute | solution.py:809
  319.3 3.1 collective-permute-done.44
  323.7 3.7 collective-permute-start.45
  338.4 5.3 %collective-permute-start.36 = (bf16[64,256]{1,0:T(8,128)(2,1)S(1)}, bf16[64,256]{1,0:T(8,128)(2,1)S(1)}, u32[]{:S(2)}, u32[]{:S(2)}) collective-permute-start(bf16[64,256]{1,0:T(8,128)(2,1)S(1)} %fusion.21), channel_id=1, source_target_pairs={{0,1},{1,0},{2,3},{3,2},{4,5},{5,4},{6,7},{7,6},{8,9},{9,8},{10,11... | collective-permute-start | bytes 98312 | tf_op jit(solution)/shard_map/ppermute | solution.py:801
  350.4 6.6 %all-to-all-start.6 = ((bf16[16,432,128]{2,1,0:T(8,128)(2,1)}), bf16[16,432,128]{2,1,0:T(8,128)(2,1)}, u32[]{:S(2)}, u32[]{:S(2)}) async-start(bf16[16,432,128]{2,1,0:T(8,128)(2,1)} %broadcast_in_dim.36), calls=%async_computation.7 | async-start | bytes 3538944 | tf_op jit(solution)/shard_map/all_to_all | solution.py:841
  359.3 3.1 collective-permute-start.39
  363.4 4.6 %collective-permute-done.40 = bf16[128,1024]{1,0:T(8,128)(2,1)S(1)} collective-permute-done((bf16[128,1024]{1,0:T(8,128)(2,1)S(1)}, bf16[128,1024]{1,0:T(8,128)(2,1)S(1)}, u32[]{:S(2)}, u32[]{:S(2)}) %collective-permute-start.40) | collective-permute-done | bytes 262176 | tf_op jit(solution)/shard_map/ppermute | solution.py:809
  368.1 6.1 %collective-permute-done.39 = bf16[128,1024]{1,0:T(8,128)(2,1)S(1)} collective-permute-done((bf16[128,1024]{1,0:T(8,128)(2,1)S(1)}, bf16[128,1024]{1,0:T(8,128)(2,1)S(1)}, u32[]{:S(2)}, u32[]{:S(2)}) %collective-permute-start.39) | collective-permute-done | bytes 262176 | tf_op jit(solution)/shard_map/ppermute | solution.py:809
  375.1 12.0 %all-to-all-done.6.mine = bf16[16,432,128]{2,1,0:T(8,128)(2,1)} async-done(((bf16[16,432,128]{2,1,0:T(8,128)(2,1)}), bf16[16,432,128]{2,1,0:T(8,128)(2,1)}, u32[]{:S(2)}, u32[]{:S(2)}) %all-to-all-start.6) | async-done | bytes 1769504 | tf_op jit(solution)/shard_map/all_to_all | solution.py:841
  387.2 3.0 collective-permute-start.41
  390.2 5.4 %all-gather.3.cloned.1.call-done = bf16[12288,128]{1,0:T(8,128)(2,1)} async-done(((bf16[768,128]{1,0:T(8,128)(2,1)}), bf16[12288,128]{1,0:T(8,128)(2,1)}) %all-gather.3.cloned.1.call-update) | async-done | bytes 3145744 | tf_op jit(solution)/shard_map/all_gather | solution.py:1025
  400.4 5.1 %mixer_grads.1 = (f32[256,4096]{1,0:T(8,128)}, f32[256,2048]{1,0:T(8,128)}, f32[256,128]{1,0:T(8,128)S(1)}) custom-call(f32[4]{0:T(128)S(1)} %pad_maximum_fusion.13.numbers, bf16[16,432,128]{2,1,0:T(8,128)(2,1)} %all-to-all-done.6.mine, bf16[16,432,128]{2,1,0:T(8,128)(2,1)} %copy-done.31, bf16[256,4096]{1,0:T(8,128)(2,1)} %weight.2, ...), custom_call_target="tpu_custom_call" | custom-call | flops 4000000000 | bytes 12000000 | tf_op jit(solution)/shard_map/mixer_grads/pallas_call | solution.py:766
  406.9 9.7 %ff_grads.1 = (f32[256,5632]{1,0:T(8,128)}, f32[704,1024]{1,0:T(8,128)}, f32[512,1024]{1,0:T(8,128)}, f32[256,128]{1,0:T(8,128)S(1)}) custom-call(f32[4]{0:T(128)S(1)} %pad_maximum_fusion.13.numbers, s32[6]{0:T(128)S(1)} %stack.84.places.numbers, bf16[16,768,128]{2,1,0:T(8,128)(2,1)} %bitcast.217, bf16[16,768,128]{2,1,0:T(8,128)(2,1)} %collective-permute-done.46.theirs, ...), custom_call_target="tpu_custom_call" | custom-call | flops 8000000000 | bytes 24000000 | tf_op jit(solution)/shard_map/ff_grads/pallas_call | solution.py:716
  (314 shorter events, 95.0 us)
Async XLA Ops:
  11.8 25.9 %collective-permute-start = (bf16[256,640]{1,0:T(8,128)(2,1)S(1)}, bf16[256,640]{1,0:T(8,128)(2,1)S(1)}, u32[]{:S(2)}, u32[]{:S(2)}) collective-permute-start(bf16[256,640]{1,0:T(8,128)(2,1)S(1)} %concatenate.61.weight_0), channel_id=1, source_target_pairs={{0,32},{32,64},{64,96},{96,0},{1,33},{33,65},{65,97},{97,1},{2,34}... | collective-permute-start | bytes 983048 | tf_op jit(solution)/shard_map/ppermute | solution.py:809
  14.4 23.2 %collective-permute-start.1 = (bf16[256,640]{1,0:T(8,128)(2,1)S(1)}, bf16[256,640]{1,0:T(8,128)(2,1)S(1)}, u32[]{:S(2)}, u32[]{:S(2)}) collective-permute-start(bf16[256,640]{1,0:T(8,128)(2,1)S(1)} %concatenate.61.weight_0), channel_id=1, source_target_pairs={{0,64},{32,96},{64,0},{96,32},{1,65},{33,97},{65,1},{97,33},{2,66}... | collective-permute-start | bytes 983048 | tf_op jit(solution)/shard_map/ppermute | solution.py:809
  17.7 17.7 %collective-permute-start.2 = (bf16[256,640]{1,0:T(8,128)(2,1)S(1)}, bf16[256,640]{1,0:T(8,128)(2,1)S(1)}, u32[]{:S(2)}, u32[]{:S(2)}) collective-permute-start(bf16[256,640]{1,0:T(8,128)(2,1)S(1)} %concatenate.61.weight_0), channel_id=1, source_target_pairs={{0,96},{32,0},{64,32},{96,64},{1,97},{33,1},{65,33},{97,65},{2,98}... | collective-permute-start | bytes 983048 | tf_op jit(solution)/shard_map/ppermute | solution.py:809
  20.3 22.0 %collective-permute-start.3 = (bf16[256,1024]{1,0:T(8,128)(2,1)}, bf16[256,1024]{1,0:T(8,128)(2,1)}, u32[]{:S(2)}, u32[]{:S(2)}) collective-permute-start(bf16[256,1024]{1,0:T(8,128)(2,1)} %constant_dynamic-slice_fusion.7), channel_id=1, source_target_pairs={{0,32},{32,64},{64,96},{96,0},{1,33},{33,65},{65,97},{97,1},{2,34}... | collective-permute-start | bytes 1572872 | tf_op jit(solution)/shard_map/ppermute | solution.py:809
  21.0 33.4 %collective-permute-start.4 = (bf16[256,1024]{1,0:T(8,128)(2,1)}, bf16[256,1024]{1,0:T(8,128)(2,1)}, u32[]{:S(2)}, u32[]{:S(2)}) collective-permute-start(bf16[256,1024]{1,0:T(8,128)(2,1)} %constant_dynamic-slice_fusion.7), channel_id=1, source_target_pairs={{0,64},{32,96},{64,0},{96,32},{1,65},{33,97},{65,1},{97,33},{2,66}... | collective-permute-start | bytes 1572872 | tf_op jit(solution)/shard_map/ppermute | solution.py:809
  21.5 33.8 %all-to-all-start = ((bf16[16,64,1024]{2,1,0:T(8,128)(2,1)}), bf16[16,64,1024]{2,1,0:T(8,128)(2,1)}, u32[]{:S(2)}, u32[]{:S(2)}) async-start(bf16[16,64,1024]{2,1,0:T(8,128)(2,1)} %bitcast.187), calls=%async_computation | async-start | bytes 4194304 | tf_op jit(solution)/shard_map/all_to_all | solution.py:841
  35.4 19.0 %collective-permute-start.5 = (bf16[256,1024]{1,0:T(8,128)(2,1)}, bf16[256,1024]{1,0:T(8,128)(2,1)S(1)}, u32[]{:S(2)}, u32[]{:S(2)}) collective-permute-start(bf16[256,1024]{1,0:T(8,128)(2,1)} %constant_dynamic-slice_fusion.7), channel_id=1, source_target_pairs={{0,96},{32,0},{64,32},{96,64},{1,97},{33,1},{65,33},{97,65},{2,98}... | collective-permute-start | bytes 1572872 | tf_op jit(solution)/shard_map/ppermute | solution.py:809
  55.3 10.7 %collective-permute-start.6 = (bf16[16,64,1024]{2,1,0:T(8,128)(2,1)}, bf16[16,64,1024]{2,1,0:T(8,128)(2,1)}, u32[]{:S(2)}, u32[]{:S(2)}) collective-permute-start(bf16[16,64,1024]{2,1,0:T(8,128)(2,1)} %all-to-all-done.mine), channel_id=1, source_target_pairs={{0,1},{1,0},{2,3},{3,2},{4,5},{5,4},{6,7},{7,6},{8,9},{9,8},{10,11... | collective-permute-start | bytes 6291464 | tf_op jit(solution)/shard_map/ppermute | solution.py:801
  61.1 35.5 %all-to-all-start.1 = ((bf16[4,256,768]{2,1,0:T(8,128)(2,1)}), bf16[4,256,768]{2,1,0:T(8,128)(2,1)}, u32[]{:S(2)}, u32[]{:S(2)}) async-start(bf16[4,256,768]{2,1,0:T(8,128)(2,1)} %pad_maximum_fusion), calls=%async_computation.1 | async-start | bytes 3145728 | tf_op jit(solution)/shard_map/all_to_all | solution.py:954
  109.1 23.5 %collective-permute-start.11 = (bf16[1024,1024]{1,0:T(8,128)(2,1)}, bf16[1024,1024]{1,0:T(8,128)(2,1)}, u32[]{:S(2)}, u32[]{:S(2)}) collective-permute-start(bf16[1024,1024]{1,0:T(8,128)(2,1)} %constant_dynamic-update-slice_fusion.mine), channel_id=1, source_target_pairs={{0,1},{1,0},{2,3},{3,2},{4,5},{5,4},{6,7},{7,6},{8,9},{9,8},{10,11... | collective-permute-start | bytes 6291464 | tf_op jit(solution)/shard_map/ppermute | solution.py:801
  109.3 23.4 %all-to-all-start.2 = ((bf16[32,64,128]{2,1,0:T(8,128)(2,1)}), bf16[32,64,128]{2,1,0:T(8,128)(2,1)S(1)}, u32[]{:S(2)}, u32[]{:S(2)}) async-start(bf16[32,64,128]{2,1,0:T(8,128)(2,1)} %bitcast.18), calls=%async_computation.2 | async-start | bytes 1048576 | tf_op jit(solution)/shard_map/all_to_all | solution.py:964
  113.2 175.6 %reduce-scatter.2.cloned.1.call-start = ((), (), s32[]{:S(2)}) async-start(), calls=%async_computation.8 | async-start | bytes 5570560 | tf_op jit(solution)/shard_map/reduce_scatter | solution.py:837
  113.3 13.9 %collective-permute-start.10 = (bf16[128,1024]{1,0:T(8,128)(2,1)S(1)}, bf16[128,1024]{1,0:T(8,128)(2,1)S(1)}, u32[]{:S(2)}, u32[]{:S(2)}) collective-permute-start(bf16[128,1024]{1,0:T(8,128)(2,1)S(1)} %bitcast_convert_fusion), channel_id=1, source_target_pairs={{0,96},{32,0},{64,32},{96,64},{1,97},{33,1},{65,33},{97,65},{2,98}... | collective-permute-start | bytes 786440 | tf_op jit(solution)/shard_map/ppermute | solution.py:809
  116.3 11.0 %collective-permute-start.9 = (bf16[128,1024]{1,0:T(8,128)(2,1)S(1)}, bf16[128,1024]{1,0:T(8,128)(2,1)S(1)}, u32[]{:S(2)}, u32[]{:S(2)}) collective-permute-start(bf16[128,1024]{1,0:T(8,128)(2,1)S(1)} %bitcast_convert_fusion), channel_id=1, source_target_pairs={{0,64},{32,96},{64,0},{96,32},{1,65},{33,97},{65,1},{97,33},{2,66}... | collective-permute-start | bytes 786440 | tf_op jit(solution)/shard_map/ppermute | solution.py:809
  117.0 14.6 %collective-permute-start.8 = (bf16[128,1024]{1,0:T(8,128)(2,1)S(1)}, bf16[128,1024]{1,0:T(8,128)(2,1)S(1)}, u32[]{:S(2)}, u32[]{:S(2)}) collective-permute-start(bf16[128,1024]{1,0:T(8,128)(2,1)S(1)} %bitcast_convert_fusion), channel_id=1, source_target_pairs={{0,32},{32,64},{64,96},{96,0},{1,33},{33,65},{65,97},{97,1},{2,34}... | collective-permute-start | bytes 786440 | tf_op jit(solution)/shard_map/ppermute | solution.py:809
  136.7 14.3 %collective-permute-start.12 = (bf16[128,1024]{1,0:T(8,128)(2,1)S(1)}, bf16[128,1024]{1,0:T(8,128)(2,1)S(1)}, u32[]{:S(2)}, u32[]{:S(2)}) collective-permute-start(bf16[128,1024]{1,0:T(8,128)(2,1)S(1)} %get-tuple-element.161), channel_id=1, source_target_pairs={{0,32},{32,64},{64,96},{96,0},{1,33},{33,65},{65,97},{97,1},{2,34}... | collective-permute-start | bytes 786440 | tf_op jit(solution)/shard_map/ppermute | solution.py:809
  136.7 14.2 %collective-permute-start.13 = (bf16[128,1024]{1,0:T(8,128)(2,1)S(1)}, bf16[128,1024]{1,0:T(8,128)(2,1)S(1)}, u32[]{:S(2)}, u32[]{:S(2)}) collective-permute-start(bf16[128,1024]{1,0:T(8,128)(2,1)S(1)} %get-tuple-element.161), channel_id=1, source_target_pairs={{0,64},{32,96},{64,0},{96,32},{1,65},{33,97},{65,1},{97,33},{2,66}... | collective-permute-start | bytes 786440 | tf_op jit(solution)/shard_map/ppermute | solution.py:809
  137.5 15.6 %collective-permute-start.16 = (bf16[512,1024]{1,0:T(8,128)(2,1)S(1)}, bf16[512,1024]{1,0:T(8,128)(2,1)S(1)}, u32[]{:S(2)}, u32[]{:S(2)}) collective-permute-start(bf16[512,1024]{1,0:T(8,128)(2,1)S(1)} %copy-done.22), channel_id=1, source_target_pairs={{0,1},{1,0},{2,3},{3,2},{4,5},{5,4},{6,7},{7,6},{8,9},{9,8},{10,11... | collective-permute-start | bytes 3145736 | tf_op jit(solution)/shard_map/ppermute | solution.py:801
  139.3 12.1 %collective-permute-start.14 = (bf16[128,1024]{1,0:T(8,128)(2,1)S(1)}, bf16[128,1024]{1,0:T(8,128)(2,1)S(1)}, u32[]{:S(2)}, u32[]{:S(2)}) collective-permute-start(bf16[128,1024]{1,0:T(8,128)(2,1)S(1)} %get-tuple-element.161), channel_id=1, source_target_pairs={{0,96},{32,0},{64,32},{96,64},{1,97},{33,1},{65,33},{97,65},{2,98}... | collective-permute-start | bytes 786440 | tf_op jit(solution)/shard_map/ppermute | solution.py:809
  164.0 10.7 %collective-permute-start.18 = (bf16[2,2,2,64,128]{4,3,2,1,0:T(8,128)(2,1)S(1)}, bf16[2,2,2,64,128]{4,3,2,1,0:T(8,128)(2,1)S(1)}, u32[]{:S(2)}, u32[]{:S(2)}) collective-permute-start(bf16[2,2,2,64,128]{4,3,2,1,0:T(8,128)(2,1)S(1)} %get-tuple-element.264), channel_id=1, source_target_pairs={{0,32},{32,64},{64,96},{96,0},{1,33},{33,65},{65,97},{97,1},{2,34}... | collective-permute-start | bytes 393224 | tf_op jit(solution)/shard_map/ppermute | solution.py:809
  164.1 10.6 %collective-permute-start.19 = (bf16[2,2,2,64,128]{4,3,2,1,0:T(8,128)(2,1)S(1)}, bf16[2,2,2,64,128]{4,3,2,1,0:T(8,128)(2,1)S(1)}, u32[]{:S(2)}, u32[]{:S(2)}) collective-permute-start(bf16[2,2,2,64,128]{4,3,2,1,0:T(8,128)(2,1)S(1)} %get-tuple-element.263), channel_id=1, source_target_pairs={{0,64},{32,96},{64,0},{96,32},{1,65},{33,97},{65,1},{97,33},{2,66}... | collective-permute-start | bytes 393224 | tf_op jit(solution)/shard_map/ppermute | solution.py:809
  167.6 7.1 %collective-permute-start.20 = (bf16[2,2,2,64,128]{4,3,2,1,0:T(8,128)(2,1)S(1)}, bf16[2,2,2,64,128]{4,3,2,1,0:T(8,128)(2,1)S(1)}, u32[]{:S(2)}, u32[]{:S(2)}) collective-permute-start(bf16[2,2,2,64,128]{4,3,2,1,0:T(8,128)(2,1)S(1)} %get-tuple-element.262), channel_id=1, source_target_pairs={{0,96},{32,0},{64,32},{96,64},{1,97},{33,1},{65,33},{97,65},{2,98}... | collective-permute-start | bytes 393224 | tf_op jit(solution)/shard_map/ppermute | solution.py:809
  175.9 11.4 %collective-permute-start.23 = (bf16[128,1024]{1,0:T(8,128)(2,1)S(1)}, bf16[128,1024]{1,0:T(8,128)(2,1)S(1)}, u32[]{:S(2)}, u32[]{:S(2)}) collective-permute-start(bf16[128,1024]{1,0:T(8,128)(2,1)S(1)} %get-tuple-element.260), channel_id=1, source_target_pairs={{0,32},{32,64},{64,96},{96,0},{1,33},{33,65},{65,97},{97,1},{2,34}... | collective-permute-start | bytes 786440 | tf_op jit(solution)/shard_map/ppermute | solution.py:809
  177.0 14.2 %collective-permute-start.22 = (bf16[128,1024]{1,0:T(8,128)(2,1)S(1)}, bf16[128,1024]{1,0:T(8,128)(2,1)S(1)}, u32[]{:S(2)}, u32[]{:S(2)}) collective-permute-start(bf16[128,1024]{1,0:T(8,128)(2,1)S(1)} %get-tuple-element.261), channel_id=1, source_target_pairs={{0,64},{32,96},{64,0},{96,32},{1,65},{33,97},{65,1},{97,33},{2,66}... | collective-permute-start | bytes 786440 | tf_op jit(solution)/shard_map/ppermute | solution.py:809
  179.5 11.7 %collective-permute-start.21 = (bf16[128,1024]{1,0:T(8,128)(2,1)S(1)}, bf16[128,1024]{1,0:T(8,128)(2,1)S(1)}, u32[]{:S(2)}, u32[]{:S(2)}) collective-permute-start(bf16[128,1024]{1,0:T(8,128)(2,1)S(1)} %get-tuple-element.259), channel_id=1, source_target_pairs={{0,96},{32,0},{64,32},{96,64},{1,97},{33,1},{65,33},{97,65},{2,98}... | collective-permute-start | bytes 786440 | tf_op jit(solution)/shard_map/ppermute | solution.py:809
  197.3 28.4 %all-to-all-start.3 = ((f32[32,64,128]{2,1,0:T(8,128)}), f32[32,64,128]{2,1,0:T(8,128)}, u32[]{:S(2)}, u32[]{:S(2)}) async-start(f32[32,64,128]{2,1,0:T(8,128)} %d_gated.1), calls=%async_computation.3 | async-start | bytes 2097152 | tf_op jit(solution)/shard_map/all_to_all | solution.py:991
  205.6 9.0 %collective-permute-start.24 = (bf16[128,1024]{1,0:T(8,128)(2,1)S(1)}, bf16[128,1024]{1,0:T(8,128)(2,1)S(1)}, u32[]{:S(2)}, u32[]{:S(2)}) collective-permute-start(bf16[128,1024]{1,0:T(8,128)(2,1)S(1)} %get-tuple-element.184.grads.grads_0), channel_id=1, source_target_pairs={{0,32},{32,64},{64,96},{96,0},{1,33},{33,65},{65,97},{97,1},{2,34}... | collective-permute-start | bytes 786440 | tf_op jit(solution)/shard_map/ppermute | solution.py:809
  206.1 14.6 %collective-permute-start.25 = (bf16[128,1024]{1,0:T(8,128)(2,1)S(1)}, bf16[128,1024]{1,0:T(8,128)(2,1)S(1)}, u32[]{:S(2)}, u32[]{:S(2)}) collective-permute-start(bf16[128,1024]{1,0:T(8,128)(2,1)S(1)} %get-tuple-element.184.grads.grads_0), channel_id=1, source_target_pairs={{0,64},{32,96},{64,0},{96,32},{1,65},{33,97},{65,1},{97,33},{2,66}... | collective-permute-start | bytes 786440 | tf_op jit(solution)/shard_map/ppermute | solution.py:809
  208.9 12.5 %collective-permute-start.26 = (bf16[128,1024]{1,0:T(8,128)(2,1)S(1)}, bf16[128,1024]{1,0:T(8,128)(2,1)S(1)}, u32[]{:S(2)}, u32[]{:S(2)}) collective-permute-start(bf16[128,1024]{1,0:T(8,128)(2,1)S(1)} %get-tuple-element.184.grads.grads_0), channel_id=1, source_target_pairs={{0,96},{32,0},{64,32},{96,64},{1,97},{33,1},{65,33},{97,65},{2,98}... | collective-permute-start | bytes 786440 | tf_op jit(solution)/shard_map/ppermute | solution.py:809
  235.1 6.5 %collective-permute-start.27 = (f32[4,4,128]{2,1,0:T(4,128)S(1)}, f32[4,4,128]{2,1,0:T(4,128)S(1)}, u32[]{:S(2)}, u32[]{:S(2)}) collective-permute-start(f32[4,4,128]{2,1,0:T(4,128)S(1)} %get-tuple-element.190.in_mine), channel_id=1, source_target_pairs={{0,1},{1,0},{2,3},{3,2},{4,5},{5,4},{6,7},{7,6},{8,9},{9,8},{10,11... | collective-permute-start | bytes 24584 | tf_op jit(solution)/shard_map/ppermute | solution.py:801
  237.1 42.8 %all-to-all-start.4 = ((bf16[16,256,128]{2,1,0:T(8,128)(2,1)}), bf16[16,256,128]{2,1,0:T(8,128)(2,1)}, u32[]{:S(2)}, u32[]{:S(2)}) async-start(bf16[16,256,128]{2,1,0:T(8,128)(2,1)} %output_weights.1), calls=%async_computation.5 | async-start | bytes 2097152 | tf_op jit(solution)/shard_map/all_to_all | solution.py:841
  288.8 40.9 %all-to-all-start.5 = ((bf16[16,64,1024]{2,1,0:T(8,128)(2,1)}), bf16[16,64,1024]{2,1,0:T(8,128)(2,1)}, u32[]{:S(2)}, u32[]{:S(2)}) async-start(bf16[16,64,1024]{2,1,0:T(8,128)(2,1)} %add_convert_fusion), calls=%async_computation.6 | async-start | bytes 4194304 | tf_op jit(solution)/shard_map/all_to_all | solution.py:841
  295.6 100.0 %all-gather.3.cloned.1.call-start = ((), (), s32[]{:S(2)}) async-start(), calls=%async_computation.9 | async-start | bytes 3342336 | tf_op jit(solution)/shard_map/all_gather | solution.py:1025
  296.0 27.6 %collective-permute-start.32 = (f32[24,128]{1,0:T(8,128)S(1)}, f32[24,128]{1,0:T(8,128)S(1)}, u32[]{:S(2)}, u32[]{:S(2)}) collective-permute-start(f32[24,128]{1,0:T(8,128)S(1)} %get-tuple-element.283), channel_id=1, source_target_pairs={{0,32},{32,64},{64,96},{96,0},{1,33},{33,65},{65,97},{97,1},{2,34}... | collective-permute-start | bytes 36872 | tf_op jit(solution)/shard_map/ppermute | solution.py:809
  296.4 27.3 %collective-permute-start.33 = (f32[24,128]{1,0:T(8,128)S(1)}, f32[24,128]{1,0:T(8,128)S(1)}, u32[]{:S(2)}, u32[]{:S(2)}) collective-permute-start(f32[24,128]{1,0:T(8,128)S(1)} %get-tuple-element.284), channel_id=1, source_target_pairs={{0,64},{32,96},{64,0},{96,32},{1,65},{33,97},{65,1},{97,33},{2,66}... | collective-permute-start | bytes 36872 | tf_op jit(solution)/shard_map/ppermute | solution.py:809
  300.3 28.0 %collective-permute-start.29 = (bf16[256,512]{1,0:T(8,128)(2,1)S(1)}, bf16[256,512]{1,0:T(8,128)(2,1)S(1)}, u32[]{:S(2)}, u32[]{:S(2)}) collective-permute-start(bf16[256,512]{1,0:T(8,128)(2,1)S(1)} %get-tuple-element.258), channel_id=1, source_target_pairs={{0,32},{32,64},{64,96},{96,0},{1,33},{33,65},{65,97},{97,1},{2,34}... | collective-permute-start | bytes 786440 | tf_op jit(solution)/shard_map/ppermute | solution.py:809
  300.5 27.8 %collective-permute-start.30 = (bf16[256,512]{1,0:T(8,128)(2,1)S(1)}, bf16[256,512]{1,0:T(8,128)(2,1)S(1)}, u32[]{:S(2)}, u32[]{:S(2)}) collective-permute-start(bf16[256,512]{1,0:T(8,128)(2,1)S(1)} %get-tuple-element.257), channel_id=1, source_target_pairs={{0,64},{32,96},{64,0},{96,32},{1,65},{33,97},{65,1},{97,33},{2,66}... | collective-permute-start | bytes 786440 | tf_op jit(solution)/shard_map/ppermute | solution.py:809
  301.6 13.0 %collective-permute-start.42 = (bf16[96,128]{1,0:T(8,128)(2,1)S(1)}, bf16[96,128]{1,0:T(8,128)(2,1)S(1)}, u32[]{:S(2)}, u32[]{:S(2)}) collective-permute-start(bf16[96,128]{1,0:T(8,128)(2,1)S(1)} %get-tuple-element.271), channel_id=1, source_target_pairs={{0,32},{32,64},{64,96},{96,0},{1,33},{33,65},{65,97},{97,1},{2,34}... | collective-permute-start | bytes 73736 | tf_op jit(solution)/shard_map/ppermute | solution.py:809
  322.3 7.4 %collective-permute-start.31 = (bf16[256,512]{1,0:T(8,128)(2,1)S(1)}, bf16[256,512]{1,0:T(8,128)(2,1)S(1)}, u32[]{:S(2)}, u32[]{:S(2)}) collective-permute-start(bf16[256,512]{1,0:T(8,128)(2,1)S(1)} %get-tuple-element.256), channel_id=1, source_target_pairs={{0,96},{32,0},{64,32},{96,64},{1,97},{33,1},{65,33},{97,65},{2,98}... | collective-permute-start | bytes 786440 | tf_op jit(solution)/shard_map/ppermute | solution.py:809
  323.7 10.7 %collective-permute-start.45 = (bf16[128,128]{1,0:T(8,128)(2,1)S(1)}, bf16[128,128]{1,0:T(8,128)(2,1)S(1)}, u32[]{:S(2)}, u32[]{:S(2)}) collective-permute-start(bf16[128,128]{1,0:T(8,128)(2,1)S(1)} %fusion.22), channel_id=1, source_target_pairs={{0,1},{1,0},{2,3},{3,2},{4,5},{5,4},{6,7},{7,6},{8,9},{9,8},{10,11... | collective-permute-start | bytes 98312 | tf_op jit(solution)/shard_map/ppermute | solution.py:801
  338.4 6.2 %collective-permute-start.36 = (bf16[64,256]{1,0:T(8,128)(2,1)S(1)}, bf16[64,256]{1,0:T(8,128)(2,1)S(1)}, u32[]{:S(2)}, u32[]{:S(2)}) collective-permute-start(bf16[64,256]{1,0:T(8,128)(2,1)S(1)} %fusion.21), channel_id=1, source_target_pairs={{0,1},{1,0},{2,3},{3,2},{4,5},{5,4},{6,7},{7,6},{8,9},{9,8},{10,11... | collective-permute-start | bytes 98312 | tf_op jit(solution)/shard_map/ppermute | solution.py:801
  346.3 10.9 %collective-permute-start.37 = (bf16[512,1024]{1,0:T(8,128)(2,1)}, bf16[512,1024]{1,0:T(8,128)(2,1)}, u32[]{:S(2)}, u32[]{:S(2)}) collective-permute-start(bf16[512,1024]{1,0:T(8,128)(2,1)} %convolution_convert_fusion), channel_id=1, source_target_pairs={{0,1},{1,0},{2,3},{3,2},{4,5},{5,4},{6,7},{7,6},{8,9},{9,8},{10,11... | collective-permute-start | bytes 3145736 | tf_op jit(solution)/shard_map/ppermute | solution.py:801
  350.4 36.8 %all-to-all-start.6 = ((bf16[16,432,128]{2,1,0:T(8,128)(2,1)}), bf16[16,432,128]{2,1,0:T(8,128)(2,1)}, u32[]{:S(2)}, u32[]{:S(2)}) async-start(bf16[16,432,128]{2,1,0:T(8,128)(2,1)} %broadcast_in_dim.36), calls=%async_computation.7 | async-start | bytes 3538944 | tf_op jit(solution)/shard_map/all_to_all | solution.py:841
  359.2 8.8 %collective-permute-start.40 = (bf16[128,1024]{1,0:T(8,128)(2,1)S(1)}, bf16[128,1024]{1,0:T(8,128)(2,1)S(1)}, u32[]{:S(2)}, u32[]{:S(2)}) collective-permute-start(bf16[128,1024]{1,0:T(8,128)(2,1)S(1)} %get-tuple-element.254), channel_id=1, source_target_pairs={{0,32},{32,64},{64,96},{96,0},{1,33},{33,65},{65,97},{97,1},{2,34}... | collective-permute-start | bytes 786440 | tf_op jit(solution)/shard_map/ppermute | solution.py:809
  359.3 14.8 %collective-permute-start.39 = (bf16[128,1024]{1,0:T(8,128)(2,1)S(1)}, bf16[128,1024]{1,0:T(8,128)(2,1)S(1)}, u32[]{:S(2)}, u32[]{:S(2)}) collective-permute-start(bf16[128,1024]{1,0:T(8,128)(2,1)S(1)} %get-tuple-element.255), channel_id=1, source_target_pairs={{0,64},{32,96},{64,0},{96,32},{1,65},{33,97},{65,1},{97,33},{2,66}... | collective-permute-start | bytes 786440 | tf_op jit(solution)/shard_map/ppermute | solution.py:809
  362.4 11.7 %collective-permute-start.38 = (bf16[128,1024]{1,0:T(8,128)(2,1)S(1)}, bf16[128,1024]{1,0:T(8,128)(2,1)S(1)}, u32[]{:S(2)}, u32[]{:S(2)}) collective-permute-start(bf16[128,1024]{1,0:T(8,128)(2,1)S(1)} %get-tuple-element.253), channel_id=1, source_target_pairs={{0,96},{32,0},{64,32},{96,64},{1,97},{33,1},{65,33},{97,65},{2,98}... | collective-permute-start | bytes 786440 | tf_op jit(solution)/shard_map/ppermute | solution.py:809
  387.2 10.1 %collective-permute-start.41 = (bf16[16,432,128]{2,1,0:T(8,128)(2,1)}, bf16[16,432,128]{2,1,0:T(8,128)(2,1)S(1)}, u32[]{:S(2)}, u32[]{:S(2)}) collective-permute-start(bf16[16,432,128]{2,1,0:T(8,128)(2,1)} %all-to-all-done.6.mine), channel_id=1, source_target_pairs={{0,1},{1,0},{2,3},{3,2},{4,5},{5,4},{6,7},{7,6},{8,9},{9,8},{10,11... | collective-permute-start | bytes 5308424 | tf_op jit(solution)/shard_map/ppermute | solution.py:801
  395.6 11.1 %collective-permute-start.46 = (bf16[16,768,128]{2,1,0:T(8,128)(2,1)}, bf16[16,768,128]{2,1,0:T(8,128)(2,1)}, u32[]{:S(2)}, u32[]{:S(2)}) collective-permute-start(bf16[16,768,128]{2,1,0:T(8,128)(2,1)} %bitcast.216), channel_id=1, source_target_pairs={{0,1},{1,0},{2,3},{3,2},{4,5},{5,4},{6,7},{7,6},{8,9},{9,8},{10,11... | collective-permute-start | bytes 9437192 | tf_op jit(solution)/shard_map/ppermute | solution.py:801
  (50 other events, 471.7 us)
Sparse Core Ops, SparseCore 0:
  192.7 96.0 reduce-scatter.1
  335.1 60.4 all-gather.2

commit v4 on v3

--- a/solution.py
+++ b/solution.py
@@ -14,6 +14,9 @@
 ROWS = CHUNK * GROUP
 
 FF = 2816
+WIDE_GROUP = 8
+WIDE_ROWS = CHUNK * WIDE_GROUP
+VMEM_LIMIT = 60 * 1024 * 1024
 
 CHIPS = [[chip * 2 + core for chip in range(16)] for core in range(2)]
 OTHER_CORE = [(place, place ^ 1) for place in range(32)]
@@ -112,7 +115,7 @@
             held[block_of(places, steps), :] = weight[...]
 
     first = core < 0.5
-    for at in range(GROUP):
+    for at in range(WIDE_GROUP):
         one, two = mine[at], theirs[at]
         x = jnp.concatenate([jnp.where(first, one, two), jnp.where(first, two, one)], axis=0).astype(f32)
         rate = lax.rsqrt(jnp.mean(x * x, axis=-1, keepdims=True) + epsilon)
@@ -122,14 +125,14 @@
     mixed_out[...] = mixed
     gate_out[...] = projected[:, 384:512]
     rates = projected[:, 512:]
-    ext[8 : 8 + ROWS, :] = mixed.astype(f32)
-    conv = taps[0:1, :] * ext[5 : 5 + ROWS, :]
+    ext[8 : 8 + WIDE_ROWS, :] = mixed.astype(f32)
+    conv = taps[0:1, :] * ext[5 : 5 + WIDE_ROWS, :]
     for lag in range(1, CONV):
-        conv = conv + taps[lag : lag + 1, :] * ext[5 + lag : 5 + lag + ROWS, :]
-    ext[0:8, :] = ext[ROWS : ROWS + 8, :]
+        conv = conv + taps[lag : lag + 1, :] * ext[5 + lag : 5 + lag + WIDE_ROWS, :]
+    ext[0:8, :] = ext[WIDE_ROWS : WIDE_ROWS + 8, :]
     conv_out[...] = conv
-    lanes = lax.broadcasted_iota(jnp.int32, (ROWS, 128), 1)
-    sums_in = jnp.broadcast_to(rates[:, 1:2], (ROWS, 128)) + bias
+    lanes = lax.broadcasted_iota(jnp.int32, (WIDE_ROWS, 128), 1)
+    sums_in = jnp.broadcast_to(rates[:, 1:2], (WIDE_ROWS, 128)) + bias
     glog = -scale * softplus(sums_in)
     cols_all = jnp.where(lanes == 0, jax.nn.sigmoid(rates), jnp.where(lanes == 3, jax.nn.sigmoid(sums_in), glog))
     rows, cols = square_iota()
@@ -137,7 +140,7 @@
     tri3 = jnp.concatenate([tri, tri, tri], axis=1)
     lane = lax.broadcasted_iota(jnp.int32, (CHUNK, CHUNK), 1)
     lowers, kept = [], []
-    for at in range(GROUP):
+    for at in range(WIDE_GROUP):
         here = slice(at * CHUNK, (at + 1) * CHUNK)
         q, k, rq, rk = unit_norms(silu(conv[here, :256]))
         queries, keys = q * (rq * 128**-0.5), k * rk
@@ -162,12 +165,12 @@
         kept.append((split(scores), right, ends, split(growth * queries), jnp.exp(last)))
     found = inverses(lowers, rows, cols)
     both = []
-    for at in range(GROUP):
+    for at in range(WIDE_GROUP):
         here = slice(at * CHUNK, (at + 1) * CHUNK)
         inv_out[here, :] = found[at]
         both.append(dot3(split(found[at]), kept[at][1], NN))
     maps = []
-    for at in range(GROUP):
+    for at in range(WIDE_GROUP):
         here = slice(at * CHUNK, (at + 1) * CHUNK)
         from_out[here, :] = both[at][:, :128]
         ended = dot3(kept[at][2], split(both[at]), TN)
@@ -176,7 +179,7 @@
         maps.append((split(move), ended[:, 128:]))
     current = state[...]
     states = []
-    for at in range(GROUP):
+    for at in range(WIDE_GROUP):
         here = slice(at * CHUNK, (at + 1) * CHUNK)
         state_out[here, :] = current
         pair = split(current)
@@ -184,7 +187,7 @@
         current = dot3(maps[at][0], pair, NN) + maps[at][1]
     state[...] = current
     ones = jnp.ones((8, 256), bf16)
-    for at in range(GROUP):
+    for at in range(WIDE_GROUP):
         here = slice(at * CHUNK, (at + 1) * CHUNK)
         product = dot3(stacked(split(both[at][:, :128]), kept[at][3]), states[at], NN)
         updates = both[at][:, 128:] - product[:CHUNK]
@@ -196,9 +199,9 @@
 
 
 def forward_call(numbers, places, mine, theirs, gain, weights, taps):
-    steps = 16 // GROUP
+    steps = 16 // WIDE_GROUP
     shape = jax.ShapeDtypeStruct
-    blocks = lambda width: pl.BlockSpec((ROWS, width), lambda i: (i, 0))
+    blocks = lambda width: pl.BlockSpec((WIDE_ROWS, width), lambda i: (i, 0))
     whole = lambda *dims: pl.BlockSpec(dims, lambda i: (0,) * len(dims))
     square = shape((2048, 128), f32)
     return pl.pallas_call(
@@ -207,15 +210,15 @@
         in_specs=[
             pl.BlockSpec(memory_space=pltpu.SMEM),
             pl.BlockSpec(memory_space=pltpu.SMEM),
-            pl.BlockSpec((GROUP, 64, 1024), lambda i: (i, 0, 0)),
-            pl.BlockSpec((GROUP, 64, 1024), lambda i: (i, 0, 0)),
+            pl.BlockSpec((WIDE_GROUP, 64, 1024), lambda i: (i, 0, 0)),
+            pl.BlockSpec((WIDE_GROUP, 64, 1024), lambda i: (i, 0, 0)),
             whole(1, 1024),
         ]
         + [whole(256, 640)] * 4
         + [whole(4, 384)],
         out_specs=[blocks(1024), blocks(384), blocks(128), blocks(384)]
         + [blocks(128)] * 8
-        + [pl.BlockSpec((1, GROUP, 128), lambda i: (i, 0, 0))],
+        + [pl.BlockSpec((1, WIDE_GROUP, 128), lambda i: (i, 0, 0))],
         out_shape=[
             shape((2048, 1024), bf16),
             shape((2048, 384), bf16),
@@ -223,14 +226,14 @@
             shape((2048, 384), f32),
         ]
         + [square] * 8
-        + [shape((steps, GROUP, 128), f32)],
+        + [shape((steps, WIDE_GROUP, 128), f32)],
         scratch_shapes=[
             pltpu.VMEM((128, 128), f32),
-            pltpu.VMEM((ROWS + 8, 384), f32),
+            pltpu.VMEM((WIDE_ROWS + 8, 384), f32),
             pltpu.VMEM((1024, 640), bf16),
         ],
         compiler_params=pltpu.CompilerParams(
-            dimension_semantics=("arbitrary",), vmem_limit_bytes=52 * 1024 * 1024
+            dimension_semantics=("arbitrary",), vmem_limit_bytes=VMEM_LIMIT
         ),
         cost_estimate=cost(30),
         name="delta_forward",
@@ -241,8 +244,8 @@
     numbers, places, taps, conv_in, cols_in, inv_in, from_in, upd_in, score_in, move_in, state_in, mixed_in,
     normed_in, heads_in, sq_mine, sq_theirs, in_mine, in_theirs, hidden_in, gate_in,
     weight_0, weight_1, weight_2, weight_3,
-    keep_out, give_out, unit_out, low_out, logits_out, taps_out, sums_out,
-    after, ext, d_all, held,
+    head_in, keep_out, give_out, unit_out, low_out,
+    after, ext, d_all, held, logits_out, taps_out, sums_out,
 ):
     step = pl.program_id(0)
     scale = numbers[2]
@@ -361,7 +364,14 @@
 
     @pl.when(step == 16 // GROUP - 1)
     def _():
-        low_out[...] = unit_out[...].astype(bf16)
+        edge = [head_in[0:1, :], sums_out[0:2, :], jnp.zeros((1, 128), f32)]
+        edge = jnp.concatenate([taps_out[0:4, :], jnp.concatenate(edge, axis=0)], axis=1)
+        for grp in range(4):
+            here = slice(grp * 256, grp * 256 + 256)
+            low_out[grp, 0:256, :] = unit_out[here, :].astype(bf16)
+            line = jnp.concatenate([logits_out[0:1, here], logits_out[1:2, here]], axis=1)
+            small = jnp.concatenate([edge, line, jnp.zeros((3, 512), f32)], axis=0)
+            low_out[grp, 256:272, :] = jnp.concatenate(split(small), axis=0)
 
 
 def backward_call(numbers, places, taps, *arrays):
@@ -380,25 +390,26 @@
         + [blocks(384), blocks(128), blocks(128)]
         + [lines] * 4
         + [blocks(1024), blocks(128)]
-        + [whole(256, 640)] * 4,
-        out_specs=[halves, halves, whole(1024, 512), whole(1024, 512), whole(8, 1024), whole(8, 384), whole(8, 128)],
+        + [whole(256, 640)] * 4
+        + [whole(8, 128)],
+        out_specs=[halves, halves, whole(1024, 512), whole(4, 272, 512)],
         out_shape=[
             shape((16, 64, 1024), f32),
             shape((16, 64, 1024), bf16),
             shape((1024, 512), f32),
-            shape((1024, 512), bf16),
-            shape((8, 1024), f32),
-            shape((8, 384), f32),
-            shape((8, 128), f32),
+            shape((4, 272, 512), bf16),
         ],
         scratch_shapes=[
             pltpu.VMEM((128, 128), f32),
             pltpu.VMEM((ROWS + 8, 384), f32),
             pltpu.VMEM((ROWS, 640), bf16),
             pltpu.VMEM((1024, 640), bf16),
+            pltpu.VMEM((8, 1024), f32),
+            pltpu.VMEM((8, 384), f32),
+            pltpu.VMEM((8, 128), f32),
         ],
         compiler_params=pltpu.CompilerParams(
-            dimension_semantics=("arbitrary",), vmem_limit_bytes=52 * 1024 * 1024
+            dimension_semantics=("arbitrary",), vmem_limit_bytes=VMEM_LIMIT
         ),
         cost_estimate=cost(36),
         name="delta_backward",
@@ -442,7 +453,7 @@
 
 
 def params():
-    return pltpu.CompilerParams(dimension_semantics=("arbitrary",), vmem_limit_bytes=52 * 1024 * 1024)
+    return pltpu.CompilerParams(dimension_semantics=("arbitrary",), vmem_limit_bytes=VMEM_LIMIT)
 
 
 def gate_call(heads, gate, mine, theirs, gain):
@@ -458,13 +469,16 @@
     )(heads, gate, mine, theirs, gain)
 
 
-def middle_kernel(numbers, gated, tokens, mine, theirs, gain, middle_out, hidden_out):
-    core = numbers[0]
+def middle_kernel(places, gated, tokens, *refs):
+    weights, (gain, middle_out, hidden_out) = refs[:8], refs[8:]
+    core = places[0]
     for at in range(2):
         line = tokens[at].astype(f32)
-        for weight, parity in ((mine, core), (theirs, 1 - core)):
-            found = [gated[at * 16 + numbers[2 + grp] * 4 + parity * 2 + half] for grp in range(4) for half in range(2)]
-            line = line + raw(jnp.concatenate(found, axis=1), weight[...], NN)
+        for side, parity in enumerate((core, 1 - core)):
+            for grp in range(4):
+                first = at * 16 + places[2 + grp] * 4 + parity * 2
+                found = jnp.concatenate([gated[first], gated[first + 1]], axis=1)
+                line = line + raw(found, weights[side * 4 + grp][...], NN)
         rows = slice(at * 64, at * 64 + 64)
         middle_out[rows, :] = line
         rate = lax.rsqrt(jnp.mean(line * line, axis=-1, keepdims=True) + epsilon)
@@ -475,35 +489,35 @@
     shape = jax.ShapeDtypeStruct
     return pl.pallas_call(
         middle_kernel,
-        in_specs=[pl.BlockSpec(memory_space=pltpu.SMEM)] + [pl.BlockSpec(memory_space=pltpu.VMEM)] * 5,
+        in_specs=[pl.BlockSpec(memory_space=pltpu.SMEM)] + [pl.BlockSpec(memory_space=pltpu.VMEM)] * 11,
         out_shape=[shape((128, 1024), f32), shape((128, 1024), bf16)],
-        compiler_params=pltpu.CompilerParams(vmem_limit_bytes=52 * 1024 * 1024),
+        compiler_params=pltpu.CompilerParams(vmem_limit_bytes=VMEM_LIMIT),
         cost_estimate=cost(4),
         name="middle",
-    )(places, gated, tokens, mine, theirs, gain)
-
-
-def d_gated_kernel(places, grads, mine, theirs, out):
+    )(places, gated, tokens, *mine, *theirs, gain)
+
+
+def d_gated_kernel(places, grads, *refs):
+    weights, out = refs[:8], refs[8]
     core = places[0]
-    for weight, parity in ((mine, core), (theirs, 1 - core)):
-        found = raw(grads[...], weight[...], NT)
-        for seq in range(2):
-            for grp in range(4):
+    for side, parity in enumerate((core, 1 - core)):
+        for grp in range(4):
+            found = raw(grads[...], weights[side * 4 + grp][...], NT)
+            for seq in range(2):
                 for half in range(2):
-                    at = (grp * 2 + half) * 128
                     to = seq * 16 + places[2 + grp] * 4 + parity * 2 + half
-                    out[to] = found[seq * 64 : seq * 64 + 64, at : at + 128]
+                    out[to] = found[seq * 64 : seq * 64 + 64, half * 128 : half * 128 + 128]
 
 
 def d_gated_call(places, grads, mine, theirs):
     return pl.pallas_call(
         d_gated_kernel,
-        in_specs=[pl.BlockSpec(memory_space=pltpu.SMEM)] + [pl.BlockSpec(memory_space=pltpu.VMEM)] * 3,
+        in_specs=[pl.BlockSpec(memory_space=pltpu.SMEM)] + [pl.BlockSpec(memory_space=pltpu.VMEM)] * 9,
         out_shape=jax.ShapeDtypeStruct((32, 64, 128), f32),
-        compiler_params=pltpu.CompilerParams(vmem_limit_bytes=52 * 1024 * 1024),
+        compiler_params=pltpu.CompilerParams(vmem_limit_bytes=VMEM_LIMIT),
         cost_estimate=cost(3),
         name="d_gated",
-    )(places, grads, mine, theirs)
+    )(places, grads, *mine, *theirs)
 
 
 def output_weights_kernel(
@@ -526,7 +540,7 @@
         output_weights_kernel,
         in_specs=[pl.BlockSpec(memory_space=pltpu.VMEM)] * 8,
         out_shape=jax.ShapeDtypeStruct((16, 256, 128), bf16),
-        compiler_params=pltpu.CompilerParams(vmem_limit_bytes=52 * 1024 * 1024),
+        compiler_params=pltpu.CompilerParams(vmem_limit_bytes=VMEM_LIMIT),
         cost_estimate=cost(3),
         name="output_weights",
     )(*arrays)
@@ -835,6 +849,10 @@
 def sum_chips(value):
     flat = value.reshape(-1, 128)
     return lax.psum_scatter(flat, "ctx", scatter_dimension=0, tiled=True, axis_index_groups=CHIPS)
+
+
+def wide_columns(value):
+    return jnp.concatenate([value[:, at * 128 : at * 128 + 128] for at in range(4)], axis=0)
 
 
 def over_chips(value):
@@ -957,18 +975,19 @@
         squares,
     ) = forward_call(numbers, places, x_mine, x_theirs, gain_one, w_unit, taps)
     heads_out, squares, gateup_pieces = lax.optimization_barrier((heads_out, squares, gateup_pieces))
+    squares = squares.reshape(16 // GROUP, GROUP, 128)
     squares_theirs = other_core(squares)
     gated = gate_call(heads_out, outgate, squares, squares_theirs, head_half)
 
     dy_low, output_pieces, gated = lax.optimization_barrier((dy_low, output_pieces, gated))
     gated_tokens = lax.all_to_all(gated.reshape(32, 64, 128), "ctx", 0, 0)
-    dy_mine = jnp.concatenate(from_grp(dy_low), axis=0)
-    output_mine = jnp.concatenate(output_pieces, axis=0)
-    output_theirs = other_core(output_mine)
-    gated_tokens, dy_mine = lax.optimization_barrier((gated_tokens, dy_mine))
+    output_theirs = [other_core(piece) for piece in output_pieces]
+    dy_pieces = from_grp(dy_low)
+    middle, hidden_two = middle_call(places, gated_tokens, block_input, output_pieces, output_theirs, gain_two)
+    r_two = lax.rsqrt(jnp.mean(middle * middle, axis=-1, keepdims=True) + epsilon)
+    dy_pieces, hidden_two = lax.optimization_barrier((dy_pieces, hidden_two))
+    dy_mine = jnp.concatenate(dy_pieces, axis=0)
     dy_theirs = other_core(dy_mine)
-    middle, hidden_two = middle_call(places, gated_tokens, block_input, output_mine, output_theirs, gain_two)
-    r_two = lax.rsqrt(jnp.mean(middle * middle, axis=-1, keepdims=True) + epsilon)
     two_mine, two_theirs = to_wide(hidden_two)
     w_gu = gateup_pieces.reshape(1024, 768)
     swi_theirs, grads_theirs, part_theirs = ff_call(two_theirs, dy_theirs, w_gu, w_dn)
@@ -986,7 +1005,7 @@
     dmix = dmiddle.astype(bf16)
     dmix, g_ff = lax.optimization_barrier((dmix, g_ff))
     g_ff = sum_chips(g_ff)
-    d_gated = d_gated_call(places, dmix, output_mine, output_theirs)
+    d_gated = d_gated_call(places, dmix, output_pieces, output_theirs)
     dmix, d_gated = lax.optimization_barrier((dmix, d_gated))
     d_gated = lax.all_to_all(d_gated, "ctx", 0, 0)
 
@@ -999,9 +1018,9 @@
         d_gated.reshape(2048, 128), heads_out, outgate, squares, squares_theirs, head_half
     )
     inner_theirs = other_core(inner)
-    keep, give, g_unit, g_unit_low, g_rates, g_taps, g_sums = backward_call(
+    keep, give, g_unit, g_unit_low = backward_call(
         numbers, places, taps, conv, columns, inverse, from_state, updates, scores, moves, states, mixed_in,
-        d_normed, heads_out, squares, squares_theirs, inner, inner_theirs, hidden_one, d_outgate, *w_unit,
+        d_normed, heads_out, squares, squares_theirs, inner, inner_theirs, hidden_one, d_outgate, *w_unit, g_head,
     )
 
     give, g_output = lax.optimization_barrier((give, g_output))
@@ -1009,29 +1028,23 @@
     d_sent = (keep + give_theirs.astype(f32)).astype(bf16)
     g_ff, g_output, g_unit_low, d_sent = lax.optimization_barrier((g_ff, g_output, g_unit_low, d_sent))
     d_tokens = over_chips(d_sent)
-    g_unit_pieces = exchange_grp(g_unit_low.reshape(4, 256, 512), grp)[1:]
+    g_unit_pieces = exchange_grp(g_unit_low, grp)
     g_output = g_output.astype(f32).sum(axis=0).reshape(2, 128, 128)
     g_output_theirs = other_core(lax.dynamic_index_in_dim(g_output, 1 - core, 0, False).astype(bf16))
     g_output = lax.dynamic_index_in_dim(g_output, core, 0, False) + g_output_theirs.astype(f32)
     g_gu = exchange_grp(g_ff[:384].astype(bf16).reshape(4, 96, 128), grp)
     early = jnp.concatenate(g_gu + [g_ff[384:].astype(bf16), g_output.astype(bf16)], axis=0)
-    g_rates = g_rates[:2].reshape(2, 4, 2, 128).transpose(1, 0, 2, 3).reshape(4, 4, 128)
-    shared = jnp.concatenate(
-        [g_taps[:4].reshape(12, 128), g_head[:1], g_sums[:2], jnp.zeros((5, 128), f32)], axis=0
-    )
-    g_small = jnp.concatenate([jnp.broadcast_to(shared, (4, 20, 128)), g_rates], axis=1)
-    g_small = exchange_grp(g_small, grp)
-    g_unit_pieces, g_small, d_tokens = lax.optimization_barrier((g_unit_pieces, g_small, d_tokens))
+    g_unit_pieces, d_tokens = lax.optimization_barrier((g_unit_pieces, d_tokens))
     early_mine = lax.all_gather(early, "ctx", axis_index_groups=CHIPS)
     early_theirs = other_core(early_mine)
     grad_gateup, grad_down, grad_output, mlp_sums = ff_grads_call(
         numbers, places, early_mine, early_theirs, w_gateup, jnp.broadcast_to(mlp_gain[:, None], (256, 128))
     )
 
-    g_small = sum(g_small)
+    g_small = sum(piece[256:264].astype(f32) + piece[264:].astype(f32) for piece in g_unit_pieces)
     g_sum = lax.dynamic_index_in_dim(g_unit.reshape(4, 256, 512), grp, 0, False)
-    for other in g_unit_pieces:
-        g_sum = g_sum + other.astype(f32)
+    for other in g_unit_pieces[1:]:
+        g_sum = g_sum + other[:256].astype(f32)
     g_sum = g_sum.reshape(2, 128, 512)
 
     dhidden_one = d_tokens.astype(f32)
@@ -1052,7 +1065,7 @@
     late = jnp.concatenate(late, axis=0).astype(bf16)
     small_high = lax.optimization_barrier(g_small.astype(bf16))
     small_low = (g_small - small_high.astype(f32)).astype(bf16)
-    late = jnp.concatenate([late, small_high, small_low], axis=0)
+    late = jnp.concatenate([late, wide_columns(small_high), wide_columns(small_low)], axis=0)
     late, swi_mine, swi_theirs = lax.optimization_barrier((late, swi_mine, swi_theirs))
     late_mine = over_chips(jnp.broadcast_to(late, (16,) + late.shape))
     block_out = middle + over_grp(*over_cores(mm(swi_mine, w_dn), mm(swi_theirs, w_dn), bf16))
@@ -1060,22 +1073,21 @@
     late_mine, block_output, input_grad = lax.optimization_barrier((late_mine, block_output, input_grad))
     late_theirs = other_core(late_mine)
     grad_mixer, grad_outgate, mixer_sums = mixer_grads_call(numbers, late_mine, late_theirs, w_mixer, w_outgate)
-    small_one = (late_mine[:, 384:408].astype(f32) + late_mine[:, 408:].astype(f32)).reshape(2, 8, 24, 128)
-    small_two = (late_theirs[:, 384:408].astype(f32) + late_theirs[:, 408:].astype(f32)).reshape(2, 8, 24, 128)
-    small_one, small_two = small_one.sum(axis=0), small_two.sum(axis=0)
+    small_of = lambda found: (found[:, 384:416].astype(f32) + found[:, 416:448].astype(f32)).reshape(2, 8, 32, 128).sum(axis=0)
+    small_one, small_two = small_of(late_mine), small_of(late_theirs)
+    small_low, small_high = jnp.where(core == 0, small_one, small_two), jnp.where(core == 0, small_two, small_one)
     both = small_one + small_two
-    g_low = jnp.where(core == 0, small_one, small_two)
-    g_high = jnp.where(core == 0, small_two, small_one)
-    taps_at = lambda value, at: value[:, :12].reshape(8, 4, 3, 128)[:, :, at].transpose(1, 0, 2).reshape(4, 1024)
-    taps_v = jnp.stack([g_low[:, :12], g_high[:, :12]], axis=1).reshape(8, 2, 4, 3, 128)[:, :, :, 2]
-    taps_v = taps_v.transpose(2, 0, 1, 3).reshape(4, 2048)
-    grad_conv = jnp.concatenate([taps_at(both, 0), taps_at(both, 1), taps_v], axis=1)
+    taps_q = both[:, 0:4].transpose(1, 0, 2).reshape(4, 1024)
+    taps_k = both[:, 8:12].transpose(1, 0, 2).reshape(4, 1024)
+    taps_v = jnp.stack([small_low[:, 16:20], small_high[:, 16:20]], axis=1).transpose(2, 0, 1, 3).reshape(4, 2048)
+    grad_conv = jnp.concatenate([taps_q, taps_k, taps_v], axis=1)
     grad_conv = lax.dynamic_slice_in_dim(grad_conv, grp * 1024, 1024, axis=1)
-    grad_head = jnp.concatenate([g_low[:, 12].sum(axis=0), g_high[:, 12].sum(axis=0)])
+    grad_head = jnp.concatenate([small_low[:, 24].sum(axis=0), small_high[:, 24].sum(axis=0)])
     grad_head = lax.dynamic_slice_in_dim(grad_head, grp * 64, 64, axis=0)
-    grad_scale = lax.dynamic_slice_in_dim(both[:, 13, 1], grp * 2, 2, axis=0)
-    grad_bias = lax.dynamic_slice_in_dim(both[:, 14, 1], grp * 2, 2, axis=0)
-    grad_rates = both[:, 20:].reshape(8, 2, 256).transpose(1, 0, 2).reshape(16, 256).T
+    grad_scale = lax.dynamic_slice_in_dim(both[:, 25, 1], grp * 2, 2, axis=0)
+    grad_bias = lax.dynamic_slice_in_dim(both[:, 26, 1], grp * 2, 2, axis=0)
+    rates = jnp.stack([both[:, 4], both[:, 12], both[:, 20], both[:, 28]], axis=1)
+    grad_rates = rates.reshape(8, 2, 256).transpose(1, 0, 2).reshape(16, 256).T
     grad_in_gain = (
         mixer_sums[:, 0]
         + jnp.sum(grad_rates * w_rates.astype(f32), axis=1)

time: 431 us -> 409 us (0.949)
  waiting for transfers between devices: 116 us -> 95.8 us
  other arithmetic: 24.5 us -> 19.3 us
    ppermute x33 -> x30, waiting for transfers between devices: 82.2 us -> 47.1 us  [along_grp(): lax.ppermute(value, 'grp', [(at, (at + steps) % 4) for at in range(4)])]
    ppermute x33 -> x30, starting transfers between devices: 37.7 us -> 47.1 us  [along_grp(): lax.ppermute(value, 'grp', [(at, (at + steps) % 4) for at in range(4)])]
    unnamed x110 -> x123, local copies, waits for them, and re-layouts: 18.6 us -> 9.68 us
    all_to_all x4, waiting for transfers between devices: 12.9 us -> 21 us  [over_chips(): return lax.all_to_all(value, 'ctx', 0, 0, axis_index_groups=CHIPS)]
    all_to_all x4, starting transfers between devices: 24.8 us -> 18.9 us  [over_chips(): return lax.all_to_all(value, 'ctx', 0, 0, axis_index_groups=CHIPS)]
    all_to_all x1, waiting for transfers between devices: 0.01 us -> 5.52 us  [body(): gated_tokens = lax.all_to_all(gated.reshape(32, 64, 128), 'ctx', 0, 0)]
    all_gather x1, waiting for transfers between devices: 5.43 us -> 0.01 us  [body(): early_mine = lax.all_gather(early, 'ctx', axis_index_groups=CHIPS)]
    ppermute x13 -> x16, waiting for transfers between devices: 9.06 us -> 11.6 us  [other_core(): return lax.ppermute(value, 'ctx', OTHER_CORE)]
  transfers between devices with their start and end apart: 56 -> 56, of which waited for: 25 -> 21; matrix products, arithmetic and copies ran while one was open for 9% -> 11% of each run, Pallas kernels for 23% -> 26%
where the time goes in v4:
time: 409 us; the launch traced here: 402 us
  Pallas kernels  124 us (30%)
  starting transfers between devices  106 us (26%)
  waiting for transfers between devices  95.8 us (23%)
  local copies, waits for them, and re-layouts  37.2 us (9%)
  other arithmetic  19.3 us (5%)
  between operations  16.2 us (4%)
    ppermute x30, waiting for transfers between devices, along_grp(): lax.ppermute(value, 'grp', [(at, (at + steps) % 4) for at in range(4)])  47.1 us
    ppermute x30, starting transfers between devices, along_grp(): lax.ppermute(value, 'grp', [(at, (at + steps) % 4) for at in range(4)])  47.1 us
    pallas_call x1, Pallas kernels, backward_call(): pl.pallas_call(backward_kernel, grid=(steps,), in_specs=[pl.BlockSpec(mem...  37.8 us
    pallas_call x1, Pallas kernels, forward_call(): pl.pallas_call(forward_kernel, grid=(steps,), in_specs=[pl.BlockSpec(memo...  28.4 us
    ppermute x16, starting transfers between devices, other_core(): return lax.ppermute(value, 'ctx', OTHER_CORE)  22.7 us
    all_to_all x4, waiting for transfers between devices, over_chips(): return lax.all_to_all(value, 'ctx', 0, 0, axis_index_groups=CHIPS)  21 us
    all_to_all x4, starting transfers between devices, over_chips(): return lax.all_to_all(value, 'ctx', 0, 0, axis_index_groups=CHIPS)  18.9 us
    ppermute x16, waiting for transfers between devices, other_core(): return lax.ppermute(value, 'ctx', OTHER_CORE)  11.6 us
  transfers between devices with their start and end apart: 56, of which 21 were waited for; matrix products, arithmetic and copies ran while one was open for 11% of the time, Pallas kernels for 26%

profile of v4, /device:TPU:1, one launch (start us, length us, event | category | flops | bytes accessed | tf_op | source)
XLA Modules:
  0.0 401.9 jit_solution(18392814185023140153)
XLA Ops:
  7.3 2.7 broadcast_in_dim.10
  12.6 2.5 collective-permute-start
  15.1 3.3 collective-permute-start.1
  21.2 6.8 %all-to-all-start = ((bf16[16,64,1024]{2,1,0:T(8,128)(2,1)}), bf16[16,64,1024]{2,1,0:T(8,128)(2,1)}, u32[]{:S(2)}, u32[]{:S(2)}) async-start(bf16[16,64,1024]{2,1,0:T(8,128)(2,1)} %bitcast.4), calls=%async_computation | async-start | bytes 4194304 | tf_op jit(solution)/shard_map/all_to_all | solution.py:859
  46.3 9.0 %collective-permute-done.4.refs_2_ = bf16[256,1024]{1,0:T(8,128)(2,1)} collective-permute-done((bf16[256,1024]{1,0:T(8,128)(2,1)}, bf16[256,1024]{1,0:T(8,128)(2,1)}, u32[]{:S(2)}, u32[]{:S(2)}) %collective-permute-start.4) | collective-permute-done | bytes 524320 | tf_op jit(solution)/shard_map/ppermute | solution.py:823
  55.4 4.2 %collective-permute-start.6 = (bf16[16,64,1024]{2,1,0:T(8,128)(2,1)}, bf16[16,64,1024]{2,1,0:T(8,128)(2,1)}, u32[]{:S(2)}, u32[]{:S(2)}) collective-permute-start(bf16[16,64,1024]{2,1,0:T(8,128)(2,1)} %all-to-all-done.mine), channel_id=1, source_target_pairs={{0,1},{1,0},{2,3},{3,2},{4,5},{5,4},{6,7},{7,6},{8,9},{9,8},{10,11... | collective-permute-start | bytes 6291464 | tf_op jit(solution)/shard_map/ppermute | solution.py:815
  59.9 3.8 all-to-all-start.1
  63.7 28.4 %delta_forward.1 = (bf16[2048,1024]{1,0:T(8,128)(2,1)}, bf16[2048,384]{1,0:T(8,128)(2,1)}, f32[2048,128]{1,0:T(8,128)}, f32[2048,384]{1,0:T(8,128)}, f32[2048,12...) custom-call(f32[4]{0:T(128)} %pad_maximum_fusion.12.numbers, ...), custom_call_target="tpu_custom_call" | custom-call | flops 30000001024 | bytes 90000000 | tf_op jit(solution)/shard_map/delta_forward/pallas_call | solution.py:207
  94.2 3.7 gate.1
  99.0 4.9 %all-to-all-start.2 = ((bf16[32,64,128]{2,1,0:T(8,128)(2,1)}), bf16[32,64,128]{2,1,0:T(8,128)(2,1)S(1)}, u32[]{:S(2)}, u32[]{:S(2)}) async-start(bf16[32,64,128]{2,1,0:T(8,128)(2,1)} %bitcast.179), calls=%async_computation.2 | async-start | bytes 1048576 | tf_op jit(solution)/shard_map/all_to_all | solution.py:983
  106.2 2.5 collective-permute-start.13
  109.9 5.5 %all-to-all-done.2.gated = bf16[32,64,128]{2,1,0:T(8,128)(2,1)S(1)} async-done(((bf16[32,64,128]{2,1,0:T(8,128)(2,1)}), bf16[32,64,128]{2,1,0:T(8,128)(2,1)S(1)}, u32[]{:S(2)}, u32[]{:S(2)}) %all-to-all-start.2) | async-done | bytes 524320 | tf_op jit(solution)/shard_map/all_to_all | solution.py:983
  116.2 4.9 %middle.1 = (f32[128,1024]{1,0:T(8,128)}, bf16[128,1024]{1,0:T(8,128)(2,1)}) custom-call(s32[6]{0:T(128)} %stack.87.places, bf16[32,64,128]{2,1,0:T(8,128)(2,1)} %copy-done.13, bf16[2,64,1024]{2,1,0:T(8,128)(2,1)} %tokens.1, bf16[256,1024]{1,0:T(8,128)(2,1)} %constant_dynamic-slice_fusion.7.refs_0_, bf16[256,1024]{1,0:T(8,128)(2,1)} %collective-permute-done.3.refs_1_, ...), custom_call_target="tpu_custom_call" | custom-call | flops 4000000000 | bytes 12000000 | tf_op jit(solution)/shard_map/middle/pallas_call | solution.py:490
  123.5 2.4 collective-permute-start.16
  128.5 2.4 collective-permute-done.15
  130.9 6.7 %collective-permute-done.16 = bf16[128,1024]{1,0:T(8,128)(2,1)S(1)} collective-permute-done((bf16[128,1024]{1,0:T(8,128)(2,1)}, bf16[128,1024]{1,0:T(8,128)(2,1)S(1)}, u32[]{:S(2)}, u32[]{:S(2)}) %collective-permute-start.16) | collective-permute-done | bytes 262176 | tf_op jit(solution)/shard_map/ppermute | solution.py:823
  142.4 6.4 %ff.1 = (bf16[512,384]{1,0:T(8,128)(2,1)}, bf16[512,768]{1,0:T(8,128)(2,1)}, f32[512,1024]{1,0:T(8,128)}) custom-call(bf16[512,1024]{1,0:T(8,128)(2,1)} %copy-done.36, bf16[512,1024]{1,0:T(8,128)(2,1)} %copy-done.35, bf16[1024,768]{1,0:T(8,128)(2,1)} %bitcast.174, bf16[384,1024]{1,0:T(8,128)(2,1)} %concatenate.49.down), custom_call_target="tpu_custom_call" | custom-call | flops 5000000000 | bytes 15000000 | tf_op jit(solution)/shard_map/ff/pallas_call | solution.py:565
  154.3 7.0 %ff_sum.1 = (bf16[512,384]{1,0:T(8,128)(2,1)}, bf16[512,768]{1,0:T(8,128)(2,1)}, bf16[512,1024]{1,0:T(8,128)(2,1)}, f32[128,1024]{1,0:T(8,128)}) custom-call(bf16[512,1024]{1,0:T(8,128)(2,1)} %copy-done.22, bf16[512,1024]{1,0:T(8,128)(2,1)} %copy-done.23, bf16[1024,768]{1,0:T(8,128)(2,1)} %bitcast.175, bf16[384,1024]{1,0:T(8,128)(2,1)} %concatenate.49.down, ...), custom_call_target="tpu_custom_call" | custom-call | flops 5000000000 | bytes 15000000 | tf_op jit(solution)/shard_map/ff_sum/pallas_call | solution.py:591
  166.1 8.3 %ff_weights.1 = f32[16,640,128]{2,1,0:T(8,128)} custom-call(bf16[512,1024]{1,0:T(8,128)(2,1)} %copy-done.22, bf16[512,1024]{1,0:T(8,128)(2,1)} %copy-done.36, bf16[512,768]{1,0:T(8,128)(2,1)} %get-tuple-element.172.grads_0, bf16[512,768]{1,0:T(8,128)(2,1)} %get-tuple-element.173.grads_1, bf16[512,384]{1,0:T(8,128)(2,1)} %get-tuple-element.209.swi_0, ...), custom_call_target="tpu_custom_call" | custom-call | flops 7000000000 | bytes 21000000 | tf_op jit(solution)/shard_map/ff_weights/pallas_call | solution.py:676
  178.8 4.7 %d_gated.1 = f32[32,64,128]{2,1,0:T(8,128)} custom-call(s32[6]{0:T(128)} %stack.87.places, bf16[128,1024]{1,0:T(8,128)(2,1)} %get-tuple-element.184.grads.grads_0, bf16[256,1024]{1,0:T(8,128)(2,1)} %constant_dynamic-slice_fusion.7.refs_0_, bf16[256,1024]{1,0:T(8,128)(2,1)} %collective-permute-done.3.refs_1_, ...), custom_call_target="tpu_custom_call" | custom-call | flops 3000000000 | bytes 9000000 | tf_op jit(solution)/shard_map/d_gated/pallas_call | solution.py:513
  183.5 7.3 %all-to-all-start.3 = ((f32[32,64,128]{2,1,0:T(8,128)}), f32[32,64,128]{2,1,0:T(8,128)S(1)}, u32[]{:S(2)}, u32[]{:S(2)}) async-start(f32[32,64,128]{2,1,0:T(8,128)} %d_gated.1), calls=%async_computation.3 | async-start | bytes 2097152 | tf_op jit(solution)/shard_map/all_to_all | solution.py:1010
  191.6 3.1 collective-permute-start.28
  194.6 5.2 %collective-permute-done.27.grads_1 = bf16[128,1024]{1,0:T(8,128)(2,1)S(1)} collective-permute-done((bf16[128,1024]{1,0:T(8,128)(2,1)S(1)}, bf16[128,1024]{1,0:T(8,128)(2,1)S(1)}, u32[]{:S(2)}, u32[]{:S(2)}) %collective-permute-start.27) | collective-permute-done | bytes 262176 | tf_op jit(solution)/shard_map/ppermute | solution.py:823
  199.9 6.4 %collective-permute-done.28.grads_2 = bf16[128,1024]{1,0:T(8,128)(2,1)S(1)} collective-permute-done((bf16[128,1024]{1,0:T(8,128)(2,1)S(1)}, bf16[128,1024]{1,0:T(8,128)(2,1)S(1)}, u32[]{:S(2)}, u32[]{:S(2)}) %collective-permute-start.28) | collective-permute-done | bytes 262176 | tf_op jit(solution)/shard_map/ppermute | solution.py:823
  206.2 4.6 %all-to-all-done.3 = f32[32,64,128]{2,1,0:T(8,128)S(1)} async-done(((f32[32,64,128]{2,1,0:T(8,128)}), f32[32,64,128]{2,1,0:T(8,128)S(1)}, u32[]{:S(2)}, u32[]{:S(2)}) %all-to-all-start.3) | async-done | bytes 1048608 | tf_op jit(solution)/shard_map/all_to_all | solution.py:1010
  210.8 3.5 output_weights.1
  214.3 4.1 %gate_back.1 = (f32[2048,128]{1,0:T(8,128)}, bf16[2048,128]{1,0:T(8,128)(2,1)}, f32[4,4,128]{2,1,0:T(4,128)}, f32[8,128]{1,0:T(8,128)}) custom-call(f32[2048,128]{1,0:T(8,128)} %bitcast.176, f32[2048,128]{1,0:T(8,128)} %get-tuple-element.147.heads.heads_in, f32[2048,128]{1,0:T(8,128)} %get-tuple-element.148.gate, f32[4,4,128]{2,1,0:T(4,128)} %bitcast.208, ...), custom_call_target="tpu_custom_call" | custom-call | flops 4000000000 | bytes 12000000 | tf_op jit(solution)/shard_map/gate_back/pallas_call | solution.py:637
  220.6 3.7 all-to-all-start.4
  224.9 37.8 %delta_backward.1 = (f32[16,64,1024]{2,1,0:T(8,128)}, bf16[16,64,1024]{2,1,0:T(8,128)(2,1)}, f32[1024,512]{1,0:T(8,128)}, bf16[4,272,512]{2,1,0:T(8,128)(2,1)}) custom-call(f32[4]{0:T(128)} %pad_maximum_fusion.12.numbers, s32[6]{0:T(128)} %stack.87.places, f32[4,384]{1,0:T(4,128)} %pad_maximum_fusion.10.taps, f32[2048,384]{1,0:T(8,128)} %get-tuple-element.131.conv_in, ...), custom_call_target="tpu_custom_call" | custom-call | flops 35999997952 | bytes 108000000 | tf_op jit(solution)/shard_map/delta_backward/pallas_call | solution.py:384
  262.8 4.4 %collective-permute-done.31 = bf16[16,64,1024]{2,1,0:T(8,128)(2,1)S(1)} collective-permute-done((bf16[16,64,1024]{2,1,0:T(8,128)(2,1)}, bf16[16,64,1024]{2,1,0:T(8,128)(2,1)S(1)}, u32[]{:S(2)}, u32[]{:S(2)}) %collective-permute-start.31) | collective-permute-done | bytes 2097184 | tf_op jit(solution)/shard_map/ppermute | solution.py:815
  267.2 4.4 %add_convert_fusion = bf16[16,64,1024]{2,1,0:T(8,128)(2,1)} fusion(f32[16,64,1024]{2,1,0:T(8,128)} %get-tuple-element.200, bf16[16,64,1024]{2,1,0:T(8,128)(2,1)S(1)} %collective-permute-done.31), kind=kLoop, calls=%fused_computation.1 | loop fusion | flops 3145728 | bytes 8388608 | tf_op jit(solution)/shard_map/convert_element_type | solution.py:1028
  271.6 2.5 reduce-scatter.2.cloned.1.call-done
  274.0 4.7 %all-to-all-start.5 = ((bf16[16,64,1024]{2,1,0:T(8,128)(2,1)}), bf16[16,64,1024]{2,1,0:T(8,128)(2,1)S(1)}, u32[]{:S(2)}, u32[]{:S(2)}) async-start(bf16[16,64,1024]{2,1,0:T(8,128)(2,1)} %add_convert_fusion), calls=%async_computation.6 | async-start | bytes 4194304 | tf_op jit(solution)/shard_map/all_to_all | solution.py:859
  282.5 2.6 collective-permute-start.33
  288.5 4.6 %collective-permute-done.42 = bf16[96,128]{1,0:T(8,128)(2,1)S(1)} collective-permute-done((bf16[96,128]{1,0:T(8,128)(2,1)S(1)}, bf16[96,128]{1,0:T(8,128)(2,1)S(1)}, u32[]{:S(2)}, u32[]{:S(2)}) %collective-permute-start.42) | collective-permute-done | bytes 24608 | tf_op jit(solution)/shard_map/ppermute | solution.py:823
  293.1 3.7 collective-permute-start.44
  297.4 3.4 collective-permute-start.45
  303.3 2.5 all-to-all-done.5
  309.3 3.4 collective-permute-done.35
  312.8 5.7 %collective-permute-start.36 = (bf16[64,256]{1,0:T(8,128)(2,1)S(1)}, bf16[64,256]{1,0:T(8,128)(2,1)S(1)}, u32[]{:S(2)}, u32[]{:S(2)}) collective-permute-start(bf16[64,256]{1,0:T(8,128)(2,1)S(1)} %fusion.21), channel_id=1, source_target_pairs={{0,1},{1,0},{2,3},{3,2},{4,5},{5,4},{6,7},{7,6},{8,9},{9,8},{10,11... | collective-permute-start | bytes 98312 | tf_op jit(solution)/shard_map/ppermute | solution.py:815
  324.5 3.7 all-to-all-start.6
  332.0 2.6 collective-permute-start.39
  336.7 3.2 collective-permute-done.40
  339.9 6.6 %collective-permute-done.39 = bf16[128,1024]{1,0:T(8,128)(2,1)S(1)} collective-permute-done((bf16[128,1024]{1,0:T(8,128)(2,1)S(1)}, bf16[128,1024]{1,0:T(8,128)(2,1)S(1)}, u32[]{:S(2)}, u32[]{:S(2)}) %collective-permute-start.39) | collective-permute-done | bytes 262176 | tf_op jit(solution)/shard_map/ppermute | solution.py:823
  347.5 18.5 %all-to-all-done.6.mine = bf16[16,448,128]{2,1,0:T(8,128)(2,1)S(1)} async-done(((bf16[16,448,128]{2,1,0:T(8,128)(2,1)}), bf16[16,448,128]{2,1,0:T(8,128)(2,1)S(1)}, u32[]{:S(2)}, u32[]{:S(2)}) %all-to-all-start.6) | async-done | bytes 1835040 | tf_op jit(solution)/shard_map/all_to_all | solution.py:859
  368.4 3.7 collective-permute-done.41.theirs
  376.0 5.3 %mixer_grads.1 = (f32[256,4096]{1,0:T(8,128)}, f32[256,2048]{1,0:T(8,128)}, f32[256,128]{1,0:T(8,128)}) custom-call(f32[4]{0:T(128)} %pad_maximum_fusion.12.numbers, bf16[16,448,128]{2,1,0:T(8,128)(2,1)} %copy-done.8, bf16[16,448,128]{2,1,0:T(8,128)(2,1)} %collective-permute-done.41.theirs, bf16[256,4096]{1,0:T(8,128)(2,1)} %weight.2, ...), custom_call_target="tpu_custom_call" | custom-call | flops 4000000000 | bytes 12000000 | tf_op jit(solution)/shard_map/mixer_grads/pallas_call | solution.py:780
  383.6 9.7 %ff_grads.1 = (f32[256,5632]{1,0:T(8,128)}, f32[704,1024]{1,0:T(8,128)}, f32[512,1024]{1,0:T(8,128)}, f32[256,128]{1,0:T(8,128)}) custom-call(f32[4]{0:T(128)} %pad_maximum_fusion.12.numbers, s32[6]{0:T(128)} %stack.87.places, bf16[16,768,128]{2,1,0:T(8,128)(2,1)} %bitcast.205, bf16[16,768,128]{2,1,0:T(8,128)(2,1)} %collective-permute-done.46.theirs, ...), custom_call_target="tpu_custom_call" | custom-call | flops 8000000000 | bytes 24000000 | tf_op jit(solution)/shard_map/ff_grads/pallas_call | solution.py:730
  (314 shorter events, 95.0 us)
Async XLA Ops:
  12.6 27.2 %collective-permute-start = (bf16[256,640]{1,0:T(8,128)(2,1)}, bf16[256,640]{1,0:T(8,128)(2,1)}, u32[]{:S(2)}, u32[]{:S(2)}) collective-permute-start(bf16[256,640]{1,0:T(8,128)(2,1)} %concatenate.51.weight_0), channel_id=1, source_target_pairs={{0,32},{32,64},{64,96},{96,0},{1,33},{33,65},{65,97},{97,1},{2,34}... | collective-permute-start | bytes 983048 | tf_op jit(solution)/shard_map/ppermute | solution.py:823
  15.1 23.7 %collective-permute-start.1 = (bf16[256,640]{1,0:T(8,128)(2,1)}, bf16[256,640]{1,0:T(8,128)(2,1)}, u32[]{:S(2)}, u32[]{:S(2)}) collective-permute-start(bf16[256,640]{1,0:T(8,128)(2,1)} %concatenate.51.weight_0), channel_id=1, source_target_pairs={{0,64},{32,96},{64,0},{96,32},{1,65},{33,97},{65,1},{97,33},{2,66}... | collective-permute-start | bytes 983048 | tf_op jit(solution)/shard_map/ppermute | solution.py:823
  18.4 17.4 %collective-permute-start.2 = (bf16[256,640]{1,0:T(8,128)(2,1)}, bf16[256,640]{1,0:T(8,128)(2,1)}, u32[]{:S(2)}, u32[]{:S(2)}) collective-permute-start(bf16[256,640]{1,0:T(8,128)(2,1)} %concatenate.51.weight_0), channel_id=1, source_target_pairs={{0,96},{32,0},{64,32},{96,64},{1,97},{33,1},{65,33},{97,65},{2,98}... | collective-permute-start | bytes 983048 | tf_op jit(solution)/shard_map/ppermute | solution.py:823
  20.0 26.4 %collective-permute-start.3 = (bf16[256,1024]{1,0:T(8,128)(2,1)}, bf16[256,1024]{1,0:T(8,128)(2,1)}, u32[]{:S(2)}, u32[]{:S(2)}) collective-permute-start(bf16[256,1024]{1,0:T(8,128)(2,1)} %constant_dynamic-slice_fusion.7.refs_0_), channel_id=1, source_target_pairs={{0,32},{32,64},{64,96},{96,0},{1,33},{33,65},{65,97},{97,1},{2,34}... | collective-permute-start | bytes 1572872 | tf_op jit(solution)/shard_map/ppermute | solution.py:823
  20.7 34.6 %collective-permute-start.4 = (bf16[256,1024]{1,0:T(8,128)(2,1)}, bf16[256,1024]{1,0:T(8,128)(2,1)}, u32[]{:S(2)}, u32[]{:S(2)}) collective-permute-start(bf16[256,1024]{1,0:T(8,128)(2,1)} %constant_dynamic-slice_fusion.7.refs_0_), channel_id=1, source_target_pairs={{0,64},{32,96},{64,0},{96,32},{1,65},{33,97},{65,1},{97,33},{2,66}... | collective-permute-start | bytes 1572872 | tf_op jit(solution)/shard_map/ppermute | solution.py:823
  21.2 34.2 %all-to-all-start = ((bf16[16,64,1024]{2,1,0:T(8,128)(2,1)}), bf16[16,64,1024]{2,1,0:T(8,128)(2,1)}, u32[]{:S(2)}, u32[]{:S(2)}) async-start(bf16[16,64,1024]{2,1,0:T(8,128)(2,1)} %bitcast.4), calls=%async_computation | async-start | bytes 4194304 | tf_op jit(solution)/shard_map/all_to_all | solution.py:859
  35.8 19.6 %collective-permute-start.5 = (bf16[256,1024]{1,0:T(8,128)(2,1)}, bf16[256,1024]{1,0:T(8,128)(2,1)S(1)}, u32[]{:S(2)}, u32[]{:S(2)}) collective-permute-start(bf16[256,1024]{1,0:T(8,128)(2,1)} %constant_dynamic-slice_fusion.7.refs_0_), channel_id=1, source_target_pairs={{0,96},{32,0},{64,32},{96,64},{1,97},{33,1},{65,33},{97,65},{2,98}... | collective-permute-start | bytes 1572872 | tf_op jit(solution)/shard_map/ppermute | solution.py:823
  55.4 8.3 %collective-permute-start.6 = (bf16[16,64,1024]{2,1,0:T(8,128)(2,1)}, bf16[16,64,1024]{2,1,0:T(8,128)(2,1)}, u32[]{:S(2)}, u32[]{:S(2)}) collective-permute-start(bf16[16,64,1024]{2,1,0:T(8,128)(2,1)} %all-to-all-done.mine), channel_id=1, source_target_pairs={{0,1},{1,0},{2,3},{3,2},{4,5},{5,4},{6,7},{7,6},{8,9},{9,8},{10,11... | collective-permute-start | bytes 6291464 | tf_op jit(solution)/shard_map/ppermute | solution.py:815
  59.9 32.3 %all-to-all-start.1 = ((bf16[4,256,768]{2,1,0:T(8,128)(2,1)}), bf16[4,256,768]{2,1,0:T(8,128)(2,1)S(1)}, u32[]{:S(2)}, u32[]{:S(2)}) async-start(bf16[4,256,768]{2,1,0:T(8,128)(2,1)} %pad_maximum_fusion), calls=%async_computation.1 | async-start | bytes 3145728 | tf_op jit(solution)/shard_map/all_to_all | solution.py:972
  98.0 8.3 %collective-permute-start.8 = (bf16[256,1024]{1,0:T(8,128)(2,1)}, bf16[256,1024]{1,0:T(8,128)(2,1)}, u32[]{:S(2)}, u32[]{:S(2)}) collective-permute-start(bf16[256,1024]{1,0:T(8,128)(2,1)} %constant_dynamic-slice_fusion.7.refs_0_), channel_id=1, source_target_pairs={{0,1},{1,0},{2,3},{3,2},{4,5},{5,4},{6,7},{7,6},{8,9},{9,8},{10,11... | collective-permute-start | bytes 1572872 | tf_op jit(solution)/shard_map/ppermute | solution.py:815
  98.3 10.4 %collective-permute-start.9 = (bf16[256,1024]{1,0:T(8,128)(2,1)}, bf16[256,1024]{1,0:T(8,128)(2,1)S(1)}, u32[]{:S(2)}, u32[]{:S(2)}) collective-permute-start(bf16[256,1024]{1,0:T(8,128)(2,1)} %collective-permute-done.3.refs_1_), channel_id=1, source_target_pairs={{0,1},{1,0},{2,3},{3,2},{4,5},{5,4},{6,7},{7,6},{8,9},{9,8},{10,11... | collective-permute-start | bytes 1572872 | tf_op jit(solution)/shard_map/ppermute | solution.py:815
  98.5 16.9 %collective-permute-start.10 = (bf16[256,1024]{1,0:T(8,128)(2,1)}, bf16[256,1024]{1,0:T(8,128)(2,1)}, u32[]{:S(2)}, u32[]{:S(2)}) collective-permute-start(bf16[256,1024]{1,0:T(8,128)(2,1)} %collective-permute-done.4.refs_2_), channel_id=1, source_target_pairs={{0,1},{1,0},{2,3},{3,2},{4,5},{5,4},{6,7},{7,6},{8,9},{9,8},{10,11... | collective-permute-start | bytes 1572872 | tf_op jit(solution)/shard_map/ppermute | solution.py:815
  98.8 16.6 %collective-permute-start.11 = (bf16[256,1024]{1,0:T(8,128)(2,1)S(1)}, bf16[256,1024]{1,0:T(8,128)(2,1)}, u32[]{:S(2)}, u32[]{:S(2)}) collective-permute-start(bf16[256,1024]{1,0:T(8,128)(2,1)S(1)} %collective-permute-done.5.refs_3_), channel_id=1, source_target_pairs={{0,1},{1,0},{2,3},{3,2},{4,5},{5,4},{6,7},{7,6},{8,9},{9,8},{10,11... | collective-permute-start | bytes 1572872 | tf_op jit(solution)/shard_map/ppermute | solution.py:815
  99.0 16.4 %all-to-all-start.2 = ((bf16[32,64,128]{2,1,0:T(8,128)(2,1)}), bf16[32,64,128]{2,1,0:T(8,128)(2,1)S(1)}, u32[]{:S(2)}, u32[]{:S(2)}) async-start(bf16[32,64,128]{2,1,0:T(8,128)(2,1)} %bitcast.179), calls=%async_computation.2 | async-start | bytes 1048576 | tf_op jit(solution)/shard_map/all_to_all | solution.py:983
  103.8 170.2 %reduce-scatter.2.cloned.1.call-start = ((), (), s32[]{:S(2)}) async-start(), calls=%async_computation.8 | async-start | bytes 5570560 | tf_op jit(solution)/shard_map/reduce_scatter | solution.py:851
  104.5 16.6 %collective-permute-start.12 = (bf16[128,1024]{1,0:T(8,128)(2,1)S(1)}, bf16[128,1024]{1,0:T(8,128)(2,1)S(1)}, u32[]{:S(2)}, u32[]{:S(2)}) collective-permute-start(bf16[128,1024]{1,0:T(8,128)(2,1)S(1)} %bitcast_convert_fusion), channel_id=1, source_target_pairs={{0,32},{32,64},{64,96},{96,0},{1,33},{33,65},{65,97},{97,1},{2,34}... | collective-permute-start | bytes 786440 | tf_op jit(solution)/shard_map/ppermute | solution.py:823
  106.2 14.8 %collective-permute-start.13 = (bf16[128,1024]{1,0:T(8,128)(2,1)S(1)}, bf16[128,1024]{1,0:T(8,128)(2,1)S(1)}, u32[]{:S(2)}, u32[]{:S(2)}) collective-permute-start(bf16[128,1024]{1,0:T(8,128)(2,1)S(1)} %bitcast_convert_fusion), channel_id=1, source_target_pairs={{0,64},{32,96},{64,0},{96,32},{1,65},{33,97},{65,1},{97,33},{2,66}... | collective-permute-start | bytes 786440 | tf_op jit(solution)/shard_map/ppermute | solution.py:823
  108.7 12.4 %collective-permute-start.14 = (bf16[128,1024]{1,0:T(8,128)(2,1)S(1)}, bf16[128,1024]{1,0:T(8,128)(2,1)S(1)}, u32[]{:S(2)}, u32[]{:S(2)}) collective-permute-start(bf16[128,1024]{1,0:T(8,128)(2,1)S(1)} %bitcast_convert_fusion), channel_id=1, source_target_pairs={{0,96},{32,0},{64,32},{96,64},{1,97},{33,1},{65,33},{97,65},{2,98}... | collective-permute-start | bytes 786440 | tf_op jit(solution)/shard_map/ppermute | solution.py:823
  122.0 8.9 %collective-permute-start.15 = (bf16[128,1024]{1,0:T(8,128)(2,1)}, bf16[128,1024]{1,0:T(8,128)(2,1)S(1)}, u32[]{:S(2)}, u32[]{:S(2)}) collective-permute-start(bf16[128,1024]{1,0:T(8,128)(2,1)} %get-tuple-element.158), channel_id=1, source_target_pairs={{0,32},{32,64},{64,96},{96,0},{1,33},{33,65},{65,97},{97,1},{2,34}... | collective-permute-start | bytes 786440 | tf_op jit(solution)/shard_map/ppermute | solution.py:823
  123.5 14.2 %collective-permute-start.16 = (bf16[128,1024]{1,0:T(8,128)(2,1)}, bf16[128,1024]{1,0:T(8,128)(2,1)S(1)}, u32[]{:S(2)}, u32[]{:S(2)}) collective-permute-start(bf16[128,1024]{1,0:T(8,128)(2,1)} %get-tuple-element.158), channel_id=1, source_target_pairs={{0,64},{32,96},{64,0},{96,32},{1,65},{33,97},{65,1},{97,33},{2,66}... | collective-permute-start | bytes 786440 | tf_op jit(solution)/shard_map/ppermute | solution.py:823
  125.9 11.8 %collective-permute-start.17 = (bf16[128,1024]{1,0:T(8,128)(2,1)}, bf16[128,1024]{1,0:T(8,128)(2,1)S(1)}, u32[]{:S(2)}, u32[]{:S(2)}) collective-permute-start(bf16[128,1024]{1,0:T(8,128)(2,1)} %get-tuple-element.158), channel_id=1, source_target_pairs={{0,96},{32,0},{64,32},{96,64},{1,97},{33,1},{65,33},{97,65},{2,98}... | collective-permute-start | bytes 786440 | tf_op jit(solution)/shard_map/ppermute | solution.py:823
  127.2 11.9 %collective-permute-start.19 = (bf16[512,1024]{1,0:T(8,128)(2,1)S(1)}, bf16[512,1024]{1,0:T(8,128)(2,1)S(1)}, u32[]{:S(2)}, u32[]{:S(2)}) collective-permute-start(bf16[512,1024]{1,0:T(8,128)(2,1)S(1)} %constant_dynamic-update-slice_fusion.4.dy.dy_0), channel_id=1, source_target_pairs={{0,1},{1,0},{2,3},{3,2},{4,5},{5,4},{6,7},{7,6},{8,9},{9,8},{10,11... | collective-permute-start | bytes 3145736 | tf_op jit(solution)/shard_map/ppermute | solution.py:815
  149.8 11.5 %collective-permute-start.21 = (bf16[2,2,2,64,128]{4,3,2,1,0:T(8,128)(2,1)S(1)}, bf16[2,2,2,64,128]{4,3,2,1,0:T(8,128)(2,1)S(1)}, u32[]{:S(2)}, u32[]{:S(2)}) collective-permute-start(bf16[2,2,2,64,128]{4,3,2,1,0:T(8,128)(2,1)S(1)} %get-tuple-element.257), channel_id=1, source_target_pairs={{0,32},{32,64},{64,96},{96,0},{1,33},{33,65},{65,97},{97,1},{2,34}... | collective-permute-start | bytes 393224 | tf_op jit(solution)/shard_map/ppermute | solution.py:823
  150.7 10.6 %collective-permute-start.22 = (bf16[2,2,2,64,128]{4,3,2,1,0:T(8,128)(2,1)S(1)}, bf16[2,2,2,64,128]{4,3,2,1,0:T(8,128)(2,1)S(1)}, u32[]{:S(2)}, u32[]{:S(2)}) collective-permute-start(bf16[2,2,2,64,128]{4,3,2,1,0:T(8,128)(2,1)S(1)} %get-tuple-element.256), channel_id=1, source_target_pairs={{0,64},{32,96},{64,0},{96,32},{1,65},{33,97},{65,1},{97,33},{2,66}... | collective-permute-start | bytes 393224 | tf_op jit(solution)/shard_map/ppermute | solution.py:823
  152.9 8.5 %collective-permute-start.23 = (bf16[2,2,2,64,128]{4,3,2,1,0:T(8,128)(2,1)S(1)}, bf16[2,2,2,64,128]{4,3,2,1,0:T(8,128)(2,1)S(1)}, u32[]{:S(2)}, u32[]{:S(2)}) collective-permute-start(bf16[2,2,2,64,128]{4,3,2,1,0:T(8,128)(2,1)S(1)} %get-tuple-element.255), channel_id=1, source_target_pairs={{0,96},{32,0},{64,32},{96,64},{1,97},{33,1},{65,33},{97,65},{2,98}... | collective-permute-start | bytes 393224 | tf_op jit(solution)/shard_map/ppermute | solution.py:823
  162.6 11.8 %collective-permute-start.26 = (bf16[128,1024]{1,0:T(8,128)(2,1)S(1)}, bf16[128,1024]{1,0:T(8,128)(2,1)S(1)}, u32[]{:S(2)}, u32[]{:S(2)}) collective-permute-start(bf16[128,1024]{1,0:T(8,128)(2,1)S(1)} %get-tuple-element.253), channel_id=1, source_target_pairs={{0,32},{32,64},{64,96},{96,0},{1,33},{33,65},{65,97},{97,1},{2,34}... | collective-permute-start | bytes 786440 | tf_op jit(solution)/shard_map/ppermute | solution.py:823
  162.8 13.6 %collective-permute-start.25 = (bf16[128,1024]{1,0:T(8,128)(2,1)S(1)}, bf16[128,1024]{1,0:T(8,128)(2,1)S(1)}, u32[]{:S(2)}, u32[]{:S(2)}) collective-permute-start(bf16[128,1024]{1,0:T(8,128)(2,1)S(1)} %get-tuple-element.254), channel_id=1, source_target_pairs={{0,64},{32,96},{64,0},{96,32},{1,65},{33,97},{65,1},{97,33},{2,66}... | collective-permute-start | bytes 786440 | tf_op jit(solution)/shard_map/ppermute | solution.py:823
  164.7 12.6 %collective-permute-start.24 = (bf16[128,1024]{1,0:T(8,128)(2,1)S(1)}, bf16[128,1024]{1,0:T(8,128)(2,1)S(1)}, u32[]{:S(2)}, u32[]{:S(2)}) collective-permute-start(bf16[128,1024]{1,0:T(8,128)(2,1)S(1)} %get-tuple-element.252), channel_id=1, source_target_pairs={{0,96},{32,0},{64,32},{96,64},{1,97},{33,1},{65,33},{97,65},{2,98}... | collective-permute-start | bytes 786440 | tf_op jit(solution)/shard_map/ppermute | solution.py:823
  183.5 27.3 %all-to-all-start.3 = ((f32[32,64,128]{2,1,0:T(8,128)}), f32[32,64,128]{2,1,0:T(8,128)S(1)}, u32[]{:S(2)}, u32[]{:S(2)}) async-start(f32[32,64,128]{2,1,0:T(8,128)} %d_gated.1), calls=%async_computation.3 | async-start | bytes 2097152 | tf_op jit(solution)/shard_map/all_to_all | solution.py:1010
  190.8 9.1 %collective-permute-start.27 = (bf16[128,1024]{1,0:T(8,128)(2,1)S(1)}, bf16[128,1024]{1,0:T(8,128)(2,1)S(1)}, u32[]{:S(2)}, u32[]{:S(2)}) collective-permute-start(bf16[128,1024]{1,0:T(8,128)(2,1)S(1)} %copy-done.19), channel_id=1, source_target_pairs={{0,32},{32,64},{64,96},{96,0},{1,33},{33,65},{65,97},{97,1},{2,34}... | collective-permute-start | bytes 786440 | tf_op jit(solution)/shard_map/ppermute | solution.py:823
  191.6 14.7 %collective-permute-start.28 = (bf16[128,1024]{1,0:T(8,128)(2,1)S(1)}, bf16[128,1024]{1,0:T(8,128)(2,1)S(1)}, u32[]{:S(2)}, u32[]{:S(2)}) collective-permute-start(bf16[128,1024]{1,0:T(8,128)(2,1)S(1)} %copy-done.19), channel_id=1, source_target_pairs={{0,64},{32,96},{64,0},{96,32},{1,65},{33,97},{65,1},{97,33},{2,66}... | collective-permute-start | bytes 786440 | tf_op jit(solution)/shard_map/ppermute | solution.py:823
  194.6 11.6 %collective-permute-start.29 = (bf16[128,1024]{1,0:T(8,128)(2,1)S(1)}, bf16[128,1024]{1,0:T(8,128)(2,1)S(1)}, u32[]{:S(2)}, u32[]{:S(2)}) collective-permute-start(bf16[128,1024]{1,0:T(8,128)(2,1)S(1)} %copy-done.19), channel_id=1, source_target_pairs={{0,96},{32,0},{64,32},{96,64},{1,97},{33,1},{65,33},{97,65},{2,98}... | collective-permute-start | bytes 786440 | tf_op jit(solution)/shard_map/ppermute | solution.py:823
  220.6 42.1 %all-to-all-start.4 = ((bf16[16,256,128]{2,1,0:T(8,128)(2,1)}), bf16[16,256,128]{2,1,0:T(8,128)(2,1)S(1)}, u32[]{:S(2)}, u32[]{:S(2)}) async-start(bf16[16,256,128]{2,1,0:T(8,128)(2,1)} %output_weights.1), calls=%async_computation.5 | async-start | bytes 2097152 | tf_op jit(solution)/shard_map/all_to_all | solution.py:859
  274.0 31.8 %all-to-all-start.5 = ((bf16[16,64,1024]{2,1,0:T(8,128)(2,1)}), bf16[16,64,1024]{2,1,0:T(8,128)(2,1)S(1)}, u32[]{:S(2)}, u32[]{:S(2)}) async-start(bf16[16,64,1024]{2,1,0:T(8,128)(2,1)} %add_convert_fusion), calls=%async_computation.6 | async-start | bytes 4194304 | tf_op jit(solution)/shard_map/all_to_all | solution.py:859
  278.7 89.4 %all-gather.3.cloned.1.call-start = ((), (), s32[]{:S(2)}) async-start(), calls=%async_computation.9 | async-start | bytes 3342336 | tf_op jit(solution)/shard_map/all_gather | solution.py:1038
  281.1 22.2 %collective-permute-start.32 = (bf16[272,512]{1,0:T(8,128)(2,1)}, bf16[272,512]{1,0:T(8,128)(2,1)}, u32[]{:S(2)}, u32[]{:S(2)}) collective-permute-start(bf16[272,512]{1,0:T(8,128)(2,1)} %get-tuple-element.247), channel_id=1, source_target_pairs={{0,32},{32,64},{64,96},{96,0},{1,33},{33,65},{65,97},{97,1},{2,34}... | collective-permute-start | bytes 835592 | tf_op jit(solution)/shard_map/ppermute | solution.py:823
  282.5 20.8 %collective-permute-start.33 = (bf16[272,512]{1,0:T(8,128)(2,1)}, bf16[272,512]{1,0:T(8,128)(2,1)}, u32[]{:S(2)}, u32[]{:S(2)}) collective-permute-start(bf16[272,512]{1,0:T(8,128)(2,1)} %get-tuple-element.246), channel_id=1, source_target_pairs={{0,64},{32,96},{64,0},{96,32},{1,65},{33,97},{65,1},{97,33},{2,66}... | collective-permute-start | bytes 835592 | tf_op jit(solution)/shard_map/ppermute | solution.py:823
  285.1 18.3 %collective-permute-start.34 = (bf16[272,512]{1,0:T(8,128)(2,1)}, bf16[272,512]{1,0:T(8,128)(2,1)}, u32[]{:S(2)}, u32[]{:S(2)}) collective-permute-start(bf16[272,512]{1,0:T(8,128)(2,1)} %get-tuple-element.245), channel_id=1, source_target_pairs={{0,96},{32,0},{64,32},{96,64},{1,97},{33,1},{65,33},{97,65},{2,98}... | collective-permute-start | bytes 835592 | tf_op jit(solution)/shard_map/ppermute | solution.py:823
  286.2 6.9 %collective-permute-start.42 = (bf16[96,128]{1,0:T(8,128)(2,1)S(1)}, bf16[96,128]{1,0:T(8,128)(2,1)S(1)}, u32[]{:S(2)}, u32[]{:S(2)}) collective-permute-start(bf16[96,128]{1,0:T(8,128)(2,1)S(1)} %get-tuple-element.272), channel_id=1, source_target_pairs={{0,32},{32,64},{64,96},{96,0},{1,33},{33,65},{65,97},{97,1},{2,34}... | collective-permute-start | bytes 73736 | tf_op jit(solution)/shard_map/ppermute | solution.py:823
  287.4 10.0 %collective-permute-start.43 = (bf16[96,128]{1,0:T(8,128)(2,1)S(1)}, bf16[96,128]{1,0:T(8,128)(2,1)S(1)}, u32[]{:S(2)}, u32[]{:S(2)}) collective-permute-start(bf16[96,128]{1,0:T(8,128)(2,1)S(1)} %get-tuple-element.271), channel_id=1, source_target_pairs={{0,64},{32,96},{64,0},{96,32},{1,65},{33,97},{65,1},{97,33},{2,66}... | collective-permute-start | bytes 73736 | tf_op jit(solution)/shard_map/ppermute | solution.py:823
  293.1 8.3 %collective-permute-start.44 = (bf16[96,128]{1,0:T(8,128)(2,1)S(1)}, bf16[96,128]{1,0:T(8,128)(2,1)S(1)}, u32[]{:S(2)}, u32[]{:S(2)}) collective-permute-start(bf16[96,128]{1,0:T(8,128)(2,1)S(1)} %get-tuple-element.270), channel_id=1, source_target_pairs={{0,96},{32,0},{64,32},{96,64},{1,97},{33,1},{65,33},{97,65},{2,98}... | collective-permute-start | bytes 73736 | tf_op jit(solution)/shard_map/ppermute | solution.py:823
  312.8 6.5 %collective-permute-start.36 = (bf16[64,256]{1,0:T(8,128)(2,1)S(1)}, bf16[64,256]{1,0:T(8,128)(2,1)S(1)}, u32[]{:S(2)}, u32[]{:S(2)}) collective-permute-start(bf16[64,256]{1,0:T(8,128)(2,1)S(1)} %fusion.21), channel_id=1, source_target_pairs={{0,1},{1,0},{2,3},{3,2},{4,5},{5,4},{6,7},{7,6},{8,9},{9,8},{10,11... | collective-permute-start | bytes 98312 | tf_op jit(solution)/shard_map/ppermute | solution.py:815
  321.2 7.2 %collective-permute-start.37 = (bf16[512,1024]{1,0:T(8,128)(2,1)}, bf16[512,1024]{1,0:T(8,128)(2,1)}, u32[]{:S(2)}, u32[]{:S(2)}) collective-permute-start(bf16[512,1024]{1,0:T(8,128)(2,1)} %convolution_convert_fusion), channel_id=1, source_target_pairs={{0,1},{1,0},{2,3},{3,2},{4,5},{5,4},{6,7},{7,6},{8,9},{9,8},{10,11... | collective-permute-start | bytes 3145736 | tf_op jit(solution)/shard_map/ppermute | solution.py:815
  324.5 41.5 %all-to-all-start.6 = ((bf16[16,448,128]{2,1,0:T(8,128)(2,1)}), bf16[16,448,128]{2,1,0:T(8,128)(2,1)S(1)}, u32[]{:S(2)}, u32[]{:S(2)}) async-start(bf16[16,448,128]{2,1,0:T(8,128)(2,1)} %broadcast_in_dim.13), calls=%async_computation.7 | async-start | bytes 3670016 | tf_op jit(solution)/shard_map/all_to_all | solution.py:859
  330.6 9.3 %collective-permute-start.40 = (bf16[128,1024]{1,0:T(8,128)(2,1)S(1)}, bf16[128,1024]{1,0:T(8,128)(2,1)S(1)}, u32[]{:S(2)}, u32[]{:S(2)}) collective-permute-start(bf16[128,1024]{1,0:T(8,128)(2,1)S(1)} %get-tuple-element.250), channel_id=1, source_target_pairs={{0,32},{32,64},{64,96},{96,0},{1,33},{33,65},{65,97},{97,1},{2,34}... | collective-permute-start | bytes 786440 | tf_op jit(solution)/shard_map/ppermute | solution.py:823
  332.0 14.5 %collective-permute-start.39 = (bf16[128,1024]{1,0:T(8,128)(2,1)S(1)}, bf16[128,1024]{1,0:T(8,128)(2,1)S(1)}, u32[]{:S(2)}, u32[]{:S(2)}) collective-permute-start(bf16[128,1024]{1,0:T(8,128)(2,1)S(1)} %get-tuple-element.251), channel_id=1, source_target_pairs={{0,64},{32,96},{64,0},{96,32},{1,65},{33,97},{65,1},{97,33},{2,66}... | collective-permute-start | bytes 786440 | tf_op jit(solution)/shard_map/ppermute | solution.py:823
  334.6 11.9 %collective-permute-start.38 = (bf16[128,1024]{1,0:T(8,128)(2,1)S(1)}, bf16[128,1024]{1,0:T(8,128)(2,1)S(1)}, u32[]{:S(2)}, u32[]{:S(2)}) collective-permute-start(bf16[128,1024]{1,0:T(8,128)(2,1)S(1)} %get-tuple-element.249), channel_id=1, source_target_pairs={{0,96},{32,0},{64,32},{96,64},{1,97},{33,1},{65,33},{97,65},{2,98}... | collective-permute-start | bytes 786440 | tf_op jit(solution)/shard_map/ppermute | solution.py:823
  368.1 14.7 %collective-permute-start.46 = (bf16[16,768,128]{2,1,0:T(8,128)(2,1)}, bf16[16,768,128]{2,1,0:T(8,128)(2,1)}, u32[]{:S(2)}, u32[]{:S(2)}) collective-permute-start(bf16[16,768,128]{2,1,0:T(8,128)(2,1)} %bitcast.204), channel_id=1, source_target_pairs={{0,1},{1,0},{2,3},{3,2},{4,5},{5,4},{6,7},{7,6},{8,9},{9,8},{10,11... | collective-permute-start | bytes 9437192 | tf_op jit(solution)/shard_map/ppermute | solution.py:815
  (55 other events, 452.5 us)
Sparse Core Ops, SparseCore 0:
  178.9 95.0 reduce-scatter.1
  303.4 64.1 all-gather.2
